TPU v7x, 512 devices: a whole 4x8x8 slice. The times are simulated.
512 devices in a mesh: day: 16 (over y, core), bl: 32 (over z, x).
Axes of the slice: x: 4, y: 8, z: 8, core: 2. Of those that a mesh axis runs over, the one named last changes fastest.
Arguments:
- visibility: bfloat16 [16, 16, 2, 2048, 512], P('day', None, None, 'bl'), may hold values from -6 to 6
- day_weight: float32 [16, 2048, 512], P('day', 'bl'), may hold values from 0.2 to 5
- day_offset: int32 [16], replicated, may hold values from 0 to 16, as said below
- pair_index: int32 [2048], replicated, may hold values from 0 to 3, as said below
- sep_index: int32 [2048], replicated, may hold values from 0 to 511, as said below
Outputs:
- skymap: float32 [512, 32, 4, 512], P('bl', 'day')
Inputs may be any that keep to these rules, and one draw needn't show every extreme that they name: Each day's samples cover 32 bins day_offset to day_offset + 15; every 32 bin of the window is covered by some day; some day starts at 0 and some at 16. `pair_index`: each pair of cylinder separation and north-south separation is named by exactly one stacked baseline. `sep_index`: each pair of cylinder separation and north-south separation is named by exactly one stacked baseline.
All inputs are finite; a program needn't handle non-finite values.
Results may differ from a plain program's by a relative error of at most 0.0032.
Values may be sent and summed in bfloat16 or wider, within the bound.
No kernel may reach another device: no remote copies, remote signals or barrier semaphores. Data moves between devices by JAX's collectives and lax.ppermute only.
A program may use at most 64 MiB of HBM per device.

v0:
```python
import jax
import jax.numpy as jnp
from jax import lax
from jax.experimental import pallas as pl
from jax.experimental.pallas import tpu as pltpu
from jax.sharding import PartitionSpec as P

FREQ = 512
PAIRS = 4
NSEP = 512
PIXELS = 512
HALF = PIXELS // 2
RA = 32
RA_DEV = 2
SAMPLES = 16
DAYS = 16
BASES = 2048
N_BL = 32
BASE_LOC = BASES // N_BL
BAND = FREQ // N_BL
COARSE = 24
FINE = 16
CHIPS = 8
HELD = 8
SCALE = 128.0
SWAP = [(d, d ^ 1) for d in range(DAYS)]

F32 = jnp.float32
BF16 = jnp.bfloat16
F16 = jnp.float16
MIB = 1 << 20

phase_scale = 2.0 * 3.141592653589793 * 0.3048 / 299.792458


def bins_below(offset, core):
    return 2 * (offset >> 2) + jnp.clip((offset & 3) - 2 * core, 0, 2)


def select_kernel(offset_ref, weight_ref, vis_ref, out_ref, weight_buf, sems):
    day = lax.axis_index("day")
    other = 1 - (day & 1)
    offset = offset_ref[day]
    first = bins_below(offset, other)
    load = pltpu.make_async_copy(weight_ref, weight_buf, sems.at[HELD])
    load.start()
    copies = []
    for k in range(HELD):
        owned = first + k
        sample = 4 * (owned >> 1) + 2 * other + (owned & 1) - offset
        copies.append(
            pltpu.make_async_copy(
                vis_ref.at[sample], out_ref.at[owned & (HELD - 1)], sems.at[k]
            )
        )
        copies[-1].start()
    load.wait()
    weight = weight_buf[...]
    high = weight.astype(BF16)
    out_ref[HELD, 0] = high
    out_ref[HELD, 1] = (weight - high.astype(F32)).astype(BF16)
    for copy in copies:
        copy.wait()


def select(day_offset, day_weight, visibility):
    hbm = pl.BlockSpec(memory_space=pl.ANY)
    return pl.pallas_call(
        select_kernel,
        in_specs=[pl.BlockSpec(memory_space=pltpu.SMEM), hbm, hbm],
        out_specs=pl.BlockSpec(memory_space=pltpu.VMEM),
        out_shape=jax.ShapeDtypeStruct((HELD + 1, 2, BASE_LOC, FREQ), BF16),
        scratch_shapes=[
            pltpu.VMEM((BASE_LOC, FREQ), F32),
            pltpu.SemaphoreType.DMA((HELD + 1,)),
        ],
        compiler_params=pltpu.CompilerParams(vmem_limit_bytes=60 * MIB),
        name="select",
    )(day_offset, day_weight, visibility)


SENDS = (
    ((3, 0), (3, 1), (1, 0), (1, 1)),
    ((5, 0), (5, 1), (7, 0), (7, 1)),
    ((4, 0),),
    ((4, 1),),
    ((2, 0), (2, 1)),
    ((6, 0), (6, 1)),
    ((0, 0), (0, 1)),
)


def chip_kernel(offset_ref, vis_ref, weight_ref, other_ref, *out_refs):
    day = lax.axis_index("day")
    core = day & 1
    chip = day >> 1
    offset = offset_ref[day]
    first = bins_below(offset_ref[day ^ 1], core)
    weight = weight_ref[...] * SCALE
    other_weight = (other_ref[HELD, 0].astype(F32) + other_ref[HELD, 1].astype(F32)) * SCALE
    for out_ref, bins in zip(out_refs, SENDS):
        for at, (distance, which) in enumerate(bins):
            owned = 2 * ((chip + distance) & (CHIPS - 1)) + which
            sample = 4 * (owned >> 1) + 2 * core + which - offset
            valid = jnp.logical_and(sample >= 0, sample < SAMPLES)
            held = jnp.logical_and(owned >= first, owned < first + HELD)
            sample = jnp.clip(sample, 0, SAMPLES - 1)
            own = weight * jnp.where(valid, 1.0, 0.0)
            other = other_weight * jnp.where(held, 1.0, 0.0)
            for x in range(2):
                out_ref[at, x] = (
                    vis_ref[sample, x].astype(F32) * own
                    + other_ref[owned & (HELD - 1), x].astype(F32) * other
                )


def chip_sums(day_offset, visibility, day_weight, other):
    rows = 16
    block = lambda count: pl.BlockSpec((count, 2, rows, FREQ), lambda i: (0, 0, i, 0))
    return pl.pallas_call(
        chip_kernel,
        grid=(BASE_LOC // rows,),
        in_specs=[
            pl.BlockSpec(memory_space=pltpu.SMEM),
            block(SAMPLES),
            pl.BlockSpec((rows, FREQ), lambda i: (i, 0)),
            block(HELD + 1),
        ],
        out_specs=[block(len(bins)) for bins in SENDS],
        out_shape=[
            jax.ShapeDtypeStruct((len(bins), 2, BASE_LOC, FREQ), F32) for bins in SENDS
        ],
        compiler_params=pltpu.CompilerParams(vmem_limit_bytes=16 * MIB),
        name="chip_sums",
    )(day_offset, visibility, day_weight, other)


def send(values, distance):
    pairs = [
        (2 * y + c, 2 * ((y + distance) % CHIPS) + c) for y in range(CHIPS) for c in range(2)
    ]
    return lax.ppermute(values.astype(F16), "day", pairs)


def reduce_ring(sums, late):
    near_up, near_down = send(sums[0], 1), send(sums[1], -1)
    far_up, far_down = send(sums[2], 2), send(sums[3], -2)
    middle_up = sums[4] + near_up[:2].astype(F32)
    middle_up = middle_up + jnp.pad(far_up.astype(F32), ((0, 1), (0, 0), (0, 0), (0, 0)))
    middle_down = sums[5] + near_down[:2].astype(F32)
    middle_down = middle_down + jnp.pad(far_down.astype(F32), ((1, 0), (0, 0), (0, 0), (0, 0)))
    middle_up, middle_down = middle_up.astype(F16), middle_down.astype(F16)
    late = lax.optimization_barrier((*late, middle_up, middle_down))[:-2]
    last_up, last_down = send(middle_up, 2), send(middle_down, -2)
    summed = (
        sums[6]
        + near_up[2:].astype(F32)
        + near_down[2:].astype(F32)
        + last_up.astype(F32)
        + last_down.astype(F32)
    )
    return summed, late


def gather_weights(day_weight):
    same = [[2 * y + c for y in range(CHIPS)] for c in range(2)]
    copies = jnp.broadcast_to(day_weight.astype(F16)[None], (CHIPS, BASE_LOC, FREQ))
    return lax.all_to_all(
        copies, "day", split_axis=0, concat_axis=0, axis_index_groups=same, tiled=True
    )


def inverse_total(day_offset, weights):
    day = lax.axis_index("day")
    offsets = jnp.where((day & 1) == 0, day_offset[0::2], day_offset[1::2])
    weights = weights.astype(F32)

    def partial_total(owner):
        sample = (owner * RA_DEV + jnp.arange(RA_DEV))[:, None] - offsets[None, :]
        valid = jnp.logical_and(sample >= 0, sample < SAMPLES).astype(F32)
        return jnp.sum(valid[:, :, None, None] * weights[None], axis=1)

    other = lax.ppermute(partial_total(day ^ 1), "day", SWAP)
    return (1.0 / SCALE) / (partial_total(day) + other)


def base_angles(freq_at):
    factor = phase_scale * (800.0 - 400.0 * (freq_at + 0.5) / FREQ)
    sine_dir = -1.0 + 2.0 * (jnp.arange(HALF).astype(F32) + 0.5) / PIXELS
    separation = jnp.concatenate([jnp.arange(COARSE) * FINE, jnp.arange(FINE)]).astype(F32)
    phase = factor[:, None, None] * separation[None, :, None] * sine_dir[None, None, :]
    return jnp.cos(phase), jnp.sin(phase)


def pack_blocks(pieces, out_ref, rows):
    lane_group = lax.broadcasted_iota(jnp.int32, (8, 128), 1) // BAND
    for tile in range(FREQ // 128):
        parts = [piece[:, tile * 128 : (tile + 1) * 128] for piece in pieces]
        for step in (4, 2, 1):
            keep = (lane_group & step) == 0
            mixed = list(parts)
            for low in range(8):
                if low & step:
                    continue
                high = low | step
                mixed[low] = jnp.where(keep, parts[low], pltpu.roll(parts[high], step * BAND, 1))
                mixed[high] = jnp.where(
                    keep, pltpu.roll(parts[low], 128 - step * BAND, 1), parts[high]
                )
            parts = mixed
        for group in range(8):
            out_ref[tile * 8 + group, rows, :] = parts[group].astype(BF16)


def pack_kernel(sum_ref, inverse_ref, out_ref):
    half = BASE_LOC // 2
    for first in range(0, half, 16):
        for sub in range(0, 16, 8):
            rows = pl.ds(first + sub, 8)
            pieces = []
            for x in range(2):
                for r in range(RA_DEV):
                    for hi in range(2):
                        rows_in = pl.ds(hi * half + first + sub, 8)
                        pieces.append(
                            sum_ref[r, x, rows_in, :] * inverse_ref[r, rows_in, :]
                        )
            pack_blocks(pieces, out_ref, rows)


def pack(summed, inverse):
    vmem = pl.BlockSpec(memory_space=pltpu.VMEM)
    return pl.pallas_call(
        pack_kernel,
        in_specs=[vmem, vmem],
        out_specs=vmem,
        out_shape=jax.ShapeDtypeStruct((N_BL, BASE_LOC // 2, 128), BF16),
        compiler_params=pltpu.CompilerParams(vmem_limit_bytes=16 * MIB),
        name="pack",
    )(summed, inverse)


def beam_kernel(block_ref, pair_ref, sep_ref, cos_ref, sin_ref, out_ref, grid_ref, table_buf):
    flat = BASES // 2
    rows = RA_DEV * PAIRS

    turned = block_ref[...].astype(F32).reshape(flat, 128).T
    total = jnp.zeros((2 * rows * BAND, NSEP), F32)
    for hi in range(2):
        picked = [
            turned[(group * 2 + hi) * BAND : (group * 2 + hi + 1) * BAND] for group in range(4)
        ]
        pair = pair_ref[hi : hi + 1, :]
        masked = jnp.concatenate(
            [jnp.where(pair == c, part, 0.0) for part in picked for c in range(PAIRS)], axis=0
        ).astype(BF16)
        sep = sep_ref[:, hi : hi + 1]
        column = jnp.where(
            sep >= NSEP // 2, sep - NSEP // 2, jnp.where(sep == 0, NSEP // 2, NSEP - sep)
        )
        onehot = jnp.where(
            column == lax.broadcasted_iota(jnp.int32, (flat, NSEP), 1), 1.0, 0.0
        ).astype(BF16)
        total = total + jnp.dot(masked, onehot, preferred_element_type=F32)
    for tile in range(NSEP // 128):
        grid_ref[tile] = total[:, tile * 128 : (tile + 1) * 128]

    flip = (
        lax.broadcasted_iota(jnp.int32, (HALF, HALF), 0)
        + lax.broadcasted_iota(jnp.int32, (HALF, HALF), 1)
        == HALF - 1
    )
    flip = jnp.where(flip, 1.0, 0.0).astype(BF16)
    odd_part = []
    edge = NSEP // 2 // FINE
    for f in range(BAND):
        cos_b = cos_ref[f, COARSE:, :]
        sin_b = sin_ref[f, COARSE:, :]
        for a in range(edge):
            cos_a = cos_ref[f, a : a + 1, :]
            sin_a = sin_ref[f, a : a + 1, :]
            at = pl.ds(a * FINE, FINE)
            table_buf[f, at, :HALF] = (cos_a * cos_b - sin_a * sin_b).astype(BF16)
            table_buf[f, at, HALF:] = (-(sin_a * cos_b + cos_a * sin_b)).astype(BF16)
        tiles = [grid_ref[tile, pl.ds(f, 2 * rows, stride=BAND), :] for tile in range(4)]
        cells = jnp.concatenate(
            [jnp.concatenate(tiles[:2], axis=1), jnp.concatenate(tiles[2:], axis=1)], axis=0
        ).astype(BF16)
        lone = tiles[2][:, :1]
        both = jnp.dot(cells, table_buf[f], preferred_element_type=F32)
        edge_cos = cos_ref[f, edge : edge + 1, :].astype(BF16).astype(F32)
        edge_sin = sin_ref[f, edge : edge + 1, :].astype(BF16).astype(F32)
        cos_part = both[:rows, :HALF] + both[2 * rows : 3 * rows, :HALF]
        cos_part = cos_part + lone[:rows] * (edge_cos - 1.0)
        sin_part = both[rows : 2 * rows, HALF:] - both[3 * rows :, HALF:]
        sin_part = sin_part + lone[rows:] * edge_sin
        even = cos_part + sin_part
        for r in range(RA_DEV):
            out_ref[f, r, :, :HALF] = even[r * PAIRS : (r + 1) * PAIRS]
        odd_part.append(cos_part - sin_part)
    rest = jnp.concatenate(odd_part, axis=0)
    turned = jnp.zeros(rest.shape, F32)
    for _ in range(3):
        piece = rest.astype(BF16)
        rest = rest - piece.astype(F32)
        turned = turned + jnp.dot(piece, flip, preferred_element_type=F32)
    for f in range(BAND):
        for r in range(RA_DEV):
            first = f * rows + r * PAIRS
            out_ref[f, r, :, HALF:] = turned[first : first + PAIRS]


def beam(block, pair_index, sep_index, angles):
    flat = BASES // 2
    pair = pair_index.reshape(N_BL, 2, BASE_LOC // 2).transpose(1, 0, 2).reshape(2, flat)
    sep = sep_index.reshape(N_BL, 2, BASE_LOC // 2).transpose(0, 2, 1).reshape(flat, 2)
    vmem = pl.BlockSpec(memory_space=pltpu.VMEM)
    return pl.pallas_call(
        beam_kernel,
        in_specs=[vmem] * 5,
        out_specs=vmem,
        out_shape=jax.ShapeDtypeStruct((BAND, RA_DEV, PAIRS, PIXELS), F32),
        scratch_shapes=[
            pltpu.VMEM((NSEP // 128, 2 * RA_DEV * PAIRS * BAND, 128), F32),
            pltpu.VMEM((BAND, NSEP // 2, 2 * HALF), BF16),
        ],
        compiler_params=pltpu.CompilerParams(vmem_limit_bytes=32 * MIB),
        name="beam",
    )(block, pair, sep, *angles)


def day_stage(visibility, day_weight, day_offset, freq_at):
    visibility, day_weight = visibility[0], day_weight[0]
    other = lax.ppermute(select(day_offset, day_weight, visibility), "day", SWAP)
    weights = gather_weights(day_weight)
    sums = chip_sums(day_offset, visibility, day_weight, other)
    summed, (weights, freq_at) = reduce_ring(sums, (weights, freq_at))
    return summed, inverse_total(day_offset, weights), freq_at


def beam_stage(summed, inverse, pair_index, sep_index, freq_at):
    angles = base_angles(freq_at)
    packed = pack(summed, inverse)
    block = lax.all_to_all(packed, "bl", split_axis=0, concat_axis=0, tiled=True)
    return beam(block, pair_index, sep_index, angles)


def local(visibility, day_weight, day_offset, pair_index, sep_index):
    freq_at = (lax.axis_index("bl") * BAND + jnp.arange(BAND)).astype(F32)
    summed, inverse, freq_at = day_stage(visibility, day_weight, day_offset, freq_at)
    return beam_stage(summed, inverse, pair_index, sep_index, freq_at)


def solution(mesh):
    return jax.shard_map(
        local,
        mesh=mesh,
        in_specs=(P("day", None, None, "bl", None), P("day", "bl", None), P(), P(), P()),
        out_specs=P("bl", "day", None, None),
        check_vma=False,
    )
```

profile of v0, /device:TPU:1, one launch (start us, length us, event | category | flops | bytes accessed | tf_op | source)
XLA Modules:
  0.0 106.2 jit_solution(10994073562936331452)
XLA Ops:
  0.0 3.2 %select.3 = bf16[9,2,64,512]{3,2,1,0:T(8,128)(2,1)} custom-call(s32[16]{0:T(128)} %offset_ref.3, f32[64,512]{1,0:T(8,128)} %bitcast.10, bf16[16,2,64,512]{3,2,1,0:T(8,128)(2,1)} %bitcast.7), custom_call_target="tpu_custom_call" | custom-call | tf_op jit(solution)/shard_map/select/pallas_call | solution.py:68
  3.3 8.8 %collective-permute-start = (bf16[9,2,64,512]{3,2,1,0:T(8,128)(2,1)}, bf16[9,2,64,512]{3,2,1,0:T(8,128)(2,1)S(1)}, u32[]{:S(2)}, u32[]{:S(2)}) collective-permute-start(bf16[9,2,64,512]{3,2,1,0:T(8,128)(2,1)} %select.3), channel_id=1, source_target_pairs={{0,32},{32,0},{64,96},{96,64},{128,160},{160,128},{192,224},{224,1... | collective-permute-start | bytes 3538952 | tf_op jit(solution)/shard_map/ppermute | solution.py:334
  12.1 0.0 copy-done.1
  12.1 0.8 broadcast_in_dim.5
  12.9 4.1 %all-to-all-start = ((f16[8,64,512]{2,1,0:T(8,128)(2,1)}), f16[8,64,512]{2,1,0:T(8,128)(2,1)}, u32[]{:S(2)}, u32[]{:S(2)}) async-start(f16[8,64,512]{2,1,0:T(8,128)(2,1)} %broadcast_in_dim.5), calls=%async_computation | async-start | bytes 1048576 | tf_op jit(solution)/shard_map/all_to_all | solution.py:168
  17.1 0.0 copy-done.13
  17.1 0.1 slice.22
  17.2 0.1 slice.23
  17.3 0.0 collective-permute-done.other_ref
  17.3 0.0 copy-done
  17.3 2.2 %chip_sums.1 = (f32[4,2,64,512]{3,2,1,0:T(8,128)S(1)}, f32[4,2,64,512]{3,2,1,0:T(8,128)S(1)}, f32[1,2,64,512]{3,2,1,0:T(8,128)S(1)}, f32[1,2,64,512]{3,2,1,0:T(8...) custom-call(s32[16]{0:T(128)S(1)} %copy-done.13, ...), custom_call_target="tpu_custom_call" | custom-call | tf_op jit(solution)/shard_map/chip_sums/pallas_call | solution.py:120
  19.5 0.0 copy-start.2
  19.5 1.0 copy-done.2
  20.5 0.7 copy-done.10
  21.2 0.7 copy-done.12
  21.9 0.0 copy-start.11
  21.9 0.1 convert_element_type.80
  22.1 0.7 copy-done.4
  22.7 3.3 %collective-permute-start.1 = (f16[4,2,64,512]{3,2,1,0:T(8,128)(2,1)S(1)}, f16[4,2,64,512]{3,2,1,0:T(8,128)(2,1)}, u32[]{:S(2)}, u32[]{:S(2)}) collective-permute-start(f16[4,2,64,512]{3,2,1,0:T(8,128)(2,1)S(1)} %convert_element_type.80), channel_id=1, source_target_pairs={{0,64},{32,96},{64,128},{96,160},{128,192},{160,224},{192,256},{22... | collective-permute-start | bytes 1572872 | tf_op jit(solution)/shard_map/ppermute | solution.py:142
  26.1 0.0 copy-done.6
  26.1 0.0 copy-done.8
  26.1 0.0 copy-start.5
  26.1 0.0 copy-start.7
  26.1 1.7 %convert_element_type.85 = f16[1,2,64,512]{3,2,1,0:T(8,128)(2,1)} convert(f32[1,2,64,512]{3,2,1,0:T(8,128)} %copy-done.12) | non-fusion elementwise | flops 65536 | bytes 393216 | tf_op jit(solution)/shard_map/convert_element_type | solution.py:142
  27.8 4.0 %collective-permute-start.3 = (f16[1,2,64,512]{3,2,1,0:T(8,128)(2,1)}, f16[1,2,64,512]{3,2,1,0:T(8,128)(2,1)S(1)}, u32[]{:S(2)}, u32[]{:S(2)}) collective-permute-start(f16[1,2,64,512]{3,2,1,0:T(8,128)(2,1)} %convert_element_type.85), channel_id=1, source_target_pairs={{0,128},{32,160},{64,192},{96,224},{128,256},{160,288},{192,320},{... | collective-permute-start | bytes 393224 | tf_op jit(solution)/shard_map/ppermute | solution.py:142
  31.8 0.0 copy-done.3
  31.8 0.1 convert_element_type.82
  32.0 3.4 %collective-permute-start.2 = (f16[4,2,64,512]{3,2,1,0:T(8,128)(2,1)S(1)}, f16[4,2,64,512]{3,2,1,0:T(8,128)(2,1)S(1)}, u32[]{:S(2)}, u32[]{:S(2)}) collective-permute-start(f16[4,2,64,512]{3,2,1,0:T(8,128)(2,1)S(1)} %convert_element_type.82), channel_id=1, source_target_pairs={{0,448},{32,480},{64,0},{96,32},{128,64},{160,96},{192,128},{224,1... | collective-permute-start | bytes 1572872 | tf_op jit(solution)/shard_map/ppermute | solution.py:142
  35.4 0.1 and_convert_fusion.1
  35.4 0.0 copy-done.11
  35.5 2.0 %collective-permute-start.5 = (f16[1,2,64,512]{3,2,1,0:T(8,128)(2,1)S(1)}, f16[1,2,64,512]{3,2,1,0:T(8,128)(2,1)S(1)}, u32[]{:S(2)}, u32[]{:S(2)}) collective-permute-start(f16[1,2,64,512]{3,2,1,0:T(8,128)(2,1)S(1)} %convert_element_type.89), channel_id=1, source_target_pairs={{0,384},{32,416},{64,448},{96,480},{128,0},{160,32},{192,64},{224,... | collective-permute-start | bytes 393224 | tf_op jit(solution)/shard_map/ppermute | solution.py:142
  37.5 10.4 %collective-permute-done.3 = f16[1,2,64,512]{3,2,1,0:T(8,128)(2,1)S(1)} collective-permute-done((f16[1,2,64,512]{3,2,1,0:T(8,128)(2,1)}, f16[1,2,64,512]{3,2,1,0:T(8,128)(2,1)S(1)}, u32[]{:S(2)}, u32[]{:S(2)}) %collective-permute-start.3) | collective-permute-done | bytes 131104 | tf_op jit(solution)/shard_map/ppermute | solution.py:142
  48.0 0.0 collective-permute-done.1
  48.0 0.0 copy-done.7
  48.0 1.1 add_convert_fusion.1
  49.0 5.1 %collective-permute-done.5 = f16[1,2,64,512]{3,2,1,0:T(8,128)(2,1)S(1)} collective-permute-done((f16[1,2,64,512]{3,2,1,0:T(8,128)(2,1)S(1)}, f16[1,2,64,512]{3,2,1,0:T(8,128)(2,1)S(1)}, u32[]{:S(2)}, u32[]{:S(2)}) %collective-permute-start.5) | collective-permute-done | bytes 131104 | tf_op jit(solution)/shard_map/ppermute | solution.py:142
  54.2 0.0 collective-permute-done.2
  54.2 0.0 copy-done.5
  54.2 0.1 add_convert_fusion
  54.3 0.0 copy-start.15
  54.3 0.0 copy-start.9
  54.3 0.0 all-to-all-done
  54.3 1.2 %convert_element_type.95 = f32[8,64,512]{2,1,0:T(8,128)S(1)} convert(f16[8,64,512]{2,1,0:T(8,128)(2,1)} %all-to-all-done) | non-fusion elementwise | flops 262144 | bytes 1572864 | tf_op jit(solution)/shard_map/convert_element_type | solution.py:176
  55.6 0.4 multiply_reduce_fusion
  55.9 3.7 %collective-permute-start.7 = (f32[2,64,512]{2,1,0:T(8,128)S(1)}, f32[2,64,512]{2,1,0:T(8,128)S(1)}, u32[]{:S(2)}, u32[]{:S(2)}) collective-permute-start(f32[2,64,512]{2,1,0:T(8,128)S(1)} %get-tuple-element.23), channel_id=1, source_target_pairs={{0,32},{32,0},{64,96},{96,64},{128,160},{160,128},{192,224},{224,1... | collective-permute-start | bytes 786440 | tf_op jit(solution)/shard_map/ppermute | solution.py:183
  59.6 3.4 %collective-permute-start.4 = (f16[2,2,64,512]{3,2,1,0:T(8,128)(2,1)S(1)}, f16[2,2,64,512]{3,2,1,0:T(8,128)(2,1)S(1)}, u32[]{:S(2)}, u32[]{:S(2)}) collective-permute-start(f16[2,2,64,512]{3,2,1,0:T(8,128)(2,1)S(1)} %add_convert_fusion.1), channel_id=1, source_target_pairs={{0,128},{32,160},{64,192},{96,224},{128,256},{160,288},{192,320},{... | collective-permute-start | bytes 786440 | tf_op jit(solution)/shard_map/ppermute | solution.py:142
  63.0 4.0 %collective-permute-start.6 = (f16[2,2,64,512]{3,2,1,0:T(8,128)(2,1)S(1)}, f16[2,2,64,512]{3,2,1,0:T(8,128)(2,1)S(1)}, u32[]{:S(2)}, u32[]{:S(2)}) collective-permute-start(f16[2,2,64,512]{3,2,1,0:T(8,128)(2,1)S(1)} %add_convert_fusion), channel_id=1, source_target_pairs={{0,384},{32,416},{64,448},{96,480},{128,0},{160,32},{192,64},{224,... | collective-permute-start | bytes 786440 | tf_op jit(solution)/shard_map/ppermute | solution.py:142
  67.0 0.1 add_convert_fusion.2
  67.1 0.0 copy-done.14
  67.1 0.1 reshape.132
  67.2 0.3 copy.9
  67.5 0.1 reshape.130
  67.6 0.1 reshape.131.pair_ref
  67.7 0.0 collective-permute-done.7
  67.7 0.1 add_divide_fusion.inverse_ref
  67.8 7.8 %collective-permute-done.4 = f16[2,2,64,512]{3,2,1,0:T(8,128)(2,1)S(1)} collective-permute-done((f16[2,2,64,512]{3,2,1,0:T(8,128)(2,1)S(1)}, f16[2,2,64,512]{3,2,1,0:T(8,128)(2,1)S(1)}, u32[]{:S(2)}, u32[]{:S(2)}) %collective-permute-start.4) | collective-permute-done | bytes 262176 | tf_op jit(solution)/shard_map/ppermute | solution.py:142
  75.5 3.0 %collective-permute-done.6 = f16[2,2,64,512]{3,2,1,0:T(8,128)(2,1)S(1)} collective-permute-done((f16[2,2,64,512]{3,2,1,0:T(8,128)(2,1)S(1)}, f16[2,2,64,512]{3,2,1,0:T(8,128)(2,1)S(1)}, u32[]{:S(2)}, u32[]{:S(2)}) %collective-permute-start.6) | collective-permute-done | bytes 262176 | tf_op jit(solution)/shard_map/ppermute | solution.py:142
  78.5 1.2 %convert_add_fusion.sum_ref = f32[2,2,64,512]{3,2,1,0:T(8,128)S(1)} fusion(f16[2,2,64,512]{3,2,1,0:T(8,128)(2,1)S(1)} %collective-permute-done.6, f16[2,2,64,512]{3,2,1,0:T(8,128)(2,1)S(1)} %collective-permute-done.4, f32[2,2,64,512]{3,2,1,0:T(8,128)S(1)} %copy-done.9, f16[4,2,64,512]{3,2,1,0:T(8,128)(2,1)S(1)} %collective-permute-done.2, ...), kind=kLoop, calls=%fused_computation.4 | loop fusion | flops 1048576 | bytes 2097152 | tf_op jit(solution)/shard_map/add | solution.py:156
  79.7 1.4 %pack.1 = bf16[32,32,128]{2,1,0:T(8,128)(2,1)} custom-call(f32[2,2,64,512]{3,2,1,0:T(8,128)S(1)} %convert_add_fusion.sum_ref, f32[2,64,512]{2,1,0:T(8,128)S(1)} %add_divide_fusion.inverse_ref), custom_call_target="tpu_custom_call" | custom-call | tf_op jit(solution)/shard_map/pack/pallas_call | solution.py:233
  81.1 10.3 %all-to-all-start.1 = ((bf16[32,32,128]{2,1,0:T(8,128)(2,1)}), bf16[32,32,128]{2,1,0:T(8,128)(2,1)S(1)}, u32[]{:S(2)}, u32[]{:S(2)}) async-start(bf16[32,32,128]{2,1,0:T(8,128)(2,1)} %pack.1), calls=%async_computation.1 | async-start | bytes 524288 | tf_op jit(solution)/shard_map/all_to_all | solution.py:344
  91.4 0.1 broadcast_multiply_fusion
  91.5 2.3 %multiply_sine_fusion = (f32[16,40,256]{2,1,0:T(8,128)S(1)}, f32[16,40,256]{2,1,0:T(8,128)S(1)}) fusion(f32[256]{0:T(256)S(1)} %multiply_add_fusion, f32[16,40]{1,0:T(8,128)S(1)} %broadcast_multiply_fusion), kind=kLoop, calls=%fused_computation.2 | loop fusion | flops 163840 | bytes 1314304 | tf_op jit(solution)/shard_map/sin | solution.py:192
  93.8 9.1 %all-to-all-done.1.block_ref = bf16[32,32,128]{2,1,0:T(8,128)(2,1)S(1)} async-done(((bf16[32,32,128]{2,1,0:T(8,128)(2,1)}), bf16[32,32,128]{2,1,0:T(8,128)(2,1)S(1)}, u32[]{:S(2)}, u32[]{:S(2)}) %all-to-all-start.1) | async-done | bytes 262176 | tf_op jit(solution)/shard_map/all_to_all | solution.py:344
  103.0 3.2 %beam.1 = f32[16,2,4,512]{3,2,1,0:T(4,128)} custom-call(bf16[32,32,128]{2,1,0:T(8,128)(2,1)S(1)} %all-to-all-done.1.block_ref, s32[2,1024]{1,0:T(2,128)S(1)} %reshape.131.pair_ref, s32[1024,2]{1,0:T(8,128)S(1)} %bitcast.9, f32[16,40,256]{2,1,0:T(8,128)S(1)} %get-tuple-element.26.cos_ref, f32[16,40,256]{2,1,0:T(8,128)S(1)} %get-tuple-element.25.sin_ref), custom_call_target="tpu_custom_call" | custom-call | tf_op jit(solution)/shard_map/beam/pallas_call | solution.py:318
  (22 shorter events, 0.1 us)
Async XLA Ops:
  0.0 12.1 %copy-start.1 = (f32[1,64,512]{2,1,0:T(8,128)S(1)}, f32[1,64,512]{2,1,0:T(8,128)}, u32[]{:S(2)}) copy-start(f32[1,64,512]{2,1,0:T(8,128)} %param.6) | copy-start | bytes 393220
  0.0 17.1 %copy-start.13 = (s32[16]{0:T(128)S(1)}, s32[16]{0:T(128)}, u32[]{:S(2)}) copy-start(s32[16]{0:T(128)} %offset_ref.3) | copy-start | bytes 196
  0.0 17.3 %copy-start = (bf16[1,16,2,64,512]{4,3,2,1,0:T(8,128)(2,1)S(1)}, bf16[1,16,2,64,512]{4,3,2,1,0:T(8,128)(2,1)}, u32[]{:S(2)}) copy-start(bf16[1,16,2,64,512]{4,3,2,1,0:T(8,128)(2,1)} %param.5) | copy-start | bytes 6291460
  3.3 14.0 %collective-permute-start = (bf16[9,2,64,512]{3,2,1,0:T(8,128)(2,1)}, bf16[9,2,64,512]{3,2,1,0:T(8,128)(2,1)S(1)}, u32[]{:S(2)}, u32[]{:S(2)}) collective-permute-start(bf16[9,2,64,512]{3,2,1,0:T(8,128)(2,1)} %select.3), channel_id=1, source_target_pairs={{0,32},{32,0},{64,96},{96,64},{128,160},{160,128},{192,224},{224,1... | collective-permute-start | bytes 3538952 | tf_op jit(solution)/shard_map/ppermute | solution.py:334
  12.9 41.4 %all-to-all-start = ((f16[8,64,512]{2,1,0:T(8,128)(2,1)}), f16[8,64,512]{2,1,0:T(8,128)(2,1)}, u32[]{:S(2)}, u32[]{:S(2)}) async-start(f16[8,64,512]{2,1,0:T(8,128)(2,1)} %broadcast_in_dim.5), calls=%async_computation | async-start | bytes 1048576 | tf_op jit(solution)/shard_map/all_to_all | solution.py:168
  19.5 1.0 copy-start.2
  20.5 0.7 copy-start.10
  21.2 0.7 copy-start.12
  21.9 0.8 copy-start.4
  21.9 4.1 %copy-start.6 = (f32[2,2,64,512]{3,2,1,0:T(8,128)}, f32[2,2,64,512]{3,2,1,0:T(8,128)S(1)}, u32[]{:S(2)}) copy-start(f32[2,2,64,512]{3,2,1,0:T(8,128)S(1)} %get-tuple-element.17) | copy-start | bytes 1572868
  21.9 4.2 %copy-start.8 = (f32[2,2,64,512]{3,2,1,0:T(8,128)}, f32[2,2,64,512]{3,2,1,0:T(8,128)S(1)}, u32[]{:S(2)}) copy-start(f32[2,2,64,512]{3,2,1,0:T(8,128)S(1)} %get-tuple-element.14) | copy-start | bytes 1572868
  21.9 9.9 %copy-start.3 = (f32[4,2,64,512]{3,2,1,0:T(8,128)S(1)}, f32[4,2,64,512]{3,2,1,0:T(8,128)}, u32[]{:S(2)}) copy-start(f32[4,2,64,512]{3,2,1,0:T(8,128)} %copy-done.2) | copy-start | bytes 3145732
  21.9 13.5 %copy-start.11 = (f32[1,2,64,512]{3,2,1,0:T(8,128)S(1)}, f32[1,2,64,512]{3,2,1,0:T(8,128)}, u32[]{:S(2)}) copy-start(f32[1,2,64,512]{3,2,1,0:T(8,128)} %copy-done.10) | copy-start | bytes 786436
  22.7 25.3 %collective-permute-start.1 = (f16[4,2,64,512]{3,2,1,0:T(8,128)(2,1)S(1)}, f16[4,2,64,512]{3,2,1,0:T(8,128)(2,1)}, u32[]{:S(2)}, u32[]{:S(2)}) collective-permute-start(f16[4,2,64,512]{3,2,1,0:T(8,128)(2,1)S(1)} %convert_element_type.80), channel_id=1, source_target_pairs={{0,64},{32,96},{64,128},{96,160},{128,192},{160,224},{192,256},{22... | collective-permute-start | bytes 1572872 | tf_op jit(solution)/shard_map/ppermute | solution.py:142
  26.1 28.1 %copy-start.5 = (f32[2,2,64,512]{3,2,1,0:T(8,128)S(1)}, f32[2,2,64,512]{3,2,1,0:T(8,128)}, u32[]{:S(2)}) copy-start(f32[2,2,64,512]{3,2,1,0:T(8,128)} %copy-done.4) | copy-start | bytes 1572868
  26.1 21.9 %copy-start.7 = (f32[2,2,64,512]{3,2,1,0:T(8,128)S(1)}, f32[2,2,64,512]{3,2,1,0:T(8,128)}, u32[]{:S(2)}) copy-start(f32[2,2,64,512]{3,2,1,0:T(8,128)} %copy-done.6) | copy-start | bytes 1572868
  27.8 20.1 %collective-permute-start.3 = (f16[1,2,64,512]{3,2,1,0:T(8,128)(2,1)}, f16[1,2,64,512]{3,2,1,0:T(8,128)(2,1)S(1)}, u32[]{:S(2)}, u32[]{:S(2)}) collective-permute-start(f16[1,2,64,512]{3,2,1,0:T(8,128)(2,1)} %convert_element_type.85), channel_id=1, source_target_pairs={{0,128},{32,160},{64,192},{96,224},{128,256},{160,288},{192,320},{... | collective-permute-start | bytes 393224 | tf_op jit(solution)/shard_map/ppermute | solution.py:142
  32.0 22.2 %collective-permute-start.2 = (f16[4,2,64,512]{3,2,1,0:T(8,128)(2,1)S(1)}, f16[4,2,64,512]{3,2,1,0:T(8,128)(2,1)S(1)}, u32[]{:S(2)}, u32[]{:S(2)}) collective-permute-start(f16[4,2,64,512]{3,2,1,0:T(8,128)(2,1)S(1)} %convert_element_type.82), channel_id=1, source_target_pairs={{0,448},{32,480},{64,0},{96,32},{128,64},{160,96},{192,128},{224,1... | collective-permute-start | bytes 1572872 | tf_op jit(solution)/shard_map/ppermute | solution.py:142
  35.5 18.7 %collective-permute-start.5 = (f16[1,2,64,512]{3,2,1,0:T(8,128)(2,1)S(1)}, f16[1,2,64,512]{3,2,1,0:T(8,128)(2,1)S(1)}, u32[]{:S(2)}, u32[]{:S(2)}) collective-permute-start(f16[1,2,64,512]{3,2,1,0:T(8,128)(2,1)S(1)} %convert_element_type.89), channel_id=1, source_target_pairs={{0,384},{32,416},{64,448},{96,480},{128,0},{160,32},{192,64},{224,... | collective-permute-start | bytes 393224 | tf_op jit(solution)/shard_map/ppermute | solution.py:142
  54.2 12.9 %copy-start.14 = (s32[2048]{0:T(1024)S(1)}, s32[2048]{0:T(1024)}, u32[]{:S(2)}) copy-start(s32[2048]{0:T(1024)} %param.9) | copy-start | bytes 24580
  54.3 13.2 %copy-start.15 = (s32[2048]{0:T(1024)S(1)}, s32[2048]{0:T(1024)}, u32[]{:S(2)}) copy-start(s32[2048]{0:T(1024)} %param.8) | copy-start | bytes 24580
  54.3 24.2 %copy-start.9 = (f32[2,2,64,512]{3,2,1,0:T(8,128)S(1)}, f32[2,2,64,512]{3,2,1,0:T(8,128)}, u32[]{:S(2)}) copy-start(f32[2,2,64,512]{3,2,1,0:T(8,128)} %copy-done.8) | copy-start | bytes 1572868
  55.9 11.8 %collective-permute-start.7 = (f32[2,64,512]{2,1,0:T(8,128)S(1)}, f32[2,64,512]{2,1,0:T(8,128)S(1)}, u32[]{:S(2)}, u32[]{:S(2)}) collective-permute-start(f32[2,64,512]{2,1,0:T(8,128)S(1)} %get-tuple-element.23), channel_id=1, source_target_pairs={{0,32},{32,0},{64,96},{96,64},{128,160},{160,128},{192,224},{224,1... | collective-permute-start | bytes 786440 | tf_op jit(solution)/shard_map/ppermute | solution.py:183
  59.6 15.9 %collective-permute-start.4 = (f16[2,2,64,512]{3,2,1,0:T(8,128)(2,1)S(1)}, f16[2,2,64,512]{3,2,1,0:T(8,128)(2,1)S(1)}, u32[]{:S(2)}, u32[]{:S(2)}) collective-permute-start(f16[2,2,64,512]{3,2,1,0:T(8,128)(2,1)S(1)} %add_convert_fusion.1), channel_id=1, source_target_pairs={{0,128},{32,160},{64,192},{96,224},{128,256},{160,288},{192,320},{... | collective-permute-start | bytes 786440 | tf_op jit(solution)/shard_map/ppermute | solution.py:142
  63.0 15.5 %collective-permute-start.6 = (f16[2,2,64,512]{3,2,1,0:T(8,128)(2,1)S(1)}, f16[2,2,64,512]{3,2,1,0:T(8,128)(2,1)S(1)}, u32[]{:S(2)}, u32[]{:S(2)}) collective-permute-start(f16[2,2,64,512]{3,2,1,0:T(8,128)(2,1)S(1)} %add_convert_fusion), channel_id=1, source_target_pairs={{0,384},{32,416},{64,448},{96,480},{128,0},{160,32},{192,64},{224,... | collective-permute-start | bytes 786440 | tf_op jit(solution)/shard_map/ppermute | solution.py:142
  81.1 21.9 %all-to-all-start.1 = ((bf16[32,32,128]{2,1,0:T(8,128)(2,1)}), bf16[32,32,128]{2,1,0:T(8,128)(2,1)S(1)}, u32[]{:S(2)}, u32[]{:S(2)}) async-start(bf16[32,32,128]{2,1,0:T(8,128)(2,1)} %pack.1), calls=%async_computation.1 | async-start | bytes 524288 | tf_op jit(solution)/shard_map/all_to_all | solution.py:344
where the time goes:
time: 107 us; the launch traced here: 106 us
  starting transfers between devices  47 us (44%)
  waiting for transfers between devices  35.5 us (33%)
  Pallas kernels  10.1 us (9%)
  other arithmetic  8.5 us (8%)
  local copies, waits for them, and re-layouts  4.7 us (4%)
    ppermute x6, waiting for transfers between devices, send(): return lax.ppermute(values.astype(F16), 'day', pairs)  26.3 us
    ppermute x6, starting transfers between devices, send(): return lax.ppermute(values.astype(F16), 'day', pairs)  20.2 us
    all_to_all x1, starting transfers between devices, beam_stage(): lax.all_to_all(packed, 'bl', split_axis=0, concat_axis=0, tiled=True)  10.3 us
    all_to_all x1, waiting for transfers between devices, beam_stage(): lax.all_to_all(packed, 'bl', split_axis=0, concat_axis=0, tiled=True)  9.14 us
    ppermute x1, starting transfers between devices, day_stage(): lax.ppermute(select(day_offset, day_weight, visibility), 'day', SWAP)  8.78 us
    all_to_all x1, starting transfers between devices, gather_weights(): lax.all_to_all(copies, 'day', split_axis=0, concat_axis=0, axis_index_gro...  4.14 us
    ppermute x1, starting transfers between devices, inverse_total(): other = lax.ppermute(partial_total(day ^ 1), 'day', SWAP)  3.66 us
    pallas_call x1, Pallas kernels, select(): pl.pallas_call(select_kernel, in_specs=[pl.BlockSpec(memory_space=pltpu.S...  3.25 us
  transfers between devices with their start and end apart: 10, of which 5 were waited for; matrix products, arithmetic and copies ran while one was open for 7% of the time, Pallas kernels for 2%

commit v1 on v0

--- a/solution.py
+++ b/solution.py
@@ -79,39 +79,25 @@
     )(day_offset, day_weight, visibility)
 
 
-SENDS = (
-    ((3, 0), (3, 1), (1, 0), (1, 1)),
-    ((5, 0), (5, 1), (7, 0), (7, 1)),
-    ((4, 0),),
-    ((4, 1),),
-    ((2, 0), (2, 1)),
-    ((6, 0), (6, 1)),
-    ((0, 0), (0, 1)),
-)
-
-
-def chip_kernel(offset_ref, vis_ref, weight_ref, other_ref, *out_refs):
+def chip_kernel(offset_ref, vis_ref, weight_ref, other_ref, out_ref):
     day = lax.axis_index("day")
     core = day & 1
-    chip = day >> 1
     offset = offset_ref[day]
     first = bins_below(offset_ref[day ^ 1], core)
     weight = weight_ref[...] * SCALE
     other_weight = (other_ref[HELD, 0].astype(F32) + other_ref[HELD, 1].astype(F32)) * SCALE
-    for out_ref, bins in zip(out_refs, SENDS):
-        for at, (distance, which) in enumerate(bins):
-            owned = 2 * ((chip + distance) & (CHIPS - 1)) + which
-            sample = 4 * (owned >> 1) + 2 * core + which - offset
-            valid = jnp.logical_and(sample >= 0, sample < SAMPLES)
-            held = jnp.logical_and(owned >= first, owned < first + HELD)
-            sample = jnp.clip(sample, 0, SAMPLES - 1)
-            own = weight * jnp.where(valid, 1.0, 0.0)
-            other = other_weight * jnp.where(held, 1.0, 0.0)
-            for x in range(2):
-                out_ref[at, x] = (
-                    vis_ref[sample, x].astype(F32) * own
-                    + other_ref[owned & (HELD - 1), x].astype(F32) * other
-                )
+    for owned in range(2 * CHIPS):
+        sample = 4 * (owned >> 1) + 2 * core + (owned & 1) - offset
+        valid = jnp.logical_and(sample >= 0, sample < SAMPLES)
+        held = jnp.logical_and(owned >= first, owned < first + HELD)
+        sample = jnp.clip(sample, 0, SAMPLES - 1)
+        own = weight * jnp.where(valid, 1.0, 0.0)
+        other = other_weight * jnp.where(held, 1.0, 0.0)
+        for x in range(2):
+            out_ref[owned, x] = (
+                vis_ref[sample, x].astype(F32) * own
+                + other_ref[owned & (HELD - 1), x].astype(F32) * other
+            )
 
 
 def chip_sums(day_offset, visibility, day_weight, other):
@@ -126,62 +112,34 @@
             pl.BlockSpec((rows, FREQ), lambda i: (i, 0)),
             block(HELD + 1),
         ],
-        out_specs=[block(len(bins)) for bins in SENDS],
-        out_shape=[
-            jax.ShapeDtypeStruct((len(bins), 2, BASE_LOC, FREQ), F32) for bins in SENDS
-        ],
+        out_specs=block(2 * CHIPS),
+        out_shape=jax.ShapeDtypeStruct((2 * CHIPS, 2, BASE_LOC, FREQ), F32),
         compiler_params=pltpu.CompilerParams(vmem_limit_bytes=16 * MIB),
         name="chip_sums",
     )(day_offset, visibility, day_weight, other)
 
 
-def send(values, distance):
-    pairs = [
-        (2 * y + c, 2 * ((y + distance) % CHIPS) + c) for y in range(CHIPS) for c in range(2)
-    ]
-    return lax.ppermute(values.astype(F16), "day", pairs)
-
-
-def reduce_ring(sums, late):
-    near_up, near_down = send(sums[0], 1), send(sums[1], -1)
-    far_up, far_down = send(sums[2], 2), send(sums[3], -2)
-    middle_up = sums[4] + near_up[:2].astype(F32)
-    middle_up = middle_up + jnp.pad(far_up.astype(F32), ((0, 1), (0, 0), (0, 0), (0, 0)))
-    middle_down = sums[5] + near_down[:2].astype(F32)
-    middle_down = middle_down + jnp.pad(far_down.astype(F32), ((1, 0), (0, 0), (0, 0), (0, 0)))
-    middle_up, middle_down = middle_up.astype(F16), middle_down.astype(F16)
-    late = lax.optimization_barrier((*late, middle_up, middle_down))[:-2]
-    last_up, last_down = send(middle_up, 2), send(middle_down, -2)
-    summed = (
-        sums[6]
-        + near_up[2:].astype(F32)
-        + near_down[2:].astype(F32)
-        + last_up.astype(F32)
-        + last_down.astype(F32)
+def along_day(blocks):
+    same = [[2 * y + c for y in range(CHIPS)] for c in range(2)]
+    return lax.all_to_all(
+        blocks, "day", split_axis=0, concat_axis=0, axis_index_groups=same, tiled=True
     )
-    return summed, late
 
 
 def gather_weights(day_weight):
-    same = [[2 * y + c for y in range(CHIPS)] for c in range(2)]
-    copies = jnp.broadcast_to(day_weight.astype(F16)[None], (CHIPS, BASE_LOC, FREQ))
-    return lax.all_to_all(
-        copies, "day", split_axis=0, concat_axis=0, axis_index_groups=same, tiled=True
-    )
-
-
-def inverse_total(day_offset, weights):
+    return along_day(jnp.broadcast_to(day_weight.astype(F16)[None], (CHIPS, BASE_LOC, FREQ)))
+
+
+def partial_totals(day_offset, weights):
     day = lax.axis_index("day")
     offsets = jnp.where((day & 1) == 0, day_offset[0::2], day_offset[1::2])
     weights = weights.astype(F32)
-
-    def partial_total(owner):
+    totals = []
+    for owner in (day, day ^ 1):
         sample = (owner * RA_DEV + jnp.arange(RA_DEV))[:, None] - offsets[None, :]
         valid = jnp.logical_and(sample >= 0, sample < SAMPLES).astype(F32)
-        return jnp.sum(valid[:, :, None, None] * weights[None], axis=1)
-
-    other = lax.ppermute(partial_total(day ^ 1), "day", SWAP)
-    return (1.0 / SCALE) / (partial_total(day) + other)
+        totals.append(jnp.sum(valid[:, :, None, None] * weights[None], axis=1))
+    return totals
 
 
 def base_angles(freq_at):
@@ -333,9 +291,12 @@
     visibility, day_weight = visibility[0], day_weight[0]
     other = lax.ppermute(select(day_offset, day_weight, visibility), "day", SWAP)
     weights = gather_weights(day_weight)
-    sums = chip_sums(day_offset, visibility, day_weight, other)
-    summed, (weights, freq_at) = reduce_ring(sums, (weights, freq_at))
-    return summed, inverse_total(day_offset, weights), freq_at
+    sums = chip_sums(day_offset, visibility, day_weight, other).astype(F16)
+    weights, freq_at, _ = lax.optimization_barrier((weights, freq_at, sums))
+    sums = along_day(sums.reshape(CHIPS, RA_DEV, 2, BASE_LOC, FREQ))
+    mine, theirs = partial_totals(day_offset, weights)
+    inverse = (1.0 / SCALE) / (mine + lax.ppermute(theirs, "day", SWAP))
+    return jnp.sum(sums.astype(F32), axis=0), inverse, freq_at
 
 
 def beam_stage(summed, inverse, pair_index, sep_index, freq_at):

time: 107 us -> 119 us (1.11)
  the two profiles are of different devices: /device:TPU:1 before, /device:TPU:8 now
where the time goes in v1:
time: 119 us
  waiting for transfers between devices  68.8 us (58%)
  starting transfers between devices  29.9 us (25%)
  Pallas kernels  10 us (8%)
  other arithmetic  8.11 us (7%)
  local copies, waits for them, and re-layouts  1.61 us (1%)
    all_to_all x2, waiting for transfers between devices, along_day(): lax.all_to_all(blocks, 'day', split_axis=0, concat_axis=0, axis_index_gro...  58.1 us
    all_to_all x2, starting transfers between devices, along_day(): lax.all_to_all(blocks, 'day', split_axis=0, concat_axis=0, axis_index_gro...  15.6 us
    all_to_all x1, starting transfers between devices, beam_stage(): lax.all_to_all(packed, 'bl', split_axis=0, concat_axis=0, tiled=True)  10.6 us
    all_to_all x1, waiting for transfers between devices, beam_stage(): lax.all_to_all(packed, 'bl', split_axis=0, concat_axis=0, tiled=True)  9.9 us
    pallas_call x1, Pallas kernels, select(): pl.pallas_call(select_kernel, in_specs=[pl.BlockSpec(memory_space=pltpu.S...  3.23 us
    pallas_call x1, Pallas kernels, beam(): pl.pallas_call(beam_kernel, in_specs=[vmem] * 5, out_specs=vmem, out_shap...  3.22 us
  transfers between devices with their start and end apart: 5, of which 4 were waited for; matrix products, arithmetic and copies ran while one was open for 6% of the time, Pallas kernels for 2%

profile of v1, /device:TPU:8, one launch (start us, length us, event | category | flops | bytes accessed | tf_op | source)
XLA Modules:
  0.0 118.7 jit_solution(2380471546471908329)
XLA Ops:
  0.0 0.0 copy-start.1
  0.0 0.0 copy-start
  0.0 0.0 copy-start.2
  0.0 3.2 %select.1 = bf16[9,2,64,512]{3,2,1,0:T(8,128)(2,1)} custom-call(s32[16]{0:T(128)} %offset_ref.3, f32[64,512]{1,0:T(8,128)} %bitcast.11, bf16[16,2,64,512]{3,2,1,0:T(8,128)(2,1)} %bitcast.8), custom_call_target="tpu_custom_call" | custom-call | tf_op jit(solution)/shard_map/select/pallas_call | solution.py:68
  3.3 1.9 %collective-permute-start = (bf16[9,2,64,512]{3,2,1,0:T(8,128)(2,1)}, bf16[9,2,64,512]{3,2,1,0:T(8,128)(2,1)S(1)}, u32[]{:S(2)}, u32[]{:S(2)}) collective-permute-start(bf16[9,2,64,512]{3,2,1,0:T(8,128)(2,1)} %select.1), channel_id=1, source_target_pairs={{0,32},{32,0},{64,96},{96,64},{128,160},{160,128},{192,224},{224,1... | collective-permute-start | bytes 3538952 | tf_op jit(solution)/shard_map/ppermute | solution.py:292
  5.2 0.0 copy-done.1
  5.2 0.9 broadcast_in_dim.5
  6.1 9.8 %all-to-all-start.1 = ((f16[8,64,512]{2,1,0:T(8,128)(2,1)}), f16[8,64,512]{2,1,0:T(8,128)(2,1)}, u32[]{:S(2)}, u32[]{:S(2)}) async-start(f16[8,64,512]{2,1,0:T(8,128)(2,1)} %broadcast_in_dim.5), calls=%async_computation.1 | async-start | bytes 1048576 | tf_op jit(solution)/shard_map/all_to_all | solution.py:124
  15.9 0.0 collective-permute-done.other_ref
  15.9 0.0 copy-done
  15.9 0.0 copy-done.2
  15.9 2.1 %chip_sums.1 = f32[16,2,64,512]{3,2,1,0:T(8,128)S(1)} custom-call(s32[16]{0:T(128)S(1)} %copy-done.2, bf16[16,2,64,512]{3,2,1,0:T(8,128)(2,1)S(1)} %bitcast.9, f32[64,512]{1,0:T(8,128)S(1)} %bitcast.12, bf16[9,2,64,512]{3,2,1,0:T(8,128)(2,1)S(1)} %collective-permute-done.other_ref), custom_call_target="tpu_custom_call" | custom-call | tf_op jit(solution)/shard_map/chip_sums/pallas_call | solution.py:106
  18.1 1.9 %convert_element_type.44 = f16[16,2,64,512]{3,2,1,0:T(8,128)(2,1)} convert(f32[16,2,64,512]{3,2,1,0:T(8,128)S(1)} %chip_sums.1) | non-fusion elementwise | flops 1048576 | bytes 6291456 | tf_op jit(solution)/shard_map/convert_element_type | solution.py:294
  20.0 13.0 %all-to-all-done.1 = f16[8,64,512]{2,1,0:T(8,128)(2,1)} async-done(((f16[8,64,512]{2,1,0:T(8,128)(2,1)}), f16[8,64,512]{2,1,0:T(8,128)(2,1)}, u32[]{:S(2)}, u32[]{:S(2)}) %all-to-all-start.1) | async-done | bytes 524320 | tf_op jit(solution)/shard_map/all_to_all | solution.py:124
  33.0 5.7 %all-to-all-start = ((f16[8,2,2,64,512]{4,3,2,1,0:T(8,128)(2,1)}), f16[8,2,2,64,512]{4,3,2,1,0:T(8,128)(2,1)}, u32[]{:S(2)}, u32[]{:S(2)}) async-start(f16[8,2,2,64,512]{4,3,2,1,0:T(8,128)(2,1)} %bitcast.2), calls=%async_computation | async-start | bytes 4194304 | tf_op jit(solution)/shard_map/all_to_all | solution.py:124
  38.7 0.0 copy-start.3
  38.7 0.0 copy-start.4
  38.7 0.1 slice.6
  38.8 0.1 slice.7
  39.0 0.1 and_convert_fusion.1
  39.0 1.2 convert_element_type.49
  40.2 0.4 multiply_reduce_fusion
  40.6 1.9 %collective-permute-start.1 = (f32[2,64,512]{2,1,0:T(8,128)S(1)}, f32[2,64,512]{2,1,0:T(8,128)S(1)}, u32[]{:S(2)}, u32[]{:S(2)}) collective-permute-start(f32[2,64,512]{2,1,0:T(8,128)S(1)} %get-tuple-element.9), channel_id=1, source_target_pairs={{0,32},{32,0},{64,96},{96,64},{128,160},{160,128},{192,224},{224,1... | collective-permute-start | bytes 786440 | tf_op jit(solution)/shard_map/ppermute | solution.py:298
  42.5 0.0 copy-done.3
  42.5 0.1 reshape.134
  42.6 0.1 reshape.135.pair_ref
  42.7 0.0 copy-done.4
  42.7 0.1 reshape.136
  42.8 0.3 copy.9
  43.1 0.1 add_convert_fusion
  43.2 0.8 collective-permute-done.1
  44.0 0.1 add_divide_fusion.inverse_ref
  44.1 45.1 %all-to-all-done = f16[8,2,2,64,512]{4,3,2,1,0:T(8,128)(2,1)} async-done(((f16[8,2,2,64,512]{4,3,2,1,0:T(8,128)(2,1)}), f16[8,2,2,64,512]{4,3,2,1,0:T(8,128)(2,1)}, u32[]{:S(2)}, u32[]{:S(2)}) %all-to-all-start) | async-done | bytes 2097184 | tf_op jit(solution)/shard_map/all_to_all | solution.py:124
  89.1 2.0 %convert_reduce_fusion.sum_ref = f32[2,2,64,512]{3,2,1,0:T(8,128)S(1)} fusion(f16[8,2,2,64,512]{4,3,2,1,0:T(8,128)(2,1)} %all-to-all-done), kind=kLoop, calls=%fused_computation | loop fusion | flops 1966080 | bytes 2621440 | tf_op jit(solution)/shard_map/reduce_sum | solution.py:299
  91.1 1.4 %pack.1 = bf16[32,32,128]{2,1,0:T(8,128)(2,1)} custom-call(f32[2,2,64,512]{3,2,1,0:T(8,128)S(1)} %convert_reduce_fusion.sum_ref, f32[2,64,512]{2,1,0:T(8,128)S(1)} %add_divide_fusion.inverse_ref), custom_call_target="tpu_custom_call" | custom-call | tf_op jit(solution)/shard_map/pack/pallas_call | solution.py:191
  92.5 10.6 %all-to-all-start.2 = ((bf16[32,32,128]{2,1,0:T(8,128)(2,1)}), bf16[32,32,128]{2,1,0:T(8,128)(2,1)S(1)}, u32[]{:S(2)}, u32[]{:S(2)}) async-start(bf16[32,32,128]{2,1,0:T(8,128)(2,1)} %pack.1), calls=%async_computation.2 | async-start | bytes 524288 | tf_op jit(solution)/shard_map/all_to_all | solution.py:305
  103.1 0.1 broadcast_multiply_fusion
  103.2 2.3 %multiply_sine_fusion = (f32[16,40,256]{2,1,0:T(8,128)S(1)}, f32[16,40,256]{2,1,0:T(8,128)S(1)}) fusion(f32[256]{0:T(256)S(1)} %multiply_add_fusion, f32[16,40]{1,0:T(8,128)S(1)} %broadcast_multiply_fusion), kind=kLoop, calls=%fused_computation.3 | loop fusion | flops 163840 | bytes 1314304 | tf_op jit(solution)/shard_map/sin | solution.py:150
  105.5 9.9 %all-to-all-done.2.block_ref = bf16[32,32,128]{2,1,0:T(8,128)(2,1)S(1)} async-done(((bf16[32,32,128]{2,1,0:T(8,128)(2,1)}), bf16[32,32,128]{2,1,0:T(8,128)(2,1)S(1)}, u32[]{:S(2)}, u32[]{:S(2)}) %all-to-all-start.2) | async-done | bytes 262176 | tf_op jit(solution)/shard_map/all_to_all | solution.py:305
  115.5 3.2 %beam.1 = f32[16,2,4,512]{3,2,1,0:T(4,128)} custom-call(bf16[32,32,128]{2,1,0:T(8,128)(2,1)S(1)} %all-to-all-done.2.block_ref, s32[2,1024]{1,0:T(2,128)S(1)} %reshape.135.pair_ref, s32[1024,2]{1,0:T(8,128)S(1)} %bitcast.10, f32[16,40,256]{2,1,0:T(8,128)S(1)} %get-tuple-element.12.cos_ref, f32[16,40,256]{2,1,0:T(8,128)S(1)} %get-tuple-element.11.sin_ref), custom_call_target="tpu_custom_call" | custom-call | tf_op jit(solution)/shard_map/beam/pallas_call | solution.py:276
  (9 shorter events, 0.1 us)
Async XLA Ops:
  0.0 5.2 %copy-start.1 = (f32[1,64,512]{2,1,0:T(8,128)S(1)}, f32[1,64,512]{2,1,0:T(8,128)}, u32[]{:S(2)}) copy-start(f32[1,64,512]{2,1,0:T(8,128)} %param.6) | copy-start | bytes 393220
  0.0 15.9 %copy-start = (bf16[1,16,2,64,512]{4,3,2,1,0:T(8,128)(2,1)S(1)}, bf16[1,16,2,64,512]{4,3,2,1,0:T(8,128)(2,1)}, u32[]{:S(2)}) copy-start(bf16[1,16,2,64,512]{4,3,2,1,0:T(8,128)(2,1)} %param.5) | copy-start | bytes 6291460
  0.0 15.9 %copy-start.2 = (s32[16]{0:T(128)S(1)}, s32[16]{0:T(128)}, u32[]{:S(2)}) copy-start(s32[16]{0:T(128)} %offset_ref.3) | copy-start | bytes 196
  3.3 12.7 %collective-permute-start = (bf16[9,2,64,512]{3,2,1,0:T(8,128)(2,1)}, bf16[9,2,64,512]{3,2,1,0:T(8,128)(2,1)S(1)}, u32[]{:S(2)}, u32[]{:S(2)}) collective-permute-start(bf16[9,2,64,512]{3,2,1,0:T(8,128)(2,1)} %select.1), channel_id=1, source_target_pairs={{0,32},{32,0},{64,96},{96,64},{128,160},{160,128},{192,224},{224,1... | collective-permute-start | bytes 3538952 | tf_op jit(solution)/shard_map/ppermute | solution.py:292
  6.1 26.9 %all-to-all-start.1 = ((f16[8,64,512]{2,1,0:T(8,128)(2,1)}), f16[8,64,512]{2,1,0:T(8,128)(2,1)}, u32[]{:S(2)}, u32[]{:S(2)}) async-start(f16[8,64,512]{2,1,0:T(8,128)(2,1)} %broadcast_in_dim.5), calls=%async_computation.1 | async-start | bytes 1048576 | tf_op jit(solution)/shard_map/all_to_all | solution.py:124
  33.0 56.1 %all-to-all-start = ((f16[8,2,2,64,512]{4,3,2,1,0:T(8,128)(2,1)}), f16[8,2,2,64,512]{4,3,2,1,0:T(8,128)(2,1)}, u32[]{:S(2)}, u32[]{:S(2)}) async-start(f16[8,2,2,64,512]{4,3,2,1,0:T(8,128)(2,1)} %bitcast.2), calls=%async_computation | async-start | bytes 4194304 | tf_op jit(solution)/shard_map/all_to_all | solution.py:124
  38.7 3.8 %copy-start.3 = (s32[2048]{0:T(1024)S(1)}, s32[2048]{0:T(1024)}, u32[]{:S(2)}) copy-start(s32[2048]{0:T(1024)} %param.8) | copy-start | bytes 24580
  38.7 4.0 %copy-start.4 = (s32[2048]{0:T(1024)S(1)}, s32[2048]{0:T(1024)}, u32[]{:S(2)}) copy-start(s32[2048]{0:T(1024)} %param.9) | copy-start | bytes 24580
  40.6 3.4 %collective-permute-start.1 = (f32[2,64,512]{2,1,0:T(8,128)S(1)}, f32[2,64,512]{2,1,0:T(8,128)S(1)}, u32[]{:S(2)}, u32[]{:S(2)}) collective-permute-start(f32[2,64,512]{2,1,0:T(8,128)S(1)} %get-tuple-element.9), channel_id=1, source_target_pairs={{0,32},{32,0},{64,96},{96,64},{128,160},{160,128},{192,224},{224,1... | collective-permute-start | bytes 786440 | tf_op jit(solution)/shard_map/ppermute | solution.py:298
  92.5 22.9 %all-to-all-start.2 = ((bf16[32,32,128]{2,1,0:T(8,128)(2,1)}), bf16[32,32,128]{2,1,0:T(8,128)(2,1)S(1)}, u32[]{:S(2)}, u32[]{:S(2)}) async-start(bf16[32,32,128]{2,1,0:T(8,128)(2,1)} %pack.1), calls=%async_computation.2 | async-start | bytes 524288 | tf_op jit(solution)/shard_map/all_to_all | solution.py:305

commit v2 on v0

--- a/solution.py
+++ b/solution.py
@@ -37,30 +37,37 @@
     return 2 * (offset >> 2) + jnp.clip((offset & 3) - 2 * core, 0, 2)
 
 
-def select_kernel(offset_ref, weight_ref, vis_ref, out_ref, weight_buf, sems):
+def select_kernel(offset_ref, weight_ref, vis_ref, out_ref, weight_buf, held_buf, sems):
     day = lax.axis_index("day")
     other = 1 - (day & 1)
     offset = offset_ref[day]
     first = bins_below(offset, other)
     load = pltpu.make_async_copy(weight_ref, weight_buf, sems.at[HELD])
     load.start()
-    copies = []
+    loads, stores = [], []
     for k in range(HELD):
         owned = first + k
         sample = 4 * (owned >> 1) + 2 * other + (owned & 1) - offset
-        copies.append(
-            pltpu.make_async_copy(
-                vis_ref.at[sample], out_ref.at[owned & (HELD - 1)], sems.at[k]
-            )
+        slot = owned & (HELD - 1)
+        loads.append(pltpu.make_async_copy(vis_ref.at[sample], held_buf.at[k], sems.at[k]))
+        loads[-1].start()
+        stores.append(
+            pltpu.make_async_copy(held_buf.at[k], out_ref.at[slot], sems.at[HELD + 1 + k])
         )
-        copies[-1].start()
     load.wait()
     weight = weight_buf[...]
     high = weight.astype(BF16)
-    out_ref[HELD, 0] = high
-    out_ref[HELD, 1] = (weight - high.astype(F32)).astype(BF16)
-    for copy in copies:
-        copy.wait()
+    held_buf[HELD, 0] = high
+    held_buf[HELD, 1] = (weight - high.astype(F32)).astype(BF16)
+    stores.append(
+        pltpu.make_async_copy(held_buf.at[HELD], out_ref.at[HELD], sems.at[2 * HELD + 1])
+    )
+    stores[-1].start()
+    for k in range(HELD):
+        loads[k].wait()
+        stores[k].start()
+    for store in stores:
+        store.wait()
 
 
 def select(day_offset, day_weight, visibility):
@@ -68,11 +75,12 @@
     return pl.pallas_call(
         select_kernel,
         in_specs=[pl.BlockSpec(memory_space=pltpu.SMEM), hbm, hbm],
-        out_specs=pl.BlockSpec(memory_space=pltpu.VMEM),
+        out_specs=hbm,
         out_shape=jax.ShapeDtypeStruct((HELD + 1, 2, BASE_LOC, FREQ), BF16),
         scratch_shapes=[
             pltpu.VMEM((BASE_LOC, FREQ), F32),
-            pltpu.SemaphoreType.DMA((HELD + 1,)),
+            pltpu.VMEM((HELD + 1, 2, BASE_LOC, FREQ), BF16),
+            pltpu.SemaphoreType.DMA((2 * HELD + 2,)),
         ],
         compiler_params=pltpu.CompilerParams(vmem_limit_bytes=60 * MIB),
         name="select",
@@ -139,19 +147,20 @@
     pairs = [
         (2 * y + c, 2 * ((y + distance) % CHIPS) + c) for y in range(CHIPS) for c in range(2)
     ]
-    return lax.ppermute(values.astype(F16), "day", pairs)
+    return lax.ppermute(values, "day", pairs)
 
 
 def reduce_ring(sums, late):
-    near_up, near_down = send(sums[0], 1), send(sums[1], -1)
-    far_up, far_down = send(sums[2], 2), send(sums[3], -2)
+    first = lax.optimization_barrier([part.astype(F16) for part in sums[:4]])
+    near_up, near_down = send(first[0], 1), send(first[1], -1)
+    far_up, far_down = send(first[2], 2), send(first[3], -2)
     middle_up = sums[4] + near_up[:2].astype(F32)
     middle_up = middle_up + jnp.pad(far_up.astype(F32), ((0, 1), (0, 0), (0, 0), (0, 0)))
     middle_down = sums[5] + near_down[:2].astype(F32)
     middle_down = middle_down + jnp.pad(far_down.astype(F32), ((1, 0), (0, 0), (0, 0), (0, 0)))
     middle_up, middle_down = middle_up.astype(F16), middle_down.astype(F16)
-    late = lax.optimization_barrier((*late, middle_up, middle_down))[:-2]
     last_up, last_down = send(middle_up, 2), send(middle_down, -2)
+    late = lax.optimization_barrier((late, last_up))[0]
     summed = (
         sums[6]
         + near_up[2:].astype(F32)
@@ -329,25 +338,25 @@
     )(block, pair, sep, *angles)
 
 
-def day_stage(visibility, day_weight, day_offset, freq_at):
+def day_stage(visibility, day_weight, day_offset):
     visibility, day_weight = visibility[0], day_weight[0]
     other = lax.ppermute(select(day_offset, day_weight, visibility), "day", SWAP)
     weights = gather_weights(day_weight)
     sums = chip_sums(day_offset, visibility, day_weight, other)
-    summed, (weights, freq_at) = reduce_ring(sums, (weights, freq_at))
-    return summed, inverse_total(day_offset, weights), freq_at
+    summed, weights = reduce_ring(sums, weights)
+    return summed, inverse_total(day_offset, weights)
 
 
 def beam_stage(summed, inverse, pair_index, sep_index, freq_at):
-    angles = base_angles(freq_at)
     packed = pack(summed, inverse)
+    angles = base_angles(lax.optimization_barrier((freq_at, packed))[0])
     block = lax.all_to_all(packed, "bl", split_axis=0, concat_axis=0, tiled=True)
     return beam(block, pair_index, sep_index, angles)
 
 
 def local(visibility, day_weight, day_offset, pair_index, sep_index):
     freq_at = (lax.axis_index("bl") * BAND + jnp.arange(BAND)).astype(F32)
-    summed, inverse, freq_at = day_stage(visibility, day_weight, day_offset, freq_at)
+    summed, inverse = day_stage(visibility, day_weight, day_offset)
     return beam_stage(summed, inverse, pair_index, sep_index, freq_at)
 
 

time: 107 us -> 99.7 us (0.932)
  the two profiles are of different devices: /device:TPU:1 before, /device:TPU:8 now
where the time goes in v2:
time: 99.7 us; the launch traced here: 98.9 us
  starting transfers between devices  44.7 us (45%)
  waiting for transfers between devices  27.7 us (28%)
  Pallas kernels  9.78 us (10%)
  other arithmetic  9.11 us (9%)
  local copies, waits for them, and re-layouts  7.28 us (7%)
    ppermute x6, starting transfers between devices, send(): return lax.ppermute(values, 'day', pairs)  21.8 us
    ppermute x6, waiting for transfers between devices, send(): return lax.ppermute(values, 'day', pairs)  16.5 us
    all_to_all x1, waiting for transfers between devices, beam_stage(): lax.all_to_all(packed, 'bl', split_axis=0, concat_axis=0, tiled=True)  11 us
    all_to_all x1, starting transfers between devices, gather_weights(): lax.all_to_all(copies, 'day', split_axis=0, concat_axis=0, axis_index_gro...  9.84 us
    all_to_all x1, starting transfers between devices, beam_stage(): lax.all_to_all(packed, 'bl', split_axis=0, concat_axis=0, tiled=True)  9.15 us
    pallas_call x1, Pallas kernels, beam(): pl.pallas_call(beam_kernel, in_specs=[vmem] * 5, out_specs=vmem, out_shap...  3.22 us
    pallas_call x1, Pallas kernels, select(): pl.pallas_call(select_kernel, in_specs=[pl.BlockSpec(memory_space=pltpu.S...  2.95 us
    sin x1, other arithmetic, base_angles(): return (jnp.cos(phase), jnp.sin(phase))  2.34 us
  transfers between devices with their start and end apart: 10, of which 4 were waited for; matrix products, arithmetic and copies ran while one was open for 15% of the time, Pallas kernels for 2%

profile of v2, /device:TPU:8, one launch (start us, length us, event | category | flops | bytes accessed | tf_op | source)
XLA Modules:
  0.0 98.9 jit_solution(14585975927180697683)
XLA Ops:
  0.0 3.0 %select.3 = bf16[9,2,64,512]{3,2,1,0:T(8,128)(2,1)} custom-call(s32[16]{0:T(128)} %offset_ref.3, f32[64,512]{1,0:T(8,128)} %bitcast.10, bf16[16,2,64,512]{3,2,1,0:T(8,128)(2,1)} %bitcast.7), custom_call_target="tpu_custom_call" | custom-call | tf_op jit(solution)/shard_map/select/pallas_call | solution.py:75
  3.0 1.9 %collective-permute-start = (bf16[9,2,64,512]{3,2,1,0:T(8,128)(2,1)}, bf16[9,2,64,512]{3,2,1,0:T(8,128)(2,1)S(1)}, u32[]{:S(2)}, u32[]{:S(2)}) collective-permute-start(bf16[9,2,64,512]{3,2,1,0:T(8,128)(2,1)} %select.3), channel_id=1, source_target_pairs={{0,32},{32,0},{64,96},{96,64},{128,160},{160,128},{192,224},{224,1... | collective-permute-start | bytes 3538952 | tf_op jit(solution)/shard_map/ppermute | solution.py:343
  4.9 0.0 copy-done.1
  4.9 0.9 broadcast_in_dim.5
  5.8 9.8 %all-to-all-start = ((f16[8,64,512]{2,1,0:T(8,128)(2,1)}), f16[8,64,512]{2,1,0:T(8,128)(2,1)}, u32[]{:S(2)}, u32[]{:S(2)}) async-start(f16[8,64,512]{2,1,0:T(8,128)(2,1)} %broadcast_in_dim.5), calls=%async_computation | async-start | bytes 1048576 | tf_op jit(solution)/shard_map/all_to_all | solution.py:177
  15.6 0.0 copy-done.7
  15.6 0.1 slice.22
  15.7 0.1 slice.23
  15.8 0.0 collective-permute-done.other_ref
  15.8 0.0 copy-done
  15.9 2.2 %chip_sums.1 = (f32[4,2,64,512]{3,2,1,0:T(8,128)S(1)}, f32[4,2,64,512]{3,2,1,0:T(8,128)S(1)}, f32[1,2,64,512]{3,2,1,0:T(8,128)S(1)}, f32[1,2,64,512]{3,2,1,0:T(8...) custom-call(s32[16]{0:T(128)S(1)} %copy-done.7, ...), custom_call_target="tpu_custom_call" | custom-call | tf_op jit(solution)/shard_map/chip_sums/pallas_call | solution.py:128
  18.1 0.0 copy-start.2
  18.1 0.0 copy-start.4
  18.1 0.0 copy-start.5
  18.1 0.0 copy-start.9
  18.1 0.0 copy-start.10
  18.1 0.1 convert_element_type.80
  18.2 0.1 convert_element_type.81
  18.3 0.5 copy-done.2
  18.9 0.2 copy-done.4
  19.1 0.2 copy-done.5
  19.3 3.4 %collective-permute-start.1 = (f16[4,2,64,512]{3,2,1,0:T(8,128)(2,1)S(1)}, f16[4,2,64,512]{3,2,1,0:T(8,128)(2,1)S(1)}, u32[]{:S(2)}, u32[]{:S(2)}) collective-permute-start(f16[4,2,64,512]{3,2,1,0:T(8,128)(2,1)S(1)} %convert_element_type.80), channel_id=1, source_target_pairs={{0,64},{32,96},{64,128},{96,160},{128,192},{160,224},{192,256},{22... | collective-permute-start | bytes 1572872 | tf_op jit(solution)/shard_map/ppermute | solution.py:150
  22.6 0.7 and_convert_fusion.1
  23.3 2.5 %collective-permute-start.2 = (f16[4,2,64,512]{3,2,1,0:T(8,128)(2,1)S(1)}, f16[4,2,64,512]{3,2,1,0:T(8,128)(2,1)S(1)}, u32[]{:S(2)}, u32[]{:S(2)}) collective-permute-start(f16[4,2,64,512]{3,2,1,0:T(8,128)(2,1)S(1)} %convert_element_type.81), channel_id=1, source_target_pairs={{0,448},{32,480},{64,0},{96,32},{128,64},{160,96},{192,128},{224,1... | collective-permute-start | bytes 1572872 | tf_op jit(solution)/shard_map/ppermute | solution.py:150
  25.8 0.5 iota_multiply_fusion
  26.3 4.9 %collective-permute-start.3 = (f16[1,2,64,512]{3,2,1,0:T(8,128)(2,1)S(1)}, f16[1,2,64,512]{3,2,1,0:T(8,128)(2,1)S(1)}, u32[]{:S(2)}, u32[]{:S(2)}) collective-permute-start(f16[1,2,64,512]{3,2,1,0:T(8,128)(2,1)S(1)} %convert_element_type.82), channel_id=1, source_target_pairs={{0,128},{32,160},{64,192},{96,224},{128,256},{160,288},{192,320},{... | collective-permute-start | bytes 393224 | tf_op jit(solution)/shard_map/ppermute | solution.py:150
  31.2 0.6 add_convert_fusion.3
  31.8 0.0 copy-done.9
  31.8 0.7 reshape.132
  32.5 1.0 %copy.9 = s32[32,32,2]{2,1,0:T(8,128)S(1)} copy(s32[32,32,2]{1,2,0:T(2,128)} %bitcast.12) | data formatting | bytes 16384 | tf_op jit(solution)/shard_map/transpose | solution.py:325
  33.5 0.0 copy-done.10
  33.5 0.7 reshape.130
  34.2 1.4 %copy.8 = s32[2,32,32]{2,1,0:T(8,128)} copy(s32[2,32,32]{2,0,1:T(2,128)} %bitcast.13) | data formatting | bytes 16384 | tf_op jit(solution)/shard_map/transpose | solution.py:324
  35.6 0.8 reshape.131.pair_ref
  36.4 0.6 multiply_add_fusion
  37.0 3.0 %collective-permute-start.5 = (f16[1,2,64,512]{3,2,1,0:T(8,128)(2,1)S(1)}, f16[1,2,64,512]{3,2,1,0:T(8,128)(2,1)S(1)}, u32[]{:S(2)}, u32[]{:S(2)}) collective-permute-start(f16[1,2,64,512]{3,2,1,0:T(8,128)(2,1)S(1)} %convert_element_type.83), channel_id=1, source_target_pairs={{0,384},{32,416},{64,448},{96,480},{128,0},{160,32},{192,64},{224,... | collective-permute-start | bytes 393224 | tf_op jit(solution)/shard_map/ppermute | solution.py:150
  40.0 7.7 %collective-permute-done.3 = f16[1,2,64,512]{3,2,1,0:T(8,128)(2,1)S(1)} collective-permute-done((f16[1,2,64,512]{3,2,1,0:T(8,128)(2,1)S(1)}, f16[1,2,64,512]{3,2,1,0:T(8,128)(2,1)S(1)}, u32[]{:S(2)}, u32[]{:S(2)}) %collective-permute-start.3) | collective-permute-done | bytes 131104 | tf_op jit(solution)/shard_map/ppermute | solution.py:150
  47.7 0.0 collective-permute-done.1
  47.7 0.7 copy-done.8
  48.4 1.2 %add_convert_fusion.1 = f16[2,2,64,512]{3,2,1,0:T(8,128)(2,1)S(1)} fusion(f32[2,2,64,512]{3,2,1,0:T(8,128)} %copy-done.4, f16[4,2,64,512]{3,2,1,0:T(8,128)(2,1)S(1)} %collective-permute-done.1, f16[1,2,64,512]{3,2,1,0:T(8,128)(2,1)} %copy-done.8), kind=kLoop, calls=%fused_computation.6 | loop fusion | flops 655360 | bytes 1179648 | tf_op jit(solution)/shard_map/convert_element_type | solution.py:161
  49.5 1.9 %collective-permute-start.4 = (f16[2,2,64,512]{3,2,1,0:T(8,128)(2,1)S(1)}, f16[2,2,64,512]{3,2,1,0:T(8,128)(2,1)S(1)}, u32[]{:S(2)}, u32[]{:S(2)}) collective-permute-start(f16[2,2,64,512]{3,2,1,0:T(8,128)(2,1)S(1)} %add_convert_fusion.1), channel_id=1, source_target_pairs={{0,128},{32,160},{64,192},{96,224},{128,256},{160,288},{192,320},{... | collective-permute-start | bytes 786440 | tf_op jit(solution)/shard_map/ppermute | solution.py:150
  51.4 0.0 collective-permute-done.5
  51.5 0.0 collective-permute-done.2
  51.5 0.0 copy-done.3
  51.5 0.0 copy-start.6
  51.5 0.1 add_convert_fusion
  51.6 6.2 %collective-permute-start.6 = (f16[2,2,64,512]{3,2,1,0:T(8,128)(2,1)S(1)}, f16[2,2,64,512]{3,2,1,0:T(8,128)(2,1)}, u32[]{:S(2)}, u32[]{:S(2)}) collective-permute-start(f16[2,2,64,512]{3,2,1,0:T(8,128)(2,1)S(1)} %add_convert_fusion), channel_id=1, source_target_pairs={{0,384},{32,416},{64,448},{96,480},{128,0},{160,32},{192,64},{224,... | collective-permute-start | bytes 786440 | tf_op jit(solution)/shard_map/ppermute | solution.py:150
  57.8 0.1 add_convert_fusion.2
  57.9 0.0 all-to-all-done
  57.9 8.8 %collective-permute-done.4 = f16[2,2,64,512]{3,2,1,0:T(8,128)(2,1)S(1)} collective-permute-done((f16[2,2,64,512]{3,2,1,0:T(8,128)(2,1)S(1)}, f16[2,2,64,512]{3,2,1,0:T(8,128)(2,1)S(1)}, u32[]{:S(2)}, u32[]{:S(2)}) %collective-permute-start.4) | collective-permute-done | bytes 262176 | tf_op jit(solution)/shard_map/ppermute | solution.py:150
  66.7 1.2 %convert_element_type.94 = f32[8,64,512]{2,1,0:T(8,128)S(1)} convert(f16[8,64,512]{2,1,0:T(8,128)(2,1)} %all-to-all-done) | non-fusion elementwise | flops 262144 | bytes 1572864 | tf_op jit(solution)/shard_map/convert_element_type | solution.py:185
  67.9 0.4 multiply_reduce_fusion
  68.2 1.9 %collective-permute-start.7 = (f32[2,64,512]{2,1,0:T(8,128)S(1)}, f32[2,64,512]{2,1,0:T(8,128)S(1)}, u32[]{:S(2)}, u32[]{:S(2)}) collective-permute-start(f32[2,64,512]{2,1,0:T(8,128)S(1)} %get-tuple-element.31), channel_id=1, source_target_pairs={{0,32},{32,0},{64,96},{96,64},{128,160},{160,128},{192,224},{224,1... | collective-permute-start | bytes 786440 | tf_op jit(solution)/shard_map/ppermute | solution.py:192
  70.2 0.0 collective-permute-done.6
  70.2 1.2 %convert_add_fusion.sum_ref = f32[2,2,64,512]{3,2,1,0:T(8,128)S(1)} fusion(f16[2,2,64,512]{3,2,1,0:T(8,128)(2,1)} %collective-permute-done.6, f16[2,2,64,512]{3,2,1,0:T(8,128)(2,1)S(1)} %collective-permute-done.4, f32[2,2,64,512]{3,2,1,0:T(8,128)S(1)} %copy-done.6, f16[4,2,64,512]{3,2,1,0:T(8,128)(2,1)S(1)} %collective-permute-done.2, ...), kind=kLoop, calls=%fused_computation.4 | loop fusion | flops 1048576 | bytes 2097152 | tf_op jit(solution)/shard_map/add | solution.py:165
  71.4 0.3 collective-permute-done.7
  71.7 0.1 add_divide_fusion.inverse_ref
  71.7 1.4 %pack.1 = bf16[32,32,128]{2,1,0:T(8,128)(2,1)} custom-call(f32[2,2,64,512]{3,2,1,0:T(8,128)S(1)} %convert_add_fusion.sum_ref, f32[2,64,512]{2,1,0:T(8,128)S(1)} %add_divide_fusion.inverse_ref), custom_call_target="tpu_custom_call" | custom-call | tf_op jit(solution)/shard_map/pack/pallas_call | solution.py:242
  73.1 9.1 %all-to-all-start.1 = ((bf16[32,32,128]{2,1,0:T(8,128)(2,1)}), bf16[32,32,128]{2,1,0:T(8,128)(2,1)S(1)}, u32[]{:S(2)}, u32[]{:S(2)}) async-start(bf16[32,32,128]{2,1,0:T(8,128)(2,1)} %pack.1), calls=%async_computation.1 | async-start | bytes 524288 | tf_op jit(solution)/shard_map/all_to_all | solution.py:353
  82.3 0.0 copy-done.15
  82.3 0.1 broadcast_multiply_fusion
  82.4 2.3 %multiply_sine_fusion = (f32[16,40,256]{2,1,0:T(8,128)S(1)}, f32[16,40,256]{2,1,0:T(8,128)S(1)}) fusion(f32[256]{0:T(256)S(1)} %copy-done.13, f32[16,40]{1,0:T(8,128)S(1)} %broadcast_multiply_fusion), kind=kLoop, calls=%fused_computation.2 | loop fusion | flops 163840 | bytes 1314304 | tf_op jit(solution)/shard_map/sin | solution.py:201
  84.7 11.0 %all-to-all-done.1.block_ref = bf16[32,32,128]{2,1,0:T(8,128)(2,1)S(1)} async-done(((bf16[32,32,128]{2,1,0:T(8,128)(2,1)}), bf16[32,32,128]{2,1,0:T(8,128)(2,1)S(1)}, u32[]{:S(2)}, u32[]{:S(2)}) %all-to-all-start.1) | async-done | bytes 262176 | tf_op jit(solution)/shard_map/all_to_all | solution.py:353
  95.7 3.2 %beam.1 = f32[16,2,4,512]{3,2,1,0:T(4,128)} custom-call(bf16[32,32,128]{2,1,0:T(8,128)(2,1)S(1)} %all-to-all-done.1.block_ref, s32[2,1024]{1,0:T(2,128)S(1)} %reshape.131.pair_ref, s32[1024,2]{1,0:T(8,128)S(1)} %bitcast.9, f32[16,40,256]{2,1,0:T(8,128)S(1)} %get-tuple-element.34.cos_ref, f32[16,40,256]{2,1,0:T(8,128)S(1)} %get-tuple-element.33.sin_ref), custom_call_target="tpu_custom_call" | custom-call | tf_op jit(solution)/shard_map/beam/pallas_call | solution.py:327
  (22 shorter events, 0.1 us)
Async XLA Ops:
  0.0 4.9 %copy-start.1 = (f32[1,64,512]{2,1,0:T(8,128)S(1)}, f32[1,64,512]{2,1,0:T(8,128)}, u32[]{:S(2)}) copy-start(f32[1,64,512]{2,1,0:T(8,128)} %param.6) | copy-start | bytes 393220
  0.0 15.6 %copy-start.7 = (s32[16]{0:T(128)S(1)}, s32[16]{0:T(128)}, u32[]{:S(2)}) copy-start(s32[16]{0:T(128)} %offset_ref.3) | copy-start | bytes 196
  0.0 15.8 %copy-start = (bf16[1,16,2,64,512]{4,3,2,1,0:T(8,128)(2,1)S(1)}, bf16[1,16,2,64,512]{4,3,2,1,0:T(8,128)(2,1)}, u32[]{:S(2)}) copy-start(bf16[1,16,2,64,512]{4,3,2,1,0:T(8,128)(2,1)} %param.5) | copy-start | bytes 6291460
  3.0 12.9 %collective-permute-start = (bf16[9,2,64,512]{3,2,1,0:T(8,128)(2,1)}, bf16[9,2,64,512]{3,2,1,0:T(8,128)(2,1)S(1)}, u32[]{:S(2)}, u32[]{:S(2)}) collective-permute-start(bf16[9,2,64,512]{3,2,1,0:T(8,128)(2,1)} %select.3), channel_id=1, source_target_pairs={{0,32},{32,0},{64,96},{96,64},{128,160},{160,128},{192,224},{224,1... | collective-permute-start | bytes 3538952 | tf_op jit(solution)/shard_map/ppermute | solution.py:343
  5.8 52.1 %all-to-all-start = ((f16[8,64,512]{2,1,0:T(8,128)(2,1)}), f16[8,64,512]{2,1,0:T(8,128)(2,1)}, u32[]{:S(2)}, u32[]{:S(2)}) async-start(f16[8,64,512]{2,1,0:T(8,128)(2,1)} %broadcast_in_dim.5), calls=%async_computation | async-start | bytes 1048576 | tf_op jit(solution)/shard_map/all_to_all | solution.py:177
  18.1 0.8 copy-start.2
  18.1 1.0 copy-start.4
  18.1 1.2 %copy-start.5 = (f32[2,2,64,512]{3,2,1,0:T(8,128)}, f32[2,2,64,512]{3,2,1,0:T(8,128)S(1)}, u32[]{:S(2)}) copy-start(f32[2,2,64,512]{3,2,1,0:T(8,128)S(1)} %get-tuple-element.18) | copy-start | bytes 1572868
  18.1 13.7 %copy-start.9 = (s32[2048]{0:T(1024)S(1)}, s32[2048]{0:T(1024)}, u32[]{:S(2)}) copy-start(s32[2048]{0:T(1024)} %param.9) | copy-start | bytes 24580
  18.1 15.4 %copy-start.10 = (s32[2048]{0:T(1024)S(1)}, s32[2048]{0:T(1024)}, u32[]{:S(2)}) copy-start(s32[2048]{0:T(1024)} %param.8) | copy-start | bytes 24580
  19.0 32.4 %copy-start.3 = (f32[2,2,64,512]{3,2,1,0:T(8,128)S(1)}, f32[2,2,64,512]{3,2,1,0:T(8,128)}, u32[]{:S(2)}) copy-start(f32[2,2,64,512]{3,2,1,0:T(8,128)} %copy-done.2) | copy-start | bytes 1572868
  19.3 28.4 %collective-permute-start.1 = (f16[4,2,64,512]{3,2,1,0:T(8,128)(2,1)S(1)}, f16[4,2,64,512]{3,2,1,0:T(8,128)(2,1)S(1)}, u32[]{:S(2)}, u32[]{:S(2)}) collective-permute-start(f16[4,2,64,512]{3,2,1,0:T(8,128)(2,1)S(1)} %convert_element_type.80), channel_id=1, source_target_pairs={{0,64},{32,96},{64,128},{96,160},{128,192},{160,224},{192,256},{22... | collective-permute-start | bytes 1572872 | tf_op jit(solution)/shard_map/ppermute | solution.py:150
  23.3 28.2 %collective-permute-start.2 = (f16[4,2,64,512]{3,2,1,0:T(8,128)(2,1)S(1)}, f16[4,2,64,512]{3,2,1,0:T(8,128)(2,1)S(1)}, u32[]{:S(2)}, u32[]{:S(2)}) collective-permute-start(f16[4,2,64,512]{3,2,1,0:T(8,128)(2,1)S(1)} %convert_element_type.81), channel_id=1, source_target_pairs={{0,448},{32,480},{64,0},{96,32},{128,64},{160,96},{192,128},{224,1... | collective-permute-start | bytes 1572872 | tf_op jit(solution)/shard_map/ppermute | solution.py:150
  26.3 21.4 %collective-permute-start.3 = (f16[1,2,64,512]{3,2,1,0:T(8,128)(2,1)S(1)}, f16[1,2,64,512]{3,2,1,0:T(8,128)(2,1)S(1)}, u32[]{:S(2)}, u32[]{:S(2)}) collective-permute-start(f16[1,2,64,512]{3,2,1,0:T(8,128)(2,1)S(1)} %convert_element_type.82), channel_id=1, source_target_pairs={{0,128},{32,160},{64,192},{96,224},{128,256},{160,288},{192,320},{... | collective-permute-start | bytes 393224 | tf_op jit(solution)/shard_map/ppermute | solution.py:150
  34.2 33.6 %copy-start.11 = (f32[2,8]{1,0:T(2,128)S(1)}, f32[2,8]{1,0:T(2,128)}, u32[]{:S(2)}) copy-start(f32[2,8]{1,0:T(2,128)} %get-tuple-element.35) | copy-start | bytes 196
  34.2 33.6 %copy-start.12 = (f32[2,8]{1,0:T(2,128)S(1)}, f32[2,8]{1,0:T(2,128)}, u32[]{:S(2)}) copy-start(f32[2,8]{1,0:T(2,128)} %get-tuple-element.36) | copy-start | bytes 196
  36.4 21.4 %copy-start.14 = (s32[24]{0:T(128)S(1)}, s32[24]{0:T(128)}, u32[]{:S(2)}) copy-start(s32[24]{0:T(128)} %iota_multiply_fusion) | copy-start | bytes 292
  37.0 14.4 %collective-permute-start.5 = (f16[1,2,64,512]{3,2,1,0:T(8,128)(2,1)S(1)}, f16[1,2,64,512]{3,2,1,0:T(8,128)(2,1)S(1)}, u32[]{:S(2)}, u32[]{:S(2)}) collective-permute-start(f16[1,2,64,512]{3,2,1,0:T(8,128)(2,1)S(1)} %convert_element_type.83), channel_id=1, source_target_pairs={{0,384},{32,416},{64,448},{96,480},{128,0},{160,32},{192,64},{224,... | collective-permute-start | bytes 393224 | tf_op jit(solution)/shard_map/ppermute | solution.py:150
  47.7 0.7 copy-start.8
  49.5 17.2 %collective-permute-start.4 = (f16[2,2,64,512]{3,2,1,0:T(8,128)(2,1)S(1)}, f16[2,2,64,512]{3,2,1,0:T(8,128)(2,1)S(1)}, u32[]{:S(2)}, u32[]{:S(2)}) collective-permute-start(f16[2,2,64,512]{3,2,1,0:T(8,128)(2,1)S(1)} %add_convert_fusion.1), channel_id=1, source_target_pairs={{0,128},{32,160},{64,192},{96,224},{128,256},{160,288},{192,320},{... | collective-permute-start | bytes 786440 | tf_op jit(solution)/shard_map/ppermute | solution.py:150
  51.5 18.7 %copy-start.6 = (f32[2,2,64,512]{3,2,1,0:T(8,128)S(1)}, f32[2,2,64,512]{3,2,1,0:T(8,128)}, u32[]{:S(2)}) copy-start(f32[2,2,64,512]{3,2,1,0:T(8,128)} %copy-done.5) | copy-start | bytes 1572868
  51.6 18.6 %collective-permute-start.6 = (f16[2,2,64,512]{3,2,1,0:T(8,128)(2,1)S(1)}, f16[2,2,64,512]{3,2,1,0:T(8,128)(2,1)}, u32[]{:S(2)}, u32[]{:S(2)}) collective-permute-start(f16[2,2,64,512]{3,2,1,0:T(8,128)(2,1)S(1)} %add_convert_fusion), channel_id=1, source_target_pairs={{0,384},{32,416},{64,448},{96,480},{128,0},{160,32},{192,64},{224,... | collective-permute-start | bytes 786440 | tf_op jit(solution)/shard_map/ppermute | solution.py:150
  68.2 3.4 %collective-permute-start.7 = (f32[2,64,512]{2,1,0:T(8,128)S(1)}, f32[2,64,512]{2,1,0:T(8,128)S(1)}, u32[]{:S(2)}, u32[]{:S(2)}) collective-permute-start(f32[2,64,512]{2,1,0:T(8,128)S(1)} %get-tuple-element.31), channel_id=1, source_target_pairs={{0,32},{32,0},{64,96},{96,64},{128,160},{160,128},{192,224},{224,1... | collective-permute-start | bytes 786440 | tf_op jit(solution)/shard_map/ppermute | solution.py:192
  70.2 12.1 %copy-start.15 = (f32[16]{0:T(128)S(1)}, f32[16]{0:T(128)}, u32[]{:S(2)}) copy-start(f32[16]{0:T(128)} %add_convert_fusion.3) | copy-start | bytes 196
  70.2 12.2 %copy-start.13 = (f32[256]{0:T(256)S(1)}, f32[256]{0:T(256)}, u32[]{:S(2)}) copy-start(f32[256]{0:T(256)} %multiply_add_fusion) | copy-start | bytes 3076
  73.1 22.6 %all-to-all-start.1 = ((bf16[32,32,128]{2,1,0:T(8,128)(2,1)}), bf16[32,32,128]{2,1,0:T(8,128)(2,1)S(1)}, u32[]{:S(2)}, u32[]{:S(2)}) async-start(bf16[32,32,128]{2,1,0:T(8,128)(2,1)} %pack.1), calls=%async_computation.1 | async-start | bytes 524288 | tf_op jit(solution)/shard_map/all_to_all | solution.py:353

commit v3 on v2

--- a/solution.py
+++ b/solution.py
@@ -182,15 +182,13 @@
 def inverse_total(day_offset, weights):
     day = lax.axis_index("day")
     offsets = jnp.where((day & 1) == 0, day_offset[0::2], day_offset[1::2])
-    weights = weights.astype(F32)
-
-    def partial_total(owner):
-        sample = (owner * RA_DEV + jnp.arange(RA_DEV))[:, None] - offsets[None, :]
-        valid = jnp.logical_and(sample >= 0, sample < SAMPLES).astype(F32)
-        return jnp.sum(valid[:, :, None, None] * weights[None], axis=1)
-
-    other = lax.ppermute(partial_total(day ^ 1), "day", SWAP)
-    return (1.0 / SCALE) / (partial_total(day) + other)
+    at = jnp.arange(2 * RA_DEV)
+    bins = (day ^ (at // RA_DEV)) * RA_DEV + at % RA_DEV
+    sample = bins[:, None] - offsets[None, :]
+    valid = jnp.logical_and(sample >= 0, sample < SAMPLES).astype(F32)
+    totals = jnp.sum(valid[:, :, None, None] * weights[None].astype(F32), axis=1)
+    other = lax.ppermute(totals[RA_DEV:], "day", SWAP)
+    return (1.0 / SCALE) / (totals[:RA_DEV] + other)
 
 
 def base_angles(freq_at):
@@ -347,17 +345,20 @@
     return summed, inverse_total(day_offset, weights)
 
 
-def beam_stage(summed, inverse, pair_index, sep_index, freq_at):
+def beam_stage(summed, inverse, pair_index, sep_index):
+    freq_at = (lax.axis_index("bl") * BAND + jnp.arange(BAND)).astype(F32)
     packed = pack(summed, inverse)
-    angles = base_angles(lax.optimization_barrier((freq_at, packed))[0])
+    pair_index, sep_index, freq_at, _ = lax.optimization_barrier(
+        (pair_index, sep_index, freq_at, packed)
+    )
+    angles = base_angles(freq_at)
     block = lax.all_to_all(packed, "bl", split_axis=0, concat_axis=0, tiled=True)
     return beam(block, pair_index, sep_index, angles)
 
 
 def local(visibility, day_weight, day_offset, pair_index, sep_index):
-    freq_at = (lax.axis_index("bl") * BAND + jnp.arange(BAND)).astype(F32)
     summed, inverse = day_stage(visibility, day_weight, day_offset)
-    return beam_stage(summed, inverse, pair_index, sep_index, freq_at)
+    return beam_stage(summed, inverse, pair_index, sep_index)
 
 
 def solution(mesh):

time: 99.7 us -> 98.7 us (0.990)
  waiting for transfers between devices: 27.7 us -> 34.9 us
  local copies, waits for them, and re-layouts: 7.28 us -> 2.5 us
  other arithmetic: 9.11 us -> 5.86 us
    ppermute x6, waiting for transfers between devices: 16.5 us -> 23.4 us  [send(): return lax.ppermute(values, 'day', pairs)]
    reshape x2, local copies, waits for them, and re-layouts: 1.54 us -> 0.17 us  [beam(): pair_index.reshape(N_BL, 2, BASE_LOC // 2).transpose(1, 0, 2)]
    transpose x1, local copies, waits for them, and re-layouts: 1.37 us -> 0.01 us  [beam(): pair_index.reshape(N_BL, 2, BASE_LOC // 2).transpose(1, 0, 2)]
    convert_element_type x3, other arithmetic: 2.4 us -> 1.24 us  [the longest x1 1.16 us: inverse_total(): weights[None].astype(F32)]
    add x1, other arithmetic: 1.2 us -> 0.17 us  [reduce_ring(): sums[6] + near_up[2:].astype(F32) + near_down[2:].astype(F32)]
    ppermute x1, waiting for transfers between devices: 0.26 us -> 1.28 us  [inverse_total(): other = lax.ppermute(totals[RA_DEV:], 'day', SWAP)]
  transfers between devices with their start and end apart: 10 -> 10, of which waited for: 4 -> 4; matrix products, arithmetic and copies ran while one was open for 15% -> 8% of each run, Pallas kernels for 2% -> 2%
where the time goes in v3:
time: 98.7 us; the launch traced here: 98.1 us
  starting transfers between devices  44.7 us (45%)
  waiting for transfers between devices  34.9 us (35%)
  Pallas kernels  9.81 us (10%)
  other arithmetic  5.86 us (6%)
  local copies, waits for them, and re-layouts  2.5 us (3%)
    ppermute x6, waiting for transfers between devices, send(): return lax.ppermute(values, 'day', pairs)  23.4 us
    ppermute x6, starting transfers between devices, send(): return lax.ppermute(values, 'day', pairs)  21.9 us
    all_to_all x1, waiting for transfers between devices, beam_stage(): lax.all_to_all(packed, 'bl', split_axis=0, concat_axis=0, tiled=True)  10.2 us
    all_to_all x1, starting transfers between devices, gather_weights(): lax.all_to_all(copies, 'day', split_axis=0, concat_axis=0, axis_index_gro...  9.84 us
    all_to_all x1, starting transfers between devices, beam_stage(): lax.all_to_all(packed, 'bl', split_axis=0, concat_axis=0, tiled=True)  9.15 us
    pallas_call x1, Pallas kernels, beam(): pl.pallas_call(beam_kernel, in_specs=[vmem] * 5, out_specs=vmem, out_shap...  3.22 us
    pallas_call x1, Pallas kernels, select(): pl.pallas_call(select_kernel, in_specs=[pl.BlockSpec(memory_space=pltpu.S...  2.98 us
    sin x1, other arithmetic, base_angles(): return (jnp.cos(phase), jnp.sin(phase))  2.35 us
  transfers between devices with their start and end apart: 10, of which 4 were waited for; matrix products, arithmetic and copies ran while one was open for 8% of the time, Pallas kernels for 2%

profile of v3, /device:TPU:8, one launch (start us, length us, event | category | flops | bytes accessed | tf_op | source)
XLA Modules:
  0.0 98.1 jit_solution(9775417937226392601)
XLA Ops:
  0.0 0.0 copy-start.1
  0.0 0.0 copy-start.7
  0.0 0.0 copy-start
  0.0 3.0 %select.13 = bf16[9,2,64,512]{3,2,1,0:T(8,128)(2,1)} custom-call(s32[16]{0:T(128)} %offset_ref.3, f32[64,512]{1,0:T(8,128)} %bitcast.10, bf16[16,2,64,512]{3,2,1,0:T(8,128)(2,1)} %bitcast.7), custom_call_target="tpu_custom_call" | custom-call | tf_op jit(solution)/shard_map/select/pallas_call | solution.py:75
  3.0 1.9 %collective-permute-start = (bf16[9,2,64,512]{3,2,1,0:T(8,128)(2,1)}, bf16[9,2,64,512]{3,2,1,0:T(8,128)(2,1)S(1)}, u32[]{:S(2)}, u32[]{:S(2)}) collective-permute-start(bf16[9,2,64,512]{3,2,1,0:T(8,128)(2,1)} %select.13), channel_id=1, source_target_pairs={{0,32},{32,0},{64,96},{96,64},{128,160},{160,128},{192,224},{224,1... | collective-permute-start | bytes 3538952 | tf_op jit(solution)/shard_map/ppermute | solution.py:341
  4.9 0.0 copy-done.1
  5.0 0.8 broadcast_in_dim.5
  5.8 9.8 %all-to-all-start = ((f16[8,64,512]{2,1,0:T(8,128)(2,1)}), f16[8,64,512]{2,1,0:T(8,128)(2,1)}, u32[]{:S(2)}, u32[]{:S(2)}) async-start(f16[8,64,512]{2,1,0:T(8,128)(2,1)} %broadcast_in_dim.5), calls=%async_computation | async-start | bytes 1048576 | tf_op jit(solution)/shard_map/all_to_all | solution.py:177
  15.6 0.0 copy-done.7
  15.6 0.1 slice.28
  15.7 0.1 slice.29
  15.8 0.0 collective-permute-done.other_ref
  15.9 0.0 copy-done
  15.9 2.2 %chip_sums.1 = (f32[4,2,64,512]{3,2,1,0:T(8,128)S(1)}, f32[4,2,64,512]{3,2,1,0:T(8,128)S(1)}, f32[1,2,64,512]{3,2,1,0:T(8,128)S(1)}, f32[1,2,64,512]{3,2,1,0:T(8...) custom-call(s32[16]{0:T(128)S(1)} %copy-done.7, ...), custom_call_target="tpu_custom_call" | custom-call | tf_op jit(solution)/shard_map/chip_sums/pallas_call | solution.py:128
  18.1 0.0 copy-start.2
  18.1 0.0 copy-start.4
  18.1 0.0 copy-start.5
  18.1 0.1 convert_element_type.74
  18.2 0.1 convert_element_type.75
  18.3 0.6 copy-done.2
  18.9 0.2 copy-done.4
  19.0 0.0 copy-start.3
  19.1 0.1 copy-done.5
  19.2 3.4 %collective-permute-start.1 = (f16[4,2,64,512]{3,2,1,0:T(8,128)(2,1)S(1)}, f16[4,2,64,512]{3,2,1,0:T(8,128)(2,1)S(1)}, u32[]{:S(2)}, u32[]{:S(2)}) collective-permute-start(f16[4,2,64,512]{3,2,1,0:T(8,128)(2,1)S(1)} %convert_element_type.74), channel_id=1, source_target_pairs={{0,64},{32,96},{64,128},{96,160},{128,192},{160,224},{192,256},{22... | collective-permute-start | bytes 1572872 | tf_op jit(solution)/shard_map/ppermute | solution.py:150
  22.6 0.1 fusion.2
  22.7 2.5 %collective-permute-start.2 = (f16[4,2,64,512]{3,2,1,0:T(8,128)(2,1)S(1)}, f16[4,2,64,512]{3,2,1,0:T(8,128)(2,1)S(1)}, u32[]{:S(2)}, u32[]{:S(2)}) collective-permute-start(f16[4,2,64,512]{3,2,1,0:T(8,128)(2,1)S(1)} %convert_element_type.75), channel_id=1, source_target_pairs={{0,448},{32,480},{64,0},{96,32},{128,64},{160,96},{192,128},{224,1... | collective-permute-start | bytes 1572872 | tf_op jit(solution)/shard_map/ppermute | solution.py:150
  25.2 5.0 %collective-permute-start.3 = (f16[1,2,64,512]{3,2,1,0:T(8,128)(2,1)S(1)}, f16[1,2,64,512]{3,2,1,0:T(8,128)(2,1)S(1)}, u32[]{:S(2)}, u32[]{:S(2)}) collective-permute-start(f16[1,2,64,512]{3,2,1,0:T(8,128)(2,1)S(1)} %convert_element_type.76), channel_id=1, source_target_pairs={{0,128},{32,160},{64,192},{96,224},{128,256},{160,288},{192,320},{... | collective-permute-start | bytes 393224 | tf_op jit(solution)/shard_map/ppermute | solution.py:150
  30.2 3.0 %collective-permute-start.5 = (f16[1,2,64,512]{3,2,1,0:T(8,128)(2,1)S(1)}, f16[1,2,64,512]{3,2,1,0:T(8,128)(2,1)S(1)}, u32[]{:S(2)}, u32[]{:S(2)}) collective-permute-start(f16[1,2,64,512]{3,2,1,0:T(8,128)(2,1)S(1)} %convert_element_type.77), channel_id=1, source_target_pairs={{0,384},{32,416},{64,448},{96,480},{128,0},{160,32},{192,64},{224,... | collective-permute-start | bytes 393224 | tf_op jit(solution)/shard_map/ppermute | solution.py:150
  33.2 14.5 %collective-permute-done.3 = f16[1,2,64,512]{3,2,1,0:T(8,128)(2,1)S(1)} collective-permute-done((f16[1,2,64,512]{3,2,1,0:T(8,128)(2,1)S(1)}, f16[1,2,64,512]{3,2,1,0:T(8,128)(2,1)S(1)}, u32[]{:S(2)}, u32[]{:S(2)}) %collective-permute-start.3) | collective-permute-done | bytes 131104 | tf_op jit(solution)/shard_map/ppermute | solution.py:150
  47.7 0.0 collective-permute-done.1
  47.7 1.1 %add_convert_fusion.1 = f16[2,2,64,512]{3,2,1,0:T(8,128)(2,1)S(1)} fusion(f32[2,2,64,512]{3,2,1,0:T(8,128)} %copy-done.4, f16[4,2,64,512]{3,2,1,0:T(8,128)(2,1)S(1)} %collective-permute-done.1, f16[1,2,64,512]{3,2,1,0:T(8,128)(2,1)S(1)} %collective-permute-done.3), kind=kLoop, calls=%fused_computation.5 | loop fusion | flops 655360 | bytes 1179648 | tf_op jit(solution)/shard_map/convert_element_type | solution.py:161
  48.9 1.9 %collective-permute-start.4 = (f16[2,2,64,512]{3,2,1,0:T(8,128)(2,1)S(1)}, f16[2,2,64,512]{3,2,1,0:T(8,128)(2,1)S(1)}, u32[]{:S(2)}, u32[]{:S(2)}) collective-permute-start(f16[2,2,64,512]{3,2,1,0:T(8,128)(2,1)S(1)} %add_convert_fusion.1), channel_id=1, source_target_pairs={{0,128},{32,160},{64,192},{96,224},{128,256},{160,288},{192,320},{... | collective-permute-start | bytes 786440 | tf_op jit(solution)/shard_map/ppermute | solution.py:150
  50.8 0.0 collective-permute-done.5
  50.8 0.0 collective-permute-done.2
  50.8 0.0 copy-done.3
  50.8 0.1 add_convert_fusion
  50.9 0.0 copy-start.6
  50.9 6.2 %collective-permute-start.6 = (f16[2,2,64,512]{3,2,1,0:T(8,128)(2,1)S(1)}, f16[2,2,64,512]{3,2,1,0:T(8,128)(2,1)S(1)}, u32[]{:S(2)}, u32[]{:S(2)}) collective-permute-start(f16[2,2,64,512]{3,2,1,0:T(8,128)(2,1)S(1)} %add_convert_fusion), channel_id=1, source_target_pairs={{0,384},{32,416},{64,448},{96,480},{128,0},{160,32},{192,64},{224,... | collective-permute-start | bytes 786440 | tf_op jit(solution)/shard_map/ppermute | solution.py:150
  57.1 0.1 add_convert_fusion.2
  57.2 0.0 all-to-all-done
  57.2 8.8 %collective-permute-done.4 = f16[2,2,64,512]{3,2,1,0:T(8,128)(2,1)S(1)} collective-permute-done((f16[2,2,64,512]{3,2,1,0:T(8,128)(2,1)S(1)}, f16[2,2,64,512]{3,2,1,0:T(8,128)(2,1)S(1)}, u32[]{:S(2)}, u32[]{:S(2)}) %collective-permute-start.4) | collective-permute-done | bytes 262176 | tf_op jit(solution)/shard_map/ppermute | solution.py:150
  66.0 1.2 %convert_element_type.88 = f32[8,64,512]{2,1,0:T(8,128)S(1)} convert(f16[8,64,512]{2,1,0:T(8,128)(2,1)} %all-to-all-done) | non-fusion elementwise | flops 262144 | bytes 1572864 | tf_op jit(solution)/shard_map/convert_element_type | solution.py:189
  67.2 0.4 multiply_reduce_fusion
  67.6 1.9 %collective-permute-start.7 = (f32[2,64,512]{2,1,0:T(8,128)S(1)}, f32[2,64,512]{2,1,0:T(8,128)S(1)}, u32[]{:S(2)}, u32[]{:S(2)}) collective-permute-start(f32[2,64,512]{2,1,0:T(8,128)S(1)} %slice.37), channel_id=1, source_target_pairs={{0,32},{32,0},{64,96},{96,64},{128,160},{160,128},{192,224},{224,1... | collective-permute-start | bytes 786440 | tf_op jit(solution)/shard_map/ppermute | solution.py:190
  69.5 0.0 collective-permute-done.6
  69.5 0.0 copy-done.6
  69.5 0.0 copy-start.8
  69.5 0.0 copy-start.9
  69.6 0.2 convert_add_fusion.sum_ref
  69.7 1.3 %collective-permute-done.7 = f32[2,64,512]{2,1,0:T(8,128)S(1)} collective-permute-done((f32[2,64,512]{2,1,0:T(8,128)S(1)}, f32[2,64,512]{2,1,0:T(8,128)S(1)}, u32[]{:S(2)}, u32[]{:S(2)}) %collective-permute-start.7) | collective-permute-done | bytes 262176 | tf_op jit(solution)/shard_map/ppermute | solution.py:190
  71.0 0.1 fusion.inverse_ref
  71.1 1.4 %pack.1 = bf16[32,32,128]{2,1,0:T(8,128)(2,1)} custom-call(f32[2,2,64,512]{3,2,1,0:T(8,128)S(1)} %convert_add_fusion.sum_ref, f32[2,64,512]{2,1,0:T(8,128)S(1)} %fusion.inverse_ref), custom_call_target="tpu_custom_call" | custom-call | tf_op jit(solution)/shard_map/pack/pallas_call | solution.py:240
  72.5 9.1 %all-to-all-start.1 = ((bf16[32,32,128]{2,1,0:T(8,128)(2,1)}), bf16[32,32,128]{2,1,0:T(8,128)(2,1)S(1)}, u32[]{:S(2)}, u32[]{:S(2)}) async-start(bf16[32,32,128]{2,1,0:T(8,128)(2,1)} %pack.1), calls=%async_computation.1 | async-start | bytes 524288 | tf_op jit(solution)/shard_map/all_to_all | solution.py:355
  81.7 0.0 copy-done.8
  81.7 0.1 reshape.120
  81.8 0.3 copy.9
  82.0 0.0 copy-done.9
  82.0 0.1 reshape.118
  82.1 0.1 reshape.119.pair_ref
  82.2 0.1 broadcast_multiply_fusion
  82.3 2.3 %multiply_sine_fusion = (f32[16,40,256]{2,1,0:T(8,128)S(1)}, f32[16,40,256]{2,1,0:T(8,128)S(1)}) fusion(f32[256]{0:T(256)S(1)} %multiply_add_fusion, f32[16,40]{1,0:T(8,128)S(1)} %broadcast_multiply_fusion), kind=kLoop, calls=%fused_computation.1 | loop fusion | flops 163840 | bytes 1314304 | tf_op jit(solution)/shard_map/sin | solution.py:199
  84.7 10.2 %all-to-all-done.1.block_ref = bf16[32,32,128]{2,1,0:T(8,128)(2,1)S(1)} async-done(((bf16[32,32,128]{2,1,0:T(8,128)(2,1)}), bf16[32,32,128]{2,1,0:T(8,128)(2,1)S(1)}, u32[]{:S(2)}, u32[]{:S(2)}) %all-to-all-start.1) | async-done | bytes 262176 | tf_op jit(solution)/shard_map/all_to_all | solution.py:355
  94.9 3.2 %beam.1 = f32[16,2,4,512]{3,2,1,0:T(4,128)} custom-call(bf16[32,32,128]{2,1,0:T(8,128)(2,1)S(1)} %all-to-all-done.1.block_ref, s32[2,1024]{1,0:T(2,128)S(1)} %reshape.119.pair_ref, s32[1024,2]{1,0:T(8,128)S(1)} %bitcast.9, f32[16,40,256]{2,1,0:T(8,128)S(1)} %get-tuple-element.36.cos_ref, f32[16,40,256]{2,1,0:T(8,128)S(1)} %get-tuple-element.35.sin_ref), custom_call_target="tpu_custom_call" | custom-call | tf_op jit(solution)/shard_map/beam/pallas_call | solution.py:325
  (12 shorter events, 0.1 us)
Async XLA Ops:
  0.0 4.9 %copy-start.1 = (f32[1,64,512]{2,1,0:T(8,128)S(1)}, f32[1,64,512]{2,1,0:T(8,128)}, u32[]{:S(2)}) copy-start(f32[1,64,512]{2,1,0:T(8,128)} %param.6) | copy-start | bytes 393220
  0.0 15.6 %copy-start.7 = (s32[16]{0:T(128)S(1)}, s32[16]{0:T(128)}, u32[]{:S(2)}) copy-start(s32[16]{0:T(128)} %offset_ref.3) | copy-start | bytes 196
  0.0 15.9 %copy-start = (bf16[1,16,2,64,512]{4,3,2,1,0:T(8,128)(2,1)S(1)}, bf16[1,16,2,64,512]{4,3,2,1,0:T(8,128)(2,1)}, u32[]{:S(2)}) copy-start(bf16[1,16,2,64,512]{4,3,2,1,0:T(8,128)(2,1)} %param.5) | copy-start | bytes 6291460
  3.0 12.9 %collective-permute-start = (bf16[9,2,64,512]{3,2,1,0:T(8,128)(2,1)}, bf16[9,2,64,512]{3,2,1,0:T(8,128)(2,1)S(1)}, u32[]{:S(2)}, u32[]{:S(2)}) collective-permute-start(bf16[9,2,64,512]{3,2,1,0:T(8,128)(2,1)} %select.13), channel_id=1, source_target_pairs={{0,32},{32,0},{64,96},{96,64},{128,160},{160,128},{192,224},{224,1... | collective-permute-start | bytes 3538952 | tf_op jit(solution)/shard_map/ppermute | solution.py:341
  5.8 51.4 %all-to-all-start = ((f16[8,64,512]{2,1,0:T(8,128)(2,1)}), f16[8,64,512]{2,1,0:T(8,128)(2,1)}, u32[]{:S(2)}, u32[]{:S(2)}) async-start(f16[8,64,512]{2,1,0:T(8,128)(2,1)} %broadcast_in_dim.5), calls=%async_computation | async-start | bytes 1048576 | tf_op jit(solution)/shard_map/all_to_all | solution.py:177
  18.1 0.8 copy-start.2
  18.1 1.0 copy-start.4
  18.1 1.1 %copy-start.5 = (f32[2,2,64,512]{3,2,1,0:T(8,128)}, f32[2,2,64,512]{3,2,1,0:T(8,128)S(1)}, u32[]{:S(2)}) copy-start(f32[2,2,64,512]{3,2,1,0:T(8,128)S(1)} %get-tuple-element.20) | copy-start | bytes 1572868
  19.0 31.8 %copy-start.3 = (f32[2,2,64,512]{3,2,1,0:T(8,128)S(1)}, f32[2,2,64,512]{3,2,1,0:T(8,128)}, u32[]{:S(2)}) copy-start(f32[2,2,64,512]{3,2,1,0:T(8,128)} %copy-done.2) | copy-start | bytes 1572868
  19.2 28.5 %collective-permute-start.1 = (f16[4,2,64,512]{3,2,1,0:T(8,128)(2,1)S(1)}, f16[4,2,64,512]{3,2,1,0:T(8,128)(2,1)S(1)}, u32[]{:S(2)}, u32[]{:S(2)}) collective-permute-start(f16[4,2,64,512]{3,2,1,0:T(8,128)(2,1)S(1)} %convert_element_type.74), channel_id=1, source_target_pairs={{0,64},{32,96},{64,128},{96,160},{128,192},{160,224},{192,256},{22... | collective-permute-start | bytes 1572872 | tf_op jit(solution)/shard_map/ppermute | solution.py:150
  22.7 28.1 %collective-permute-start.2 = (f16[4,2,64,512]{3,2,1,0:T(8,128)(2,1)S(1)}, f16[4,2,64,512]{3,2,1,0:T(8,128)(2,1)S(1)}, u32[]{:S(2)}, u32[]{:S(2)}) collective-permute-start(f16[4,2,64,512]{3,2,1,0:T(8,128)(2,1)S(1)} %convert_element_type.75), channel_id=1, source_target_pairs={{0,448},{32,480},{64,0},{96,32},{128,64},{160,96},{192,128},{224,1... | collective-permute-start | bytes 1572872 | tf_op jit(solution)/shard_map/ppermute | solution.py:150
  25.2 22.5 %collective-permute-start.3 = (f16[1,2,64,512]{3,2,1,0:T(8,128)(2,1)S(1)}, f16[1,2,64,512]{3,2,1,0:T(8,128)(2,1)S(1)}, u32[]{:S(2)}, u32[]{:S(2)}) collective-permute-start(f16[1,2,64,512]{3,2,1,0:T(8,128)(2,1)S(1)} %convert_element_type.76), channel_id=1, source_target_pairs={{0,128},{32,160},{64,192},{96,224},{128,256},{160,288},{192,320},{... | collective-permute-start | bytes 393224 | tf_op jit(solution)/shard_map/ppermute | solution.py:150
  30.2 20.6 %collective-permute-start.5 = (f16[1,2,64,512]{3,2,1,0:T(8,128)(2,1)S(1)}, f16[1,2,64,512]{3,2,1,0:T(8,128)(2,1)S(1)}, u32[]{:S(2)}, u32[]{:S(2)}) collective-permute-start(f16[1,2,64,512]{3,2,1,0:T(8,128)(2,1)S(1)} %convert_element_type.77), channel_id=1, source_target_pairs={{0,384},{32,416},{64,448},{96,480},{128,0},{160,32},{192,64},{224,... | collective-permute-start | bytes 393224 | tf_op jit(solution)/shard_map/ppermute | solution.py:150
  48.9 17.2 %collective-permute-start.4 = (f16[2,2,64,512]{3,2,1,0:T(8,128)(2,1)S(1)}, f16[2,2,64,512]{3,2,1,0:T(8,128)(2,1)S(1)}, u32[]{:S(2)}, u32[]{:S(2)}) collective-permute-start(f16[2,2,64,512]{3,2,1,0:T(8,128)(2,1)S(1)} %add_convert_fusion.1), channel_id=1, source_target_pairs={{0,128},{32,160},{64,192},{96,224},{128,256},{160,288},{192,320},{... | collective-permute-start | bytes 786440 | tf_op jit(solution)/shard_map/ppermute | solution.py:150
  50.9 18.6 %copy-start.6 = (f32[2,2,64,512]{3,2,1,0:T(8,128)S(1)}, f32[2,2,64,512]{3,2,1,0:T(8,128)}, u32[]{:S(2)}) copy-start(f32[2,2,64,512]{3,2,1,0:T(8,128)} %copy-done.5) | copy-start | bytes 1572868
  50.9 18.6 %collective-permute-start.6 = (f16[2,2,64,512]{3,2,1,0:T(8,128)(2,1)S(1)}, f16[2,2,64,512]{3,2,1,0:T(8,128)(2,1)S(1)}, u32[]{:S(2)}, u32[]{:S(2)}) collective-permute-start(f16[2,2,64,512]{3,2,1,0:T(8,128)(2,1)S(1)} %add_convert_fusion), channel_id=1, source_target_pairs={{0,384},{32,416},{64,448},{96,480},{128,0},{160,32},{192,64},{224,... | collective-permute-start | bytes 786440 | tf_op jit(solution)/shard_map/ppermute | solution.py:150
  67.6 3.4 %collective-permute-start.7 = (f32[2,64,512]{2,1,0:T(8,128)S(1)}, f32[2,64,512]{2,1,0:T(8,128)S(1)}, u32[]{:S(2)}, u32[]{:S(2)}) collective-permute-start(f32[2,64,512]{2,1,0:T(8,128)S(1)} %slice.37), channel_id=1, source_target_pairs={{0,32},{32,0},{64,96},{96,64},{128,160},{160,128},{192,224},{224,1... | collective-permute-start | bytes 786440 | tf_op jit(solution)/shard_map/ppermute | solution.py:190
  69.5 12.1 %copy-start.8 = (s32[2048]{0:T(1024)S(1)}, s32[2048]{0:T(1024)}, u32[]{:S(2)}) copy-start(s32[2048]{0:T(1024)} %param.9) | copy-start | bytes 24580
  69.5 12.5 %copy-start.9 = (s32[2048]{0:T(1024)S(1)}, s32[2048]{0:T(1024)}, u32[]{:S(2)}) copy-start(s32[2048]{0:T(1024)} %param.8) | copy-start | bytes 24580
  72.5 22.4 %all-to-all-start.1 = ((bf16[32,32,128]{2,1,0:T(8,128)(2,1)}), bf16[32,32,128]{2,1,0:T(8,128)(2,1)S(1)}, u32[]{:S(2)}, u32[]{:S(2)}) async-start(bf16[32,32,128]{2,1,0:T(8,128)(2,1)} %pack.1), calls=%async_computation.1 | async-start | bytes 524288 | tf_op jit(solution)/shard_map/all_to_all | solution.py:355

commit v4 on v3

--- a/solution.py
+++ b/solution.py
@@ -173,10 +173,7 @@
 
 def gather_weights(day_weight):
     same = [[2 * y + c for y in range(CHIPS)] for c in range(2)]
-    copies = jnp.broadcast_to(day_weight.astype(F16)[None], (CHIPS, BASE_LOC, FREQ))
-    return lax.all_to_all(
-        copies, "day", split_axis=0, concat_axis=0, axis_index_groups=same, tiled=True
-    )
+    return lax.all_gather(day_weight.astype(F16), "day", axis=0, axis_index_groups=same)
 
 
 def inverse_total(day_offset, weights):
@@ -339,7 +336,7 @@
 def day_stage(visibility, day_weight, day_offset):
     visibility, day_weight = visibility[0], day_weight[0]
     other = lax.ppermute(select(day_offset, day_weight, visibility), "day", SWAP)
-    weights = gather_weights(day_weight)
+    other, weights = lax.optimization_barrier((other, gather_weights(day_weight)))
     sums = chip_sums(day_offset, visibility, day_weight, other)
     summed, weights = reduce_ring(sums, weights)
     return summed, inverse_total(day_offset, weights)

time: 98.7 us -> 105 us (1.064)
  blocking collectives: 0 us -> 30.2 us
  waiting for transfers between devices: 34.9 us -> 20.1 us
  starting transfers between devices: 44.7 us -> 37.6 us
    all_gather x0 -> x1, blocking collectives: none -> 30.2 us  [gather_weights(): lax.all_gather(day_weight.astype(F16), 'day', axis=0, axis_index_groups=s...]
    ppermute x6, waiting for transfers between devices: 23.4 us -> 9.61 us  [send(): return lax.ppermute(values, 'day', pairs)]
    all_to_all x1 -> x0, starting transfers between devices: 9.84 us -> none  [gather_weights(): lax.all_to_all(copies, 'day', split_axis=0, concat_axis=0, axis_index_gro...]
    all_to_all x1, starting transfers between devices: 9.15 us -> 10.9 us  [beam_stage(): lax.all_to_all(packed, 'bl', split_axis=0, concat_axis=0, tiled=True)]
    ppermute x6, starting transfers between devices: 21.9 us -> 22.9 us  [send(): return lax.ppermute(values, 'day', pairs)]
  transfers between devices with their start and end apart: 10 -> 9, of which waited for: 4 -> 5; matrix products, arithmetic and copies ran while one was open for 8% -> 5% of each run, Pallas kernels for 2% -> 0%
where the time goes in v4:
time: 105 us
  starting transfers between devices  37.6 us (36%)
  blocking collectives  30.2 us (29%)
  waiting for transfers between devices  20.1 us (19%)
  Pallas kernels  9.82 us (9%)
  other arithmetic  4.85 us (5%)
  local copies, waits for them, and re-layouts  1.69 us (2%)
    all_gather x1, blocking collectives, gather_weights(): lax.all_gather(day_weight.astype(F16), 'day', axis=0, axis_index_groups=s...  30.2 us
    ppermute x6, starting transfers between devices, send(): return lax.ppermute(values, 'day', pairs)  22.9 us
    all_to_all x1, starting transfers between devices, beam_stage(): lax.all_to_all(packed, 'bl', split_axis=0, concat_axis=0, tiled=True)  10.9 us
    ppermute x6, waiting for transfers between devices, send(): return lax.ppermute(values, 'day', pairs)  9.61 us
    all_to_all x1, waiting for transfers between devices, beam_stage(): lax.all_to_all(packed, 'bl', split_axis=0, concat_axis=0, tiled=True)  9.4 us
    pallas_call x1, Pallas kernels, beam(): pl.pallas_call(beam_kernel, in_specs=[vmem] * 5, out_specs=vmem, out_shap...  3.22 us
    pallas_call x1, Pallas kernels, select(): pl.pallas_call(select_kernel, in_specs=[pl.BlockSpec(memory_space=pltpu.S...  2.99 us
    sin x1, other arithmetic, base_angles(): return (jnp.cos(phase), jnp.sin(phase))  2.35 us
  transfers between devices with their start and end apart: 9, of which 5 were waited for; matrix products, arithmetic and copies ran while one was open for 5% of the time, Pallas kernels for 0%

profile of v4, /device:TPU:8, one launch (start us, length us, event | category | flops | bytes accessed | tf_op | source)
XLA Modules:
  0.0 104.6 jit_solution(242604082386634566)
XLA Ops:
  0.0 0.0 copy-start.1
  0.0 0.0 copy-start.7
  0.0 0.0 copy-start
  0.0 3.0 %select.13 = bf16[9,2,64,512]{3,2,1,0:T(8,128)(2,1)} custom-call(s32[16]{0:T(128)} %offset_ref.3, f32[64,512]{1,0:T(8,128)} %bitcast.8, bf16[16,2,64,512]{3,2,1,0:T(8,128)(2,1)} %bitcast.5), custom_call_target="tpu_custom_call" | custom-call | tf_op jit(solution)/shard_map/select/pallas_call | solution.py:75
  3.0 1.9 %collective-permute-start = (bf16[9,2,64,512]{3,2,1,0:T(8,128)(2,1)}, bf16[9,2,64,512]{3,2,1,0:T(8,128)(2,1)S(1)}, u32[]{:S(2)}, u32[]{:S(2)}) collective-permute-start(bf16[9,2,64,512]{3,2,1,0:T(8,128)(2,1)} %select.13), channel_id=1, source_target_pairs={{0,32},{32,0},{64,96},{96,64},{128,160},{160,128},{192,224},{224,1... | collective-permute-start | bytes 3538952 | tf_op jit(solution)/shard_map/ppermute | solution.py:338
  4.9 0.0 copy-done.1
  5.0 0.0 copy-done.7
  5.0 0.1 slice.28
  5.1 0.1 slice.29
  5.2 30.2 %all_gather.4 = f16[8,64,512]{2,1,0:T(8,128)(2,1)} all-gather(f16[1,64,512]{2,1,0:T(8,128)(2,1)S(1)} %convert_element_type.74), channel_id=1, replica_groups={{0,64,128,192,256,320,384,448},{32,96,160,224,288,352,416,480},{1,65,12..., dimensions={0}, use_global_device_ids=true | all-gather | bytes 589824 | tf_op jit(solution)/shard_map/all_gather | solution.py:176
  35.4 0.0 collective-permute-done.other_ref
  35.4 0.0 copy-done
  35.4 2.2 %chip_sums.1 = (f32[4,2,64,512]{3,2,1,0:T(8,128)S(1)}, f32[4,2,64,512]{3,2,1,0:T(8,128)S(1)}, f32[1,2,64,512]{3,2,1,0:T(8,128)S(1)}, f32[1,2,64,512]{3,2,1,0:T(8...) custom-call(s32[16]{0:T(128)S(1)} %copy-done.7, ...), custom_call_target="tpu_custom_call" | custom-call | tf_op jit(solution)/shard_map/chip_sums/pallas_call | solution.py:128
  37.6 0.0 copy-start.2
  37.6 0.0 copy-start.4
  37.6 0.0 copy-start.5
  37.6 0.1 convert_element_type.75
  37.7 0.0 copy-start.8
  37.7 0.1 convert_element_type.76
  37.8 0.5 copy-done.2
  38.4 0.2 copy-done.4
  38.5 0.0 copy-start.3
  38.6 0.2 copy-done.5
  38.8 3.8 %collective-permute-start.1 = (f16[4,2,64,512]{3,2,1,0:T(8,128)(2,1)S(1)}, f16[4,2,64,512]{3,2,1,0:T(8,128)(2,1)S(1)}, u32[]{:S(2)}, u32[]{:S(2)}) collective-permute-start(f16[4,2,64,512]{3,2,1,0:T(8,128)(2,1)S(1)} %convert_element_type.75), channel_id=1, source_target_pairs={{0,64},{32,96},{64,128},{96,160},{128,192},{160,224},{192,256},{22... | collective-permute-start | bytes 1572872 | tf_op jit(solution)/shard_map/ppermute | solution.py:150
  42.5 0.1 fusion.2
  42.6 3.1 %collective-permute-start.2 = (f16[4,2,64,512]{3,2,1,0:T(8,128)(2,1)S(1)}, f16[4,2,64,512]{3,2,1,0:T(8,128)(2,1)S(1)}, u32[]{:S(2)}, u32[]{:S(2)}) collective-permute-start(f16[4,2,64,512]{3,2,1,0:T(8,128)(2,1)S(1)} %convert_element_type.76), channel_id=1, source_target_pairs={{0,448},{32,480},{64,0},{96,32},{128,64},{160,96},{192,128},{224,1... | collective-permute-start | bytes 1572872 | tf_op jit(solution)/shard_map/ppermute | solution.py:150
  45.8 2.2 %collective-permute-start.3 = (f16[1,2,64,512]{3,2,1,0:T(8,128)(2,1)S(1)}, f16[1,2,64,512]{3,2,1,0:T(8,128)(2,1)S(1)}, u32[]{:S(2)}, u32[]{:S(2)}) collective-permute-start(f16[1,2,64,512]{3,2,1,0:T(8,128)(2,1)S(1)} %convert_element_type.77), channel_id=1, source_target_pairs={{0,128},{32,160},{64,192},{96,224},{128,256},{160,288},{192,320},{... | collective-permute-start | bytes 393224 | tf_op jit(solution)/shard_map/ppermute | solution.py:150
  48.0 5.8 %collective-permute-start.5 = (f16[1,2,64,512]{3,2,1,0:T(8,128)(2,1)S(1)}, f16[1,2,64,512]{3,2,1,0:T(8,128)(2,1)S(1)}, u32[]{:S(2)}, u32[]{:S(2)}) collective-permute-start(f16[1,2,64,512]{3,2,1,0:T(8,128)(2,1)S(1)} %convert_element_type.78), channel_id=1, source_target_pairs={{0,384},{32,416},{64,448},{96,480},{128,0},{160,32},{192,64},{224,... | collective-permute-start | bytes 393224 | tf_op jit(solution)/shard_map/ppermute | solution.py:150
  53.7 6.2 %collective-permute-done.3 = f16[1,2,64,512]{3,2,1,0:T(8,128)(2,1)S(1)} collective-permute-done((f16[1,2,64,512]{3,2,1,0:T(8,128)(2,1)S(1)}, f16[1,2,64,512]{3,2,1,0:T(8,128)(2,1)S(1)}, u32[]{:S(2)}, u32[]{:S(2)}) %collective-permute-start.3) | collective-permute-done | bytes 131104 | tf_op jit(solution)/shard_map/ppermute | solution.py:150
  60.0 0.0 collective-permute-done.1
  60.0 1.1 %add_convert_fusion.1 = f16[2,2,64,512]{3,2,1,0:T(8,128)(2,1)S(1)} fusion(f32[2,2,64,512]{3,2,1,0:T(8,128)} %copy-done.4, f16[4,2,64,512]{3,2,1,0:T(8,128)(2,1)S(1)} %collective-permute-done.1, f16[1,2,64,512]{3,2,1,0:T(8,128)(2,1)S(1)} %collective-permute-done.3), kind=kLoop, calls=%fused_computation.5 | loop fusion | flops 655360 | bytes 1179648 | tf_op jit(solution)/shard_map/convert_element_type | solution.py:161
  61.1 1.9 %collective-permute-start.4 = (f16[2,2,64,512]{3,2,1,0:T(8,128)(2,1)S(1)}, f16[2,2,64,512]{3,2,1,0:T(8,128)(2,1)S(1)}, u32[]{:S(2)}, u32[]{:S(2)}) collective-permute-start(f16[2,2,64,512]{3,2,1,0:T(8,128)(2,1)S(1)} %add_convert_fusion.1), channel_id=1, source_target_pairs={{0,128},{32,160},{64,192},{96,224},{128,256},{160,288},{192,320},{... | collective-permute-start | bytes 786440 | tf_op jit(solution)/shard_map/ppermute | solution.py:150
  63.0 0.0 collective-permute-done.5
  63.1 0.0 collective-permute-done.2
  63.1 0.0 copy-done.3
  63.1 0.1 add_convert_fusion
  63.2 0.0 copy-start.6
  63.2 6.2 %collective-permute-start.6 = (f16[2,2,64,512]{3,2,1,0:T(8,128)(2,1)S(1)}, f16[2,2,64,512]{3,2,1,0:T(8,128)(2,1)S(1)}, u32[]{:S(2)}, u32[]{:S(2)}) collective-permute-start(f16[2,2,64,512]{3,2,1,0:T(8,128)(2,1)S(1)} %add_convert_fusion), channel_id=1, source_target_pairs={{0,384},{32,416},{64,448},{96,480},{128,0},{160,32},{192,64},{224,... | collective-permute-start | bytes 786440 | tf_op jit(solution)/shard_map/ppermute | solution.py:150
  69.4 0.1 add_convert_fusion.2
  69.5 3.2 %collective-permute-done.4 = f16[2,2,64,512]{3,2,1,0:T(8,128)(2,1)S(1)} collective-permute-done((f16[2,2,64,512]{3,2,1,0:T(8,128)(2,1)S(1)}, f16[2,2,64,512]{3,2,1,0:T(8,128)(2,1)S(1)}, u32[]{:S(2)}, u32[]{:S(2)}) %collective-permute-start.4) | collective-permute-done | bytes 262176 | tf_op jit(solution)/shard_map/ppermute | solution.py:150
  72.7 0.0 copy-done.8
  72.7 0.1 convert_element_type.88
  72.8 0.4 multiply_reduce_fusion
  73.2 1.9 %collective-permute-start.7 = (f32[2,64,512]{2,1,0:T(8,128)S(1)}, f32[2,64,512]{2,1,0:T(8,128)S(1)}, u32[]{:S(2)}, u32[]{:S(2)}) collective-permute-start(f32[2,64,512]{2,1,0:T(8,128)S(1)} %slice.37), channel_id=1, source_target_pairs={{0,32},{32,0},{64,96},{96,64},{128,160},{160,128},{192,224},{224,1... | collective-permute-start | bytes 786440 | tf_op jit(solution)/shard_map/ppermute | solution.py:187
  75.1 0.2 collective-permute-done.6
  75.3 0.0 copy-done.6
  75.3 0.0 copy-start.9
  75.3 0.0 copy-start.10
  75.3 0.2 convert_add_fusion.sum_ref
  75.5 1.1 %collective-permute-done.7 = f32[2,64,512]{2,1,0:T(8,128)S(1)} collective-permute-done((f32[2,64,512]{2,1,0:T(8,128)S(1)}, f32[2,64,512]{2,1,0:T(8,128)S(1)}, u32[]{:S(2)}, u32[]{:S(2)}) %collective-permute-start.7) | collective-permute-done | bytes 262176 | tf_op jit(solution)/shard_map/ppermute | solution.py:187
  76.6 0.1 fusion.inverse_ref
  76.7 1.4 %pack.1 = bf16[32,32,128]{2,1,0:T(8,128)(2,1)} custom-call(f32[2,2,64,512]{3,2,1,0:T(8,128)S(1)} %convert_add_fusion.sum_ref, f32[2,64,512]{2,1,0:T(8,128)S(1)} %fusion.inverse_ref), custom_call_target="tpu_custom_call" | custom-call | tf_op jit(solution)/shard_map/pack/pallas_call | solution.py:237
  78.1 10.9 %all-to-all-start = ((bf16[32,32,128]{2,1,0:T(8,128)(2,1)}), bf16[32,32,128]{2,1,0:T(8,128)(2,1)S(1)}, u32[]{:S(2)}, u32[]{:S(2)}) async-start(bf16[32,32,128]{2,1,0:T(8,128)(2,1)} %pack.1), calls=%async_computation | async-start | bytes 524288 | tf_op jit(solution)/shard_map/all_to_all | solution.py:352
  89.0 0.0 copy-done.9
  89.0 0.1 reshape.120
  89.1 0.3 copy.11
  89.4 0.0 copy-done.10
  89.4 0.1 reshape.118
  89.5 0.1 reshape.119.pair_ref
  89.6 0.1 broadcast_multiply_fusion
  89.6 2.3 %multiply_sine_fusion = (f32[16,40,256]{2,1,0:T(8,128)S(1)}, f32[16,40,256]{2,1,0:T(8,128)S(1)}) fusion(f32[256]{0:T(256)S(1)} %multiply_add_fusion, f32[16,40]{1,0:T(8,128)S(1)} %broadcast_multiply_fusion), kind=kLoop, calls=%fused_computation.1 | loop fusion | flops 163840 | bytes 1314304 | tf_op jit(solution)/shard_map/sin | solution.py:196
  92.0 9.4 %all-to-all-done.block_ref = bf16[32,32,128]{2,1,0:T(8,128)(2,1)S(1)} async-done(((bf16[32,32,128]{2,1,0:T(8,128)(2,1)}), bf16[32,32,128]{2,1,0:T(8,128)(2,1)S(1)}, u32[]{:S(2)}, u32[]{:S(2)}) %all-to-all-start) | async-done | bytes 262176 | tf_op jit(solution)/shard_map/all_to_all | solution.py:352
  101.4 3.2 %beam.1 = f32[16,2,4,512]{3,2,1,0:T(4,128)} custom-call(bf16[32,32,128]{2,1,0:T(8,128)(2,1)S(1)} %all-to-all-done.block_ref, s32[2,1024]{1,0:T(2,128)S(1)} %reshape.119.pair_ref, s32[1024,2]{1,0:T(8,128)S(1)} %bitcast.7, f32[16,40,256]{2,1,0:T(8,128)S(1)} %get-tuple-element.40.cos_ref, f32[16,40,256]{2,1,0:T(8,128)S(1)} %get-tuple-element.39.sin_ref), custom_call_target="tpu_custom_call" | custom-call | tf_op jit(solution)/shard_map/beam/pallas_call | solution.py:322
  (12 shorter events, 0.1 us)
Async XLA Ops:
  0.0 4.9 %copy-start.1 = (f32[1,64,512]{2,1,0:T(8,128)S(1)}, f32[1,64,512]{2,1,0:T(8,128)}, u32[]{:S(2)}) copy-start(f32[1,64,512]{2,1,0:T(8,128)} %param.6) | copy-start | bytes 393220
  0.0 5.0 %copy-start.7 = (s32[16]{0:T(128)S(1)}, s32[16]{0:T(128)}, u32[]{:S(2)}) copy-start(s32[16]{0:T(128)} %offset_ref.3) | copy-start | bytes 196
  0.0 35.4 %copy-start = (bf16[1,16,2,64,512]{4,3,2,1,0:T(8,128)(2,1)S(1)}, bf16[1,16,2,64,512]{4,3,2,1,0:T(8,128)(2,1)}, u32[]{:S(2)}) copy-start(bf16[1,16,2,64,512]{4,3,2,1,0:T(8,128)(2,1)} %param.5) | copy-start | bytes 6291460
  3.0 32.3 %collective-permute-start = (bf16[9,2,64,512]{3,2,1,0:T(8,128)(2,1)}, bf16[9,2,64,512]{3,2,1,0:T(8,128)(2,1)S(1)}, u32[]{:S(2)}, u32[]{:S(2)}) collective-permute-start(bf16[9,2,64,512]{3,2,1,0:T(8,128)(2,1)} %select.13), channel_id=1, source_target_pairs={{0,32},{32,0},{64,96},{96,64},{128,160},{160,128},{192,224},{224,1... | collective-permute-start | bytes 3538952 | tf_op jit(solution)/shard_map/ppermute | solution.py:338
  37.6 0.8 copy-start.2
  37.6 1.0 copy-start.4
  37.6 1.2 %copy-start.5 = (f32[2,2,64,512]{3,2,1,0:T(8,128)}, f32[2,2,64,512]{3,2,1,0:T(8,128)S(1)}, u32[]{:S(2)}) copy-start(f32[2,2,64,512]{3,2,1,0:T(8,128)S(1)} %get-tuple-element.23) | copy-start | bytes 1572868
  37.7 35.0 %copy-start.8 = (f16[8,64,512]{2,1,0:T(8,128)(2,1)S(1)}, f16[8,64,512]{2,1,0:T(8,128)(2,1)}, u32[]{:S(2)}) copy-start(f16[8,64,512]{2,1,0:T(8,128)(2,1)} %all_gather.4) | copy-start | bytes 1572868
  38.5 24.5 %copy-start.3 = (f32[2,2,64,512]{3,2,1,0:T(8,128)S(1)}, f32[2,2,64,512]{3,2,1,0:T(8,128)}, u32[]{:S(2)}) copy-start(f32[2,2,64,512]{3,2,1,0:T(8,128)} %copy-done.2) | copy-start | bytes 1572868
  38.8 21.2 %collective-permute-start.1 = (f16[4,2,64,512]{3,2,1,0:T(8,128)(2,1)S(1)}, f16[4,2,64,512]{3,2,1,0:T(8,128)(2,1)S(1)}, u32[]{:S(2)}, u32[]{:S(2)}) collective-permute-start(f16[4,2,64,512]{3,2,1,0:T(8,128)(2,1)S(1)} %convert_element_type.75), channel_id=1, source_target_pairs={{0,64},{32,96},{64,128},{96,160},{128,192},{160,224},{192,256},{22... | collective-permute-start | bytes 1572872 | tf_op jit(solution)/shard_map/ppermute | solution.py:150
  42.6 20.4 %collective-permute-start.2 = (f16[4,2,64,512]{3,2,1,0:T(8,128)(2,1)S(1)}, f16[4,2,64,512]{3,2,1,0:T(8,128)(2,1)S(1)}, u32[]{:S(2)}, u32[]{:S(2)}) collective-permute-start(f16[4,2,64,512]{3,2,1,0:T(8,128)(2,1)S(1)} %convert_element_type.76), channel_id=1, source_target_pairs={{0,448},{32,480},{64,0},{96,32},{128,64},{160,96},{192,128},{224,1... | collective-permute-start | bytes 1572872 | tf_op jit(solution)/shard_map/ppermute | solution.py:150
  45.8 14.2 %collective-permute-start.3 = (f16[1,2,64,512]{3,2,1,0:T(8,128)(2,1)S(1)}, f16[1,2,64,512]{3,2,1,0:T(8,128)(2,1)S(1)}, u32[]{:S(2)}, u32[]{:S(2)}) collective-permute-start(f16[1,2,64,512]{3,2,1,0:T(8,128)(2,1)S(1)} %convert_element_type.77), channel_id=1, source_target_pairs={{0,128},{32,160},{64,192},{96,224},{128,256},{160,288},{192,320},{... | collective-permute-start | bytes 393224 | tf_op jit(solution)/shard_map/ppermute | solution.py:150
  48.0 15.1 %collective-permute-start.5 = (f16[1,2,64,512]{3,2,1,0:T(8,128)(2,1)S(1)}, f16[1,2,64,512]{3,2,1,0:T(8,128)(2,1)S(1)}, u32[]{:S(2)}, u32[]{:S(2)}) collective-permute-start(f16[1,2,64,512]{3,2,1,0:T(8,128)(2,1)S(1)} %convert_element_type.78), channel_id=1, source_target_pairs={{0,384},{32,416},{64,448},{96,480},{128,0},{160,32},{192,64},{224,... | collective-permute-start | bytes 393224 | tf_op jit(solution)/shard_map/ppermute | solution.py:150
  61.1 11.5 %collective-permute-start.4 = (f16[2,2,64,512]{3,2,1,0:T(8,128)(2,1)S(1)}, f16[2,2,64,512]{3,2,1,0:T(8,128)(2,1)S(1)}, u32[]{:S(2)}, u32[]{:S(2)}) collective-permute-start(f16[2,2,64,512]{3,2,1,0:T(8,128)(2,1)S(1)} %add_convert_fusion.1), channel_id=1, source_target_pairs={{0,128},{32,160},{64,192},{96,224},{128,256},{160,288},{192,320},{... | collective-permute-start | bytes 786440 | tf_op jit(solution)/shard_map/ppermute | solution.py:150
  63.2 12.1 %copy-start.6 = (f32[2,2,64,512]{3,2,1,0:T(8,128)S(1)}, f32[2,2,64,512]{3,2,1,0:T(8,128)}, u32[]{:S(2)}) copy-start(f32[2,2,64,512]{3,2,1,0:T(8,128)} %copy-done.5) | copy-start | bytes 1572868
  63.2 12.1 %collective-permute-start.6 = (f16[2,2,64,512]{3,2,1,0:T(8,128)(2,1)S(1)}, f16[2,2,64,512]{3,2,1,0:T(8,128)(2,1)S(1)}, u32[]{:S(2)}, u32[]{:S(2)}) collective-permute-start(f16[2,2,64,512]{3,2,1,0:T(8,128)(2,1)S(1)} %add_convert_fusion), channel_id=1, source_target_pairs={{0,384},{32,416},{64,448},{96,480},{128,0},{160,32},{192,64},{224,... | collective-permute-start | bytes 786440 | tf_op jit(solution)/shard_map/ppermute | solution.py:150
  73.2 3.4 %collective-permute-start.7 = (f32[2,64,512]{2,1,0:T(8,128)S(1)}, f32[2,64,512]{2,1,0:T(8,128)S(1)}, u32[]{:S(2)}, u32[]{:S(2)}) collective-permute-start(f32[2,64,512]{2,1,0:T(8,128)S(1)} %slice.37), channel_id=1, source_target_pairs={{0,32},{32,0},{64,96},{96,64},{128,160},{160,128},{192,224},{224,1... | collective-permute-start | bytes 786440 | tf_op jit(solution)/shard_map/ppermute | solution.py:187
  75.3 13.7 %copy-start.9 = (s32[2048]{0:T(1024)S(1)}, s32[2048]{0:T(1024)}, u32[]{:S(2)}) copy-start(s32[2048]{0:T(1024)} %param.9) | copy-start | bytes 24580
  75.3 14.1 %copy-start.10 = (s32[2048]{0:T(1024)S(1)}, s32[2048]{0:T(1024)}, u32[]{:S(2)}) copy-start(s32[2048]{0:T(1024)} %param.8) | copy-start | bytes 24580
  78.1 23.3 %all-to-all-start = ((bf16[32,32,128]{2,1,0:T(8,128)(2,1)}), bf16[32,32,128]{2,1,0:T(8,128)(2,1)S(1)}, u32[]{:S(2)}, u32[]{:S(2)}) async-start(bf16[32,32,128]{2,1,0:T(8,128)(2,1)} %pack.1), calls=%async_computation | async-start | bytes 524288 | tf_op jit(solution)/shard_map/all_to_all | solution.py:352

commit v5 on v4

--- a/solution.py
+++ b/solution.py
@@ -120,23 +120,24 @@
                     vis_ref[sample, x].astype(F32) * own
                     + other_ref[owned & (HELD - 1), x].astype(F32) * other
                 )
+            out_ref[at, 2] = own + other
 
 
 def chip_sums(day_offset, visibility, day_weight, other):
     rows = 16
-    block = lambda count: pl.BlockSpec((count, 2, rows, FREQ), lambda i: (0, 0, i, 0))
+    block = lambda count, parts: pl.BlockSpec((count, parts, rows, FREQ), lambda i: (0, 0, i, 0))
     return pl.pallas_call(
         chip_kernel,
         grid=(BASE_LOC // rows,),
         in_specs=[
             pl.BlockSpec(memory_space=pltpu.SMEM),
-            block(SAMPLES),
+            block(SAMPLES, 2),
             pl.BlockSpec((rows, FREQ), lambda i: (i, 0)),
-            block(HELD + 1),
+            block(HELD + 1, 2),
         ],
-        out_specs=[block(len(bins)) for bins in SENDS],
+        out_specs=[block(len(bins), 3) for bins in SENDS],
         out_shape=[
-            jax.ShapeDtypeStruct((len(bins), 2, BASE_LOC, FREQ), F32) for bins in SENDS
+            jax.ShapeDtypeStruct((len(bins), 3, BASE_LOC, FREQ), F32) for bins in SENDS
         ],
         compiler_params=pltpu.CompilerParams(vmem_limit_bytes=16 * MIB),
         name="chip_sums",
@@ -150,7 +151,7 @@
     return lax.ppermute(values, "day", pairs)
 
 
-def reduce_ring(sums, late):
+def reduce_ring(sums):
     first = lax.optimization_barrier([part.astype(F16) for part in sums[:4]])
     near_up, near_down = send(first[0], 1), send(first[1], -1)
     far_up, far_down = send(first[2], 2), send(first[3], -2)
@@ -160,32 +161,13 @@
     middle_down = middle_down + jnp.pad(far_down.astype(F32), ((1, 0), (0, 0), (0, 0), (0, 0)))
     middle_up, middle_down = middle_up.astype(F16), middle_down.astype(F16)
     last_up, last_down = send(middle_up, 2), send(middle_down, -2)
-    late = lax.optimization_barrier((late, last_up))[0]
-    summed = (
+    return (
         sums[6]
         + near_up[2:].astype(F32)
         + near_down[2:].astype(F32)
         + last_up.astype(F32)
         + last_down.astype(F32)
     )
-    return summed, late
-
-
-def gather_weights(day_weight):
-    same = [[2 * y + c for y in range(CHIPS)] for c in range(2)]
-    return lax.all_gather(day_weight.astype(F16), "day", axis=0, axis_index_groups=same)
-
-
-def inverse_total(day_offset, weights):
-    day = lax.axis_index("day")
-    offsets = jnp.where((day & 1) == 0, day_offset[0::2], day_offset[1::2])
-    at = jnp.arange(2 * RA_DEV)
-    bins = (day ^ (at // RA_DEV)) * RA_DEV + at % RA_DEV
-    sample = bins[:, None] - offsets[None, :]
-    valid = jnp.logical_and(sample >= 0, sample < SAMPLES).astype(F32)
-    totals = jnp.sum(valid[:, :, None, None] * weights[None].astype(F32), axis=1)
-    other = lax.ppermute(totals[RA_DEV:], "day", SWAP)
-    return (1.0 / SCALE) / (totals[:RA_DEV] + other)
 
 
 def base_angles(freq_at):
@@ -216,32 +198,31 @@
             out_ref[tile * 8 + group, rows, :] = parts[group].astype(BF16)
 
 
-def pack_kernel(sum_ref, inverse_ref, out_ref):
+def pack_kernel(sum_ref, out_ref):
     half = BASE_LOC // 2
     for first in range(0, half, 16):
         for sub in range(0, 16, 8):
             rows = pl.ds(first + sub, 8)
-            pieces = []
-            for x in range(2):
-                for r in range(RA_DEV):
-                    for hi in range(2):
-                        rows_in = pl.ds(hi * half + first + sub, 8)
-                        pieces.append(
-                            sum_ref[r, x, rows_in, :] * inverse_ref[r, rows_in, :]
-                        )
+            pieces = [None] * 8
+            for r in range(RA_DEV):
+                for hi in range(2):
+                    rows_in = pl.ds(hi * half + first + sub, 8)
+                    inverse = 1.0 / sum_ref[r, 2, rows_in, :]
+                    for x in range(2):
+                        pieces[x * 4 + r * 2 + hi] = sum_ref[r, x, rows_in, :] * inverse
             pack_blocks(pieces, out_ref, rows)
 
 
-def pack(summed, inverse):
+def pack(summed):
     vmem = pl.BlockSpec(memory_space=pltpu.VMEM)
     return pl.pallas_call(
         pack_kernel,
-        in_specs=[vmem, vmem],
+        in_specs=[vmem],
         out_specs=vmem,
         out_shape=jax.ShapeDtypeStruct((N_BL, BASE_LOC // 2, 128), BF16),
         compiler_params=pltpu.CompilerParams(vmem_limit_bytes=16 * MIB),
         name="pack",
-    )(summed, inverse)
+    )(summed)
 
 
 def beam_kernel(block_ref, pair_ref, sep_ref, cos_ref, sin_ref, out_ref, grid_ref, table_buf):
@@ -336,15 +317,12 @@
 def day_stage(visibility, day_weight, day_offset):
     visibility, day_weight = visibility[0], day_weight[0]
     other = lax.ppermute(select(day_offset, day_weight, visibility), "day", SWAP)
-    other, weights = lax.optimization_barrier((other, gather_weights(day_weight)))
-    sums = chip_sums(day_offset, visibility, day_weight, other)
-    summed, weights = reduce_ring(sums, weights)
-    return summed, inverse_total(day_offset, weights)
-
-
-def beam_stage(summed, inverse, pair_index, sep_index):
+    return reduce_ring(chip_sums(day_offset, visibility, day_weight, other))
+
+
+def beam_stage(summed, pair_index, sep_index):
     freq_at = (lax.axis_index("bl") * BAND + jnp.arange(BAND)).astype(F32)
-    packed = pack(summed, inverse)
+    packed = pack(summed)
     pair_index, sep_index, freq_at, _ = lax.optimization_barrier(
         (pair_index, sep_index, freq_at, packed)
     )
@@ -354,8 +332,8 @@
 
 
 def local(visibility, day_weight, day_offset, pair_index, sep_index):
-    summed, inverse = day_stage(visibility, day_weight, day_offset)
-    return beam_stage(summed, inverse, pair_index, sep_index)
+    summed = day_stage(visibility, day_weight, day_offset)
+    return beam_stage(summed, pair_index, sep_index)
 
 
 def solution(mesh):

time: 105 us -> 104 us (level)
  the two profiles are of different devices: /device:TPU:8 before, /device:TPU:16 now
where the time goes in v5:
time: 104 us
  waiting for transfers between devices  43.8 us (42%)
  starting transfers between devices  41.8 us (40%)
  Pallas kernels  9.92 us (10%)
  other arithmetic  7.34 us (7%)
    ppermute x6, waiting for transfers between devices, send(): return lax.ppermute(values, 'day', pairs)  32.2 us
    ppermute x6, starting transfers between devices, send(): return lax.ppermute(values, 'day', pairs)  25.9 us
    all_to_all x1, starting transfers between devices, beam_stage(): lax.all_to_all(packed, 'bl', split_axis=0, concat_axis=0, tiled=True)  14 us
    all_to_all x1, waiting for transfers between devices, beam_stage(): lax.all_to_all(packed, 'bl', split_axis=0, concat_axis=0, tiled=True)  8.54 us
    pallas_call x1, Pallas kernels, beam(): pl.pallas_call(beam_kernel, in_specs=[vmem] * 5, out_specs=vmem, out_shap...  3.22 us
    ppermute x1, waiting for transfers between devices, day_stage(): lax.ppermute(select(day_offset, day_weight, visibility), 'day', SWAP)  3.02 us
    pallas_call x1, Pallas kernels, select(): pl.pallas_call(select_kernel, in_specs=[pl.BlockSpec(memory_space=pltpu.S...  2.96 us
    pallas_call x1, Pallas kernels, chip_sums(): pl.pallas_call(chip_kernel, grid=(BASE_LOC // rows,), in_specs=[pl.BlockS...  2.39 us
  transfers between devices with their start and end apart: 8, of which 6 were waited for; matrix products, arithmetic and copies ran while one was open for 4% of the time, Pallas kernels for 0%

profile of v5, /device:TPU:16, one launch (start us, length us, event | category | flops | bytes accessed | tf_op | source)
XLA Modules:
  0.0 103.6 jit_solution(1241890636519897682)
XLA Ops:
  0.0 0.0 copy-start
  0.0 0.0 copy-start.3
  0.0 0.0 copy-start.4
  0.0 3.0 %select.3 = bf16[9,2,64,512]{3,2,1,0:T(8,128)(2,1)} custom-call(s32[16]{0:T(128)} %offset_ref.3, f32[64,512]{1,0:T(8,128)} %bitcast.8, bf16[16,2,64,512]{3,2,1,0:T(8,128)(2,1)} %bitcast.5), custom_call_target="tpu_custom_call" | custom-call | tf_op jit(solution)/shard_map/select/pallas_call | solution.py:75
  3.0 1.9 %collective-permute-start = (bf16[9,2,64,512]{3,2,1,0:T(8,128)(2,1)}, bf16[9,2,64,512]{3,2,1,0:T(8,128)(2,1)S(1)}, u32[]{:S(2)}, u32[]{:S(2)}) collective-permute-start(bf16[9,2,64,512]{3,2,1,0:T(8,128)(2,1)} %select.3), channel_id=1, source_target_pairs={{0,32},{32,0},{64,96},{96,64},{128,160},{160,128},{192,224},{224,1... | collective-permute-start | bytes 3538952 | tf_op jit(solution)/shard_map/ppermute | solution.py:319
  4.9 3.0 %collective-permute-done.other_ref = bf16[9,2,64,512]{3,2,1,0:T(8,128)(2,1)S(1)} collective-permute-done((bf16[9,2,64,512]{3,2,1,0:T(8,128)(2,1)}, bf16[9,2,64,512]{3,2,1,0:T(8,128)(2,1)S(1)}, u32[]{:S(2)}, u32[]{:S(2)}) %collective-permute-start) | collective-permute-done | bytes 1179680 | tf_op jit(solution)/shard_map/ppermute | solution.py:319
  7.9 0.0 copy-done
  7.9 0.0 copy-done.3
  7.9 0.0 copy-done.4
  7.9 2.4 %chip_sums.1 = (f32[4,3,64,512]{3,2,1,0:T(8,128)S(1)}, f32[4,3,64,512]{3,2,1,0:T(8,128)S(1)}, f32[1,3,64,512]{3,2,1,0:T(8,128)S(1)}, f32[1,3,64,512]{3,2,1,0:T(8...) custom-call(s32[16]{0:T(128)S(1)} %copy-done.4, ...), custom_call_target="tpu_custom_call" | custom-call | tf_op jit(solution)/shard_map/chip_sums/pallas_call | solution.py:129
  10.3 0.0 copy-start.1
  10.3 1.1 %convert_element_type.59 = f16[4,3,64,512]{3,2,1,0:T(8,128)(2,1)} convert(f32[4,3,64,512]{3,2,1,0:T(8,128)S(1)} %get-tuple-element.20) | non-fusion elementwise | flops 393216 | bytes 2359296 | tf_op jit(solution)/shard_map/convert_element_type | solution.py:155
  11.5 1.1 %convert_element_type.60 = f16[4,3,64,512]{3,2,1,0:T(8,128)(2,1)} convert(f32[4,3,64,512]{3,2,1,0:T(8,128)S(1)} %get-tuple-element.21) | non-fusion elementwise | flops 393216 | bytes 2359296 | tf_op jit(solution)/shard_map/convert_element_type | solution.py:155
  12.6 0.0 copy-done.1
  12.6 3.5 %collective-permute-start.1 = (f16[4,3,64,512]{3,2,1,0:T(8,128)(2,1)}, f16[4,3,64,512]{3,2,1,0:T(8,128)(2,1)S(1)}, u32[]{:S(2)}, u32[]{:S(2)}) collective-permute-start(f16[4,3,64,512]{3,2,1,0:T(8,128)(2,1)} %convert_element_type.59), channel_id=1, source_target_pairs={{0,64},{32,96},{64,128},{96,160},{128,192},{160,224},{192,256},{22... | collective-permute-start | bytes 2359304 | tf_op jit(solution)/shard_map/ppermute | solution.py:151
  16.1 2.3 %collective-permute-start.2 = (f16[4,3,64,512]{3,2,1,0:T(8,128)(2,1)}, f16[4,3,64,512]{3,2,1,0:T(8,128)(2,1)}, u32[]{:S(2)}, u32[]{:S(2)}) collective-permute-start(f16[4,3,64,512]{3,2,1,0:T(8,128)(2,1)} %convert_element_type.60), channel_id=1, source_target_pairs={{0,448},{32,480},{64,0},{96,32},{128,64},{160,96},{192,128},{224,1... | collective-permute-start | bytes 2359304 | tf_op jit(solution)/shard_map/ppermute | solution.py:151
  18.5 6.9 %collective-permute-start.3 = (f16[1,3,64,512]{3,2,1,0:T(8,128)(2,1)S(1)}, f16[1,3,64,512]{3,2,1,0:T(8,128)(2,1)S(1)}, u32[]{:S(2)}, u32[]{:S(2)}) collective-permute-start(f16[1,3,64,512]{3,2,1,0:T(8,128)(2,1)S(1)} %convert_element_type.61), channel_id=1, source_target_pairs={{0,128},{32,160},{64,192},{96,224},{128,256},{160,288},{192,320},{... | collective-permute-start | bytes 589832 | tf_op jit(solution)/shard_map/ppermute | solution.py:151
  25.4 3.8 %collective-permute-start.5 = (f16[1,3,64,512]{3,2,1,0:T(8,128)(2,1)S(1)}, f16[1,3,64,512]{3,2,1,0:T(8,128)(2,1)S(1)}, u32[]{:S(2)}, u32[]{:S(2)}) collective-permute-start(f16[1,3,64,512]{3,2,1,0:T(8,128)(2,1)S(1)} %convert_element_type.62), channel_id=1, source_target_pairs={{0,384},{32,416},{64,448},{96,480},{128,0},{160,32},{192,64},{224,... | collective-permute-start | bytes 589832 | tf_op jit(solution)/shard_map/ppermute | solution.py:151
  29.3 13.3 %collective-permute-done.3 = f16[1,3,64,512]{3,2,1,0:T(8,128)(2,1)S(1)} collective-permute-done((f16[1,3,64,512]{3,2,1,0:T(8,128)(2,1)S(1)}, f16[1,3,64,512]{3,2,1,0:T(8,128)(2,1)S(1)}, u32[]{:S(2)}, u32[]{:S(2)}) %collective-permute-start.3) | collective-permute-done | bytes 196640 | tf_op jit(solution)/shard_map/ppermute | solution.py:151
  42.6 0.0 collective-permute-done.1
  42.6 0.0 copy-start.2
  42.6 0.2 add_convert_fusion.1
  42.8 5.9 %collective-permute-start.4 = (f16[2,3,64,512]{3,2,1,0:T(8,128)(2,1)S(1)}, f16[2,3,64,512]{3,2,1,0:T(8,128)(2,1)S(1)}, u32[]{:S(2)}, u32[]{:S(2)}) collective-permute-start(f16[2,3,64,512]{3,2,1,0:T(8,128)(2,1)S(1)} %add_convert_fusion.1), channel_id=1, source_target_pairs={{0,128},{32,160},{64,192},{96,224},{128,256},{160,288},{192,320},{... | collective-permute-start | bytes 1179656 | tf_op jit(solution)/shard_map/ppermute | solution.py:151
  48.7 0.7 collective-permute-done.5
  49.4 0.0 collective-permute-done.2
  49.4 1.1 %add_convert_fusion = f16[2,3,64,512]{3,2,1,0:T(8,128)(2,1)S(1)} fusion(f32[2,3,64,512]{3,2,1,0:T(8,128)S(1)} %get-tuple-element.28, f16[4,3,64,512]{3,2,1,0:T(8,128)(2,1)} %collective-permute-done.2, f16[1,3,64,512]{3,2,1,0:T(8,128)(2,1)S(1)} %collective-permute-done.5), kind=kLoop, calls=%fused_computation.3 | loop fusion | flops 983040 | bytes 1769472 | tf_op jit(solution)/shard_map/convert_element_type | solution.py:162
  50.5 3.4 %collective-permute-start.6 = (f16[2,3,64,512]{3,2,1,0:T(8,128)(2,1)S(1)}, f16[2,3,64,512]{3,2,1,0:T(8,128)(2,1)S(1)}, u32[]{:S(2)}, u32[]{:S(2)}) collective-permute-start(f16[2,3,64,512]{3,2,1,0:T(8,128)(2,1)S(1)} %add_convert_fusion), channel_id=1, source_target_pairs={{0,384},{32,416},{64,448},{96,480},{128,0},{160,32},{192,64},{224,... | collective-permute-start | bytes 1179656 | tf_op jit(solution)/shard_map/ppermute | solution.py:151
  53.9 0.1 add_convert_fusion.2
  54.0 3.6 %collective-permute-done.4 = f16[2,3,64,512]{3,2,1,0:T(8,128)(2,1)S(1)} collective-permute-done((f16[2,3,64,512]{3,2,1,0:T(8,128)(2,1)S(1)}, f16[2,3,64,512]{3,2,1,0:T(8,128)(2,1)S(1)}, u32[]{:S(2)}, u32[]{:S(2)}) %collective-permute-start.4) | collective-permute-done | bytes 393248 | tf_op jit(solution)/shard_map/ppermute | solution.py:151
  57.7 14.5 %collective-permute-done.6 = f16[2,3,64,512]{3,2,1,0:T(8,128)(2,1)S(1)} collective-permute-done((f16[2,3,64,512]{3,2,1,0:T(8,128)(2,1)S(1)}, f16[2,3,64,512]{3,2,1,0:T(8,128)(2,1)S(1)}, u32[]{:S(2)}, u32[]{:S(2)}) %collective-permute-start.6) | collective-permute-done | bytes 393248 | tf_op jit(solution)/shard_map/ppermute | solution.py:151
  72.2 0.0 copy-done.2
  72.2 1.3 %convert_add_fusion.sum_ref = f32[2,3,64,512]{3,2,1,0:T(8,128)S(1)} fusion(f16[2,3,64,512]{3,2,1,0:T(8,128)(2,1)S(1)} %collective-permute-done.6, f16[2,3,64,512]{3,2,1,0:T(8,128)(2,1)S(1)} %collective-permute-done.4, f32[2,3,64,512]{3,2,1,0:T(8,128)S(1)} %copy-done.2, f16[4,3,64,512]{3,2,1,0:T(8,128)(2,1)} %collective-permute-done.2, ...), kind=kLoop, calls=%fused_computation.2 | loop fusion | flops 1572864 | bytes 3145728 | tf_op jit(solution)/shard_map/add | solution.py:165
  73.4 0.0 copy-start.5
  73.5 0.0 copy-start.6
  73.5 1.3 %pack.1 = bf16[32,32,128]{2,1,0:T(8,128)(2,1)} custom-call(f32[2,3,64,512]{3,2,1,0:T(8,128)S(1)} %convert_add_fusion.sum_ref), custom_call_target="tpu_custom_call" | custom-call | tf_op jit(solution)/shard_map/pack/pallas_call | solution.py:218
  74.8 14.0 %all-to-all-start = ((bf16[32,32,128]{2,1,0:T(8,128)(2,1)}), bf16[32,32,128]{2,1,0:T(8,128)(2,1)S(1)}, u32[]{:S(2)}, u32[]{:S(2)}) async-start(bf16[32,32,128]{2,1,0:T(8,128)(2,1)} %pack.1), calls=%async_computation | async-start | bytes 524288 | tf_op jit(solution)/shard_map/all_to_all | solution.py:330
  88.8 0.0 copy-done.5
  88.8 0.1 reshape.65
  88.9 0.3 copy.7
  89.2 0.0 copy-done.6
  89.2 0.1 reshape.63
  89.3 0.1 reshape.64.pair_ref
  89.4 0.1 broadcast_multiply_fusion
  89.5 2.3 %multiply_sine_fusion = (f32[16,40,256]{2,1,0:T(8,128)S(1)}, f32[16,40,256]{2,1,0:T(8,128)S(1)}) fusion(f32[256]{0:T(256)S(1)} %multiply_add_fusion, f32[16,40]{1,0:T(8,128)S(1)} %broadcast_multiply_fusion), kind=kLoop, calls=%fused_computation | loop fusion | flops 163840 | bytes 1314304 | tf_op jit(solution)/shard_map/sin | solution.py:178
  91.8 8.5 %all-to-all-done.block_ref = bf16[32,32,128]{2,1,0:T(8,128)(2,1)S(1)} async-done(((bf16[32,32,128]{2,1,0:T(8,128)(2,1)}), bf16[32,32,128]{2,1,0:T(8,128)(2,1)S(1)}, u32[]{:S(2)}, u32[]{:S(2)}) %all-to-all-start) | async-done | bytes 262176 | tf_op jit(solution)/shard_map/all_to_all | solution.py:330
  100.4 3.2 %beam.1 = f32[16,2,4,512]{3,2,1,0:T(4,128)} custom-call(bf16[32,32,128]{2,1,0:T(8,128)(2,1)S(1)} %all-to-all-done.block_ref, s32[2,1024]{1,0:T(2,128)S(1)} %reshape.64.pair_ref, s32[1024,2]{1,0:T(8,128)S(1)} %bitcast.7, f32[16,40,256]{2,1,0:T(8,128)S(1)} %get-tuple-element.34.cos_ref, f32[16,40,256]{2,1,0:T(8,128)S(1)} %get-tuple-element.33.sin_ref), custom_call_target="tpu_custom_call" | custom-call | tf_op jit(solution)/shard_map/beam/pallas_call | solution.py:303
  (8 shorter events, 0.1 us)
Async XLA Ops:
  0.0 7.9 %copy-start = (bf16[1,16,2,64,512]{4,3,2,1,0:T(8,128)(2,1)S(1)}, bf16[1,16,2,64,512]{4,3,2,1,0:T(8,128)(2,1)}, u32[]{:S(2)}) copy-start(bf16[1,16,2,64,512]{4,3,2,1,0:T(8,128)(2,1)} %param.5) | copy-start | bytes 6291460
  0.0 7.9 %copy-start.3 = (f32[1,64,512]{2,1,0:T(8,128)S(1)}, f32[1,64,512]{2,1,0:T(8,128)}, u32[]{:S(2)}) copy-start(f32[1,64,512]{2,1,0:T(8,128)} %param.6) | copy-start | bytes 393220
  0.0 7.9 %copy-start.4 = (s32[16]{0:T(128)S(1)}, s32[16]{0:T(128)}, u32[]{:S(2)}) copy-start(s32[16]{0:T(128)} %offset_ref.3) | copy-start | bytes 196
  3.0 5.0 %collective-permute-start = (bf16[9,2,64,512]{3,2,1,0:T(8,128)(2,1)}, bf16[9,2,64,512]{3,2,1,0:T(8,128)(2,1)S(1)}, u32[]{:S(2)}, u32[]{:S(2)}) collective-permute-start(bf16[9,2,64,512]{3,2,1,0:T(8,128)(2,1)} %select.3), channel_id=1, source_target_pairs={{0,32},{32,0},{64,96},{96,64},{128,160},{160,128},{192,224},{224,1... | collective-permute-start | bytes 3538952 | tf_op jit(solution)/shard_map/ppermute | solution.py:319
  10.3 2.2 %copy-start.1 = (f32[2,3,64,512]{3,2,1,0:T(8,128)}, f32[2,3,64,512]{3,2,1,0:T(8,128)S(1)}, u32[]{:S(2)}) copy-start(f32[2,3,64,512]{3,2,1,0:T(8,128)S(1)} %get-tuple-element.19) | copy-start | bytes 2359300
  12.6 30.0 %collective-permute-start.1 = (f16[4,3,64,512]{3,2,1,0:T(8,128)(2,1)}, f16[4,3,64,512]{3,2,1,0:T(8,128)(2,1)S(1)}, u32[]{:S(2)}, u32[]{:S(2)}) collective-permute-start(f16[4,3,64,512]{3,2,1,0:T(8,128)(2,1)} %convert_element_type.59), channel_id=1, source_target_pairs={{0,64},{32,96},{64,128},{96,160},{128,192},{160,224},{192,256},{22... | collective-permute-start | bytes 2359304 | tf_op jit(solution)/shard_map/ppermute | solution.py:151
  16.1 33.3 %collective-permute-start.2 = (f16[4,3,64,512]{3,2,1,0:T(8,128)(2,1)}, f16[4,3,64,512]{3,2,1,0:T(8,128)(2,1)}, u32[]{:S(2)}, u32[]{:S(2)}) collective-permute-start(f16[4,3,64,512]{3,2,1,0:T(8,128)(2,1)} %convert_element_type.60), channel_id=1, source_target_pairs={{0,448},{32,480},{64,0},{96,32},{128,64},{160,96},{192,128},{224,1... | collective-permute-start | bytes 2359304 | tf_op jit(solution)/shard_map/ppermute | solution.py:151
  18.5 24.1 %collective-permute-start.3 = (f16[1,3,64,512]{3,2,1,0:T(8,128)(2,1)S(1)}, f16[1,3,64,512]{3,2,1,0:T(8,128)(2,1)S(1)}, u32[]{:S(2)}, u32[]{:S(2)}) collective-permute-start(f16[1,3,64,512]{3,2,1,0:T(8,128)(2,1)S(1)} %convert_element_type.61), channel_id=1, source_target_pairs={{0,128},{32,160},{64,192},{96,224},{128,256},{160,288},{192,320},{... | collective-permute-start | bytes 589832 | tf_op jit(solution)/shard_map/ppermute | solution.py:151
  25.4 24.0 %collective-permute-start.5 = (f16[1,3,64,512]{3,2,1,0:T(8,128)(2,1)S(1)}, f16[1,3,64,512]{3,2,1,0:T(8,128)(2,1)S(1)}, u32[]{:S(2)}, u32[]{:S(2)}) collective-permute-start(f16[1,3,64,512]{3,2,1,0:T(8,128)(2,1)S(1)} %convert_element_type.62), channel_id=1, source_target_pairs={{0,384},{32,416},{64,448},{96,480},{128,0},{160,32},{192,64},{224,... | collective-permute-start | bytes 589832 | tf_op jit(solution)/shard_map/ppermute | solution.py:151
  42.6 29.6 %copy-start.2 = (f32[2,3,64,512]{3,2,1,0:T(8,128)S(1)}, f32[2,3,64,512]{3,2,1,0:T(8,128)}, u32[]{:S(2)}) copy-start(f32[2,3,64,512]{3,2,1,0:T(8,128)} %copy-done.1) | copy-start | bytes 2359300
  42.8 14.9 %collective-permute-start.4 = (f16[2,3,64,512]{3,2,1,0:T(8,128)(2,1)S(1)}, f16[2,3,64,512]{3,2,1,0:T(8,128)(2,1)S(1)}, u32[]{:S(2)}, u32[]{:S(2)}) collective-permute-start(f16[2,3,64,512]{3,2,1,0:T(8,128)(2,1)S(1)} %add_convert_fusion.1), channel_id=1, source_target_pairs={{0,128},{32,160},{64,192},{96,224},{128,256},{160,288},{192,320},{... | collective-permute-start | bytes 1179656 | tf_op jit(solution)/shard_map/ppermute | solution.py:151
  50.5 21.6 %collective-permute-start.6 = (f16[2,3,64,512]{3,2,1,0:T(8,128)(2,1)S(1)}, f16[2,3,64,512]{3,2,1,0:T(8,128)(2,1)S(1)}, u32[]{:S(2)}, u32[]{:S(2)}) collective-permute-start(f16[2,3,64,512]{3,2,1,0:T(8,128)(2,1)S(1)} %add_convert_fusion), channel_id=1, source_target_pairs={{0,384},{32,416},{64,448},{96,480},{128,0},{160,32},{192,64},{224,... | collective-permute-start | bytes 1179656 | tf_op jit(solution)/shard_map/ppermute | solution.py:151
  73.4 15.4 %copy-start.5 = (s32[2048]{0:T(1024)S(1)}, s32[2048]{0:T(1024)}, u32[]{:S(2)}) copy-start(s32[2048]{0:T(1024)} %param.9) | copy-start | bytes 24580
  73.5 15.7 %copy-start.6 = (s32[2048]{0:T(1024)S(1)}, s32[2048]{0:T(1024)}, u32[]{:S(2)}) copy-start(s32[2048]{0:T(1024)} %param.8) | copy-start | bytes 24580
  74.8 25.5 %all-to-all-start = ((bf16[32,32,128]{2,1,0:T(8,128)(2,1)}), bf16[32,32,128]{2,1,0:T(8,128)(2,1)S(1)}, u32[]{:S(2)}, u32[]{:S(2)}) async-start(bf16[32,32,128]{2,1,0:T(8,128)(2,1)} %pack.1), calls=%async_computation | async-start | bytes 524288 | tf_op jit(solution)/shard_map/all_to_all | solution.py:330

commit v6 on v3

--- a/solution.py
+++ b/solution.py
@@ -136,7 +136,8 @@
         ],
         out_specs=[block(len(bins)) for bins in SENDS],
         out_shape=[
-            jax.ShapeDtypeStruct((len(bins), 2, BASE_LOC, FREQ), F32) for bins in SENDS
+            (pltpu.HBM if at >= 4 else jax.ShapeDtypeStruct)((len(bins), 2, BASE_LOC, FREQ), F32)
+            for at, bins in enumerate(SENDS)
         ],
         compiler_params=pltpu.CompilerParams(vmem_limit_bytes=16 * MIB),
         name="chip_sums",

time: 98.7 us -> 97.6 us (0.989)
  other arithmetic: 5.86 us -> 4.83 us
  Pallas kernels: 9.81 us -> 10.8 us
    convert_element_type x2, other arithmetic: 1.25 us -> 0.22 us  [reduce_ring(): middle_up, middle_down = (middle_up.astype(F16), middle_down.astype(F16))]
    pallas_call x1, Pallas kernels: 2.19 us -> 3.19 us  [chip_sums(): pl.pallas_call(chip_kernel, grid=(BASE_LOC // rows,), in_specs=[pl.BlockS...]
  transfers between devices with their start and end apart: 10 -> 10, of which waited for: 4 -> 4; matrix products, arithmetic and copies ran while one was open for 8% -> 7% of each run, Pallas kernels for 2% -> 3%
where the time goes in v6:
time: 97.6 us; the launch traced here: 97.1 us
  starting transfers between devices  44.8 us (46%)
  waiting for transfers between devices  34.6 us (35%)
  Pallas kernels  10.8 us (11%)
  other arithmetic  4.83 us (5%)
  local copies, waits for them, and re-layouts  1.63 us (2%)
    ppermute x6, waiting for transfers between devices, send(): return lax.ppermute(values, 'day', pairs)  23.1 us
    ppermute x6, starting transfers between devices, send(): return lax.ppermute(values, 'day', pairs)  22 us
    all_to_all x1, waiting for transfers between devices, beam_stage(): lax.all_to_all(packed, 'bl', split_axis=0, concat_axis=0, tiled=True)  10.2 us
    all_to_all x1, starting transfers between devices, gather_weights(): lax.all_to_all(copies, 'day', split_axis=0, concat_axis=0, axis_index_gro...  9.84 us
    all_to_all x1, starting transfers between devices, beam_stage(): lax.all_to_all(packed, 'bl', split_axis=0, concat_axis=0, tiled=True)  9.14 us
    pallas_call x1, Pallas kernels, beam(): pl.pallas_call(beam_kernel, in_specs=[vmem] * 5, out_specs=vmem, out_shap...  3.22 us
    pallas_call x1, Pallas kernels, chip_sums(): pl.pallas_call(chip_kernel, grid=(BASE_LOC // rows,), in_specs=[pl.BlockS...  3.19 us
    pallas_call x1, Pallas kernels, select(): pl.pallas_call(select_kernel, in_specs=[pl.BlockSpec(memory_space=pltpu.S...  3 us
  transfers between devices with their start and end apart: 10, of which 4 were waited for; matrix products, arithmetic and copies ran while one was open for 7% of the time, Pallas kernels for 3%

profile of v6, /device:TPU:8, one launch (start us, length us, event | category | flops | bytes accessed | tf_op | source)
XLA Modules:
  0.0 97.1 jit_solution(12845024549928030003)
XLA Ops:
  0.0 0.0 copy-start.1
  0.0 0.0 copy-start.2
  0.0 0.0 copy-start
  0.0 3.0 %select.13 = bf16[9,2,64,512]{3,2,1,0:T(8,128)(2,1)} custom-call(s32[16]{0:T(128)} %offset_ref.3, f32[64,512]{1,0:T(8,128)} %bitcast.10, bf16[16,2,64,512]{3,2,1,0:T(8,128)(2,1)} %bitcast.7), custom_call_target="tpu_custom_call" | custom-call | tf_op jit(solution)/shard_map/select/pallas_call | solution.py:75
  3.0 1.9 %collective-permute-start = (bf16[9,2,64,512]{3,2,1,0:T(8,128)(2,1)}, bf16[9,2,64,512]{3,2,1,0:T(8,128)(2,1)S(1)}, u32[]{:S(2)}, u32[]{:S(2)}) collective-permute-start(bf16[9,2,64,512]{3,2,1,0:T(8,128)(2,1)} %select.13), channel_id=1, source_target_pairs={{0,32},{32,0},{64,96},{96,64},{128,160},{160,128},{192,224},{224,1... | collective-permute-start | bytes 3538952 | tf_op jit(solution)/shard_map/ppermute | solution.py:342
  4.9 0.0 copy-done.1
  5.0 0.8 broadcast_in_dim.5
  5.8 9.8 %all-to-all-start = ((f16[8,64,512]{2,1,0:T(8,128)(2,1)}), f16[8,64,512]{2,1,0:T(8,128)(2,1)}, u32[]{:S(2)}, u32[]{:S(2)}) async-start(f16[8,64,512]{2,1,0:T(8,128)(2,1)} %broadcast_in_dim.5), calls=%async_computation | async-start | bytes 1048576 | tf_op jit(solution)/shard_map/all_to_all | solution.py:178
  15.7 0.0 copy-done.2
  15.7 0.1 slice.28
  15.8 0.1 slice.29
  15.9 0.0 collective-permute-done.other_ref
  15.9 0.0 copy-done
  15.9 3.2 %chip_sums.1 = (f32[4,2,64,512]{3,2,1,0:T(8,128)S(1)}, f32[4,2,64,512]{3,2,1,0:T(8,128)S(1)}, f32[1,2,64,512]{3,2,1,0:T(8,128)S(1)}, f32[1,2,64,512]{3,2,1,0:T(8...) custom-call(s32[16]{0:T(128)S(1)} %copy-done.2, ...), custom_call_target="tpu_custom_call" | custom-call | tf_op jit(solution)/shard_map/chip_sums/pallas_call | solution.py:128
  19.1 0.0 copy-start.4
  19.1 0.1 convert_element_type.74
  19.2 0.0 copy-start.3
  19.2 0.1 convert_element_type.75
  19.4 3.5 %collective-permute-start.1 = (f16[4,2,64,512]{3,2,1,0:T(8,128)(2,1)S(1)}, f16[4,2,64,512]{3,2,1,0:T(8,128)(2,1)S(1)}, u32[]{:S(2)}, u32[]{:S(2)}) collective-permute-start(f16[4,2,64,512]{3,2,1,0:T(8,128)(2,1)S(1)} %convert_element_type.74), channel_id=1, source_target_pairs={{0,64},{32,96},{64,128},{96,160},{128,192},{160,224},{192,256},{22... | collective-permute-start | bytes 1572872 | tf_op jit(solution)/shard_map/ppermute | solution.py:151
  22.9 0.1 fusion.2
  23.0 2.5 %collective-permute-start.2 = (f16[4,2,64,512]{3,2,1,0:T(8,128)(2,1)S(1)}, f16[4,2,64,512]{3,2,1,0:T(8,128)(2,1)S(1)}, u32[]{:S(2)}, u32[]{:S(2)}) collective-permute-start(f16[4,2,64,512]{3,2,1,0:T(8,128)(2,1)S(1)} %convert_element_type.75), channel_id=1, source_target_pairs={{0,448},{32,480},{64,0},{96,32},{128,64},{160,96},{192,128},{224,1... | collective-permute-start | bytes 1572872 | tf_op jit(solution)/shard_map/ppermute | solution.py:151
  25.4 5.0 %collective-permute-start.3 = (f16[1,2,64,512]{3,2,1,0:T(8,128)(2,1)S(1)}, f16[1,2,64,512]{3,2,1,0:T(8,128)(2,1)S(1)}, u32[]{:S(2)}, u32[]{:S(2)}) collective-permute-start(f16[1,2,64,512]{3,2,1,0:T(8,128)(2,1)S(1)} %convert_element_type.76), channel_id=1, source_target_pairs={{0,128},{32,160},{64,192},{96,224},{128,256},{160,288},{192,320},{... | collective-permute-start | bytes 393224 | tf_op jit(solution)/shard_map/ppermute | solution.py:151
  30.4 3.0 %collective-permute-start.5 = (f16[1,2,64,512]{3,2,1,0:T(8,128)(2,1)S(1)}, f16[1,2,64,512]{3,2,1,0:T(8,128)(2,1)S(1)}, u32[]{:S(2)}, u32[]{:S(2)}) collective-permute-start(f16[1,2,64,512]{3,2,1,0:T(8,128)(2,1)S(1)} %convert_element_type.77), channel_id=1, source_target_pairs={{0,384},{32,416},{64,448},{96,480},{128,0},{160,32},{192,64},{224,... | collective-permute-start | bytes 393224 | tf_op jit(solution)/shard_map/ppermute | solution.py:151
  33.4 14.3 %collective-permute-done.3 = f16[1,2,64,512]{3,2,1,0:T(8,128)(2,1)S(1)} collective-permute-done((f16[1,2,64,512]{3,2,1,0:T(8,128)(2,1)S(1)}, f16[1,2,64,512]{3,2,1,0:T(8,128)(2,1)S(1)}, u32[]{:S(2)}, u32[]{:S(2)}) %collective-permute-start.3) | collective-permute-done | bytes 131104 | tf_op jit(solution)/shard_map/ppermute | solution.py:151
  47.7 0.0 collective-permute-done.1
  47.7 0.0 copy-done.4
  47.7 0.1 add_convert_fusion.1
  47.9 1.9 %collective-permute-start.4 = (f16[2,2,64,512]{3,2,1,0:T(8,128)(2,1)S(1)}, f16[2,2,64,512]{3,2,1,0:T(8,128)(2,1)S(1)}, u32[]{:S(2)}, u32[]{:S(2)}) collective-permute-start(f16[2,2,64,512]{3,2,1,0:T(8,128)(2,1)S(1)} %add_convert_fusion.1), channel_id=1, source_target_pairs={{0,128},{32,160},{64,192},{96,224},{128,256},{160,288},{192,320},{... | collective-permute-start | bytes 786440 | tf_op jit(solution)/shard_map/ppermute | solution.py:151
  49.8 0.0 collective-permute-done.5
  49.8 0.0 collective-permute-done.2
  49.8 0.0 copy-done.3
  49.8 0.1 add_convert_fusion
  49.9 0.0 copy-start.5
  49.9 6.2 %collective-permute-start.6 = (f16[2,2,64,512]{3,2,1,0:T(8,128)(2,1)S(1)}, f16[2,2,64,512]{3,2,1,0:T(8,128)(2,1)S(1)}, u32[]{:S(2)}, u32[]{:S(2)}) collective-permute-start(f16[2,2,64,512]{3,2,1,0:T(8,128)(2,1)S(1)} %add_convert_fusion), channel_id=1, source_target_pairs={{0,384},{32,416},{64,448},{96,480},{128,0},{160,32},{192,64},{224,... | collective-permute-start | bytes 786440 | tf_op jit(solution)/shard_map/ppermute | solution.py:151
  56.1 0.1 add_convert_fusion.2
  56.2 0.0 all-to-all-done
  56.2 8.8 %collective-permute-done.4 = f16[2,2,64,512]{3,2,1,0:T(8,128)(2,1)S(1)} collective-permute-done((f16[2,2,64,512]{3,2,1,0:T(8,128)(2,1)S(1)}, f16[2,2,64,512]{3,2,1,0:T(8,128)(2,1)S(1)}, u32[]{:S(2)}, u32[]{:S(2)}) %collective-permute-start.4) | collective-permute-done | bytes 262176 | tf_op jit(solution)/shard_map/ppermute | solution.py:151
  65.0 1.2 %convert_element_type.88 = f32[8,64,512]{2,1,0:T(8,128)S(1)} convert(f16[8,64,512]{2,1,0:T(8,128)(2,1)} %all-to-all-done) | non-fusion elementwise | flops 262144 | bytes 1572864 | tf_op jit(solution)/shard_map/convert_element_type | solution.py:190
  66.2 0.4 multiply_reduce_fusion
  66.6 1.9 %collective-permute-start.7 = (f32[2,64,512]{2,1,0:T(8,128)S(1)}, f32[2,64,512]{2,1,0:T(8,128)S(1)}, u32[]{:S(2)}, u32[]{:S(2)}) collective-permute-start(f32[2,64,512]{2,1,0:T(8,128)S(1)} %slice.37), channel_id=1, source_target_pairs={{0,32},{32,0},{64,96},{96,64},{128,160},{160,128},{192,224},{224,1... | collective-permute-start | bytes 786440 | tf_op jit(solution)/shard_map/ppermute | solution.py:191
  68.5 0.0 collective-permute-done.6
  68.5 0.0 copy-done.5
  68.5 0.0 copy-start.6
  68.5 0.0 copy-start.7
  68.5 0.2 convert_add_fusion.sum_ref
  68.7 1.3 %collective-permute-done.7 = f32[2,64,512]{2,1,0:T(8,128)S(1)} collective-permute-done((f32[2,64,512]{2,1,0:T(8,128)S(1)}, f32[2,64,512]{2,1,0:T(8,128)S(1)}, u32[]{:S(2)}, u32[]{:S(2)}) %collective-permute-start.7) | collective-permute-done | bytes 262176 | tf_op jit(solution)/shard_map/ppermute | solution.py:191
  70.0 0.1 fusion.inverse_ref
  70.1 1.4 %pack.1 = bf16[32,32,128]{2,1,0:T(8,128)(2,1)} custom-call(f32[2,2,64,512]{3,2,1,0:T(8,128)S(1)} %convert_add_fusion.sum_ref, f32[2,64,512]{2,1,0:T(8,128)S(1)} %fusion.inverse_ref), custom_call_target="tpu_custom_call" | custom-call | tf_op jit(solution)/shard_map/pack/pallas_call | solution.py:241
  71.5 9.1 %all-to-all-start.1 = ((bf16[32,32,128]{2,1,0:T(8,128)(2,1)}), bf16[32,32,128]{2,1,0:T(8,128)(2,1)S(1)}, u32[]{:S(2)}, u32[]{:S(2)}) async-start(bf16[32,32,128]{2,1,0:T(8,128)(2,1)} %pack.1), calls=%async_computation.1 | async-start | bytes 524288 | tf_op jit(solution)/shard_map/all_to_all | solution.py:356
  80.6 0.0 copy-done.6
  80.7 0.1 reshape.120
  80.7 0.3 copy.9
  81.0 0.0 copy-done.7
  81.0 0.1 reshape.118
  81.1 0.1 reshape.119.pair_ref
  81.2 0.1 broadcast_multiply_fusion
  81.3 2.3 %multiply_sine_fusion = (f32[16,40,256]{2,1,0:T(8,128)S(1)}, f32[16,40,256]{2,1,0:T(8,128)S(1)}) fusion(f32[256]{0:T(256)S(1)} %multiply_add_fusion, f32[16,40]{1,0:T(8,128)S(1)} %broadcast_multiply_fusion), kind=kLoop, calls=%fused_computation.1 | loop fusion | flops 163840 | bytes 1314304 | tf_op jit(solution)/shard_map/sin | solution.py:200
  83.6 10.2 %all-to-all-done.1.block_ref = bf16[32,32,128]{2,1,0:T(8,128)(2,1)S(1)} async-done(((bf16[32,32,128]{2,1,0:T(8,128)(2,1)}), bf16[32,32,128]{2,1,0:T(8,128)(2,1)S(1)}, u32[]{:S(2)}, u32[]{:S(2)}) %all-to-all-start.1) | async-done | bytes 262176 | tf_op jit(solution)/shard_map/all_to_all | solution.py:356
  93.9 3.2 %beam.1 = f32[16,2,4,512]{3,2,1,0:T(4,128)} custom-call(bf16[32,32,128]{2,1,0:T(8,128)(2,1)S(1)} %all-to-all-done.1.block_ref, s32[2,1024]{1,0:T(2,128)S(1)} %reshape.119.pair_ref, s32[1024,2]{1,0:T(8,128)S(1)} %bitcast.9, f32[16,40,256]{2,1,0:T(8,128)S(1)} %get-tuple-element.36.cos_ref, f32[16,40,256]{2,1,0:T(8,128)S(1)} %get-tuple-element.35.sin_ref), custom_call_target="tpu_custom_call" | custom-call | tf_op jit(solution)/shard_map/beam/pallas_call | solution.py:326
  (12 shorter events, 0.1 us)
Async XLA Ops:
  0.0 4.9 %copy-start.1 = (f32[1,64,512]{2,1,0:T(8,128)S(1)}, f32[1,64,512]{2,1,0:T(8,128)}, u32[]{:S(2)}) copy-start(f32[1,64,512]{2,1,0:T(8,128)} %param.6) | copy-start | bytes 393220
  0.0 15.7 %copy-start.2 = (s32[16]{0:T(128)S(1)}, s32[16]{0:T(128)}, u32[]{:S(2)}) copy-start(s32[16]{0:T(128)} %offset_ref.3) | copy-start | bytes 196
  0.0 15.9 %copy-start = (bf16[1,16,2,64,512]{4,3,2,1,0:T(8,128)(2,1)S(1)}, bf16[1,16,2,64,512]{4,3,2,1,0:T(8,128)(2,1)}, u32[]{:S(2)}) copy-start(bf16[1,16,2,64,512]{4,3,2,1,0:T(8,128)(2,1)} %param.5) | copy-start | bytes 6291460
  3.0 12.9 %collective-permute-start = (bf16[9,2,64,512]{3,2,1,0:T(8,128)(2,1)}, bf16[9,2,64,512]{3,2,1,0:T(8,128)(2,1)S(1)}, u32[]{:S(2)}, u32[]{:S(2)}) collective-permute-start(bf16[9,2,64,512]{3,2,1,0:T(8,128)(2,1)} %select.13), channel_id=1, source_target_pairs={{0,32},{32,0},{64,96},{96,64},{128,160},{160,128},{192,224},{224,1... | collective-permute-start | bytes 3538952 | tf_op jit(solution)/shard_map/ppermute | solution.py:342
  5.8 50.4 %all-to-all-start = ((f16[8,64,512]{2,1,0:T(8,128)(2,1)}), f16[8,64,512]{2,1,0:T(8,128)(2,1)}, u32[]{:S(2)}, u32[]{:S(2)}) async-start(f16[8,64,512]{2,1,0:T(8,128)(2,1)} %broadcast_in_dim.5), calls=%async_computation | async-start | bytes 1048576 | tf_op jit(solution)/shard_map/all_to_all | solution.py:178
  19.1 28.7 %copy-start.4 = (f32[2,2,64,512]{3,2,1,0:T(8,128)S(1)}, f32[2,2,64,512]{3,2,1,0:T(8,128)}, u32[]{:S(2)}) copy-start(f32[2,2,64,512]{3,2,1,0:T(8,128)} %get-tuple-element.27) | copy-start | bytes 1572868
  19.2 30.6 %copy-start.3 = (f32[2,2,64,512]{3,2,1,0:T(8,128)S(1)}, f32[2,2,64,512]{3,2,1,0:T(8,128)}, u32[]{:S(2)}) copy-start(f32[2,2,64,512]{3,2,1,0:T(8,128)} %get-tuple-element.29) | copy-start | bytes 1572868
  19.4 28.4 %collective-permute-start.1 = (f16[4,2,64,512]{3,2,1,0:T(8,128)(2,1)S(1)}, f16[4,2,64,512]{3,2,1,0:T(8,128)(2,1)S(1)}, u32[]{:S(2)}, u32[]{:S(2)}) collective-permute-start(f16[4,2,64,512]{3,2,1,0:T(8,128)(2,1)S(1)} %convert_element_type.74), channel_id=1, source_target_pairs={{0,64},{32,96},{64,128},{96,160},{128,192},{160,224},{192,256},{22... | collective-permute-start | bytes 1572872 | tf_op jit(solution)/shard_map/ppermute | solution.py:151
  23.0 26.8 %collective-permute-start.2 = (f16[4,2,64,512]{3,2,1,0:T(8,128)(2,1)S(1)}, f16[4,2,64,512]{3,2,1,0:T(8,128)(2,1)S(1)}, u32[]{:S(2)}, u32[]{:S(2)}) collective-permute-start(f16[4,2,64,512]{3,2,1,0:T(8,128)(2,1)S(1)} %convert_element_type.75), channel_id=1, source_target_pairs={{0,448},{32,480},{64,0},{96,32},{128,64},{160,96},{192,128},{224,1... | collective-permute-start | bytes 1572872 | tf_op jit(solution)/shard_map/ppermute | solution.py:151
  25.4 22.3 %collective-permute-start.3 = (f16[1,2,64,512]{3,2,1,0:T(8,128)(2,1)S(1)}, f16[1,2,64,512]{3,2,1,0:T(8,128)(2,1)S(1)}, u32[]{:S(2)}, u32[]{:S(2)}) collective-permute-start(f16[1,2,64,512]{3,2,1,0:T(8,128)(2,1)S(1)} %convert_element_type.76), channel_id=1, source_target_pairs={{0,128},{32,160},{64,192},{96,224},{128,256},{160,288},{192,320},{... | collective-permute-start | bytes 393224 | tf_op jit(solution)/shard_map/ppermute | solution.py:151
  30.4 19.4 %collective-permute-start.5 = (f16[1,2,64,512]{3,2,1,0:T(8,128)(2,1)S(1)}, f16[1,2,64,512]{3,2,1,0:T(8,128)(2,1)S(1)}, u32[]{:S(2)}, u32[]{:S(2)}) collective-permute-start(f16[1,2,64,512]{3,2,1,0:T(8,128)(2,1)S(1)} %convert_element_type.77), channel_id=1, source_target_pairs={{0,384},{32,416},{64,448},{96,480},{128,0},{160,32},{192,64},{224,... | collective-permute-start | bytes 393224 | tf_op jit(solution)/shard_map/ppermute | solution.py:151
  47.9 17.2 %collective-permute-start.4 = (f16[2,2,64,512]{3,2,1,0:T(8,128)(2,1)S(1)}, f16[2,2,64,512]{3,2,1,0:T(8,128)(2,1)S(1)}, u32[]{:S(2)}, u32[]{:S(2)}) collective-permute-start(f16[2,2,64,512]{3,2,1,0:T(8,128)(2,1)S(1)} %add_convert_fusion.1), channel_id=1, source_target_pairs={{0,128},{32,160},{64,192},{96,224},{128,256},{160,288},{192,320},{... | collective-permute-start | bytes 786440 | tf_op jit(solution)/shard_map/ppermute | solution.py:151
  49.9 18.6 %copy-start.5 = (f32[2,2,64,512]{3,2,1,0:T(8,128)S(1)}, f32[2,2,64,512]{3,2,1,0:T(8,128)}, u32[]{:S(2)}) copy-start(f32[2,2,64,512]{3,2,1,0:T(8,128)} %get-tuple-element.20) | copy-start | bytes 1572868
  49.9 18.6 %collective-permute-start.6 = (f16[2,2,64,512]{3,2,1,0:T(8,128)(2,1)S(1)}, f16[2,2,64,512]{3,2,1,0:T(8,128)(2,1)S(1)}, u32[]{:S(2)}, u32[]{:S(2)}) collective-permute-start(f16[2,2,64,512]{3,2,1,0:T(8,128)(2,1)S(1)} %add_convert_fusion), channel_id=1, source_target_pairs={{0,384},{32,416},{64,448},{96,480},{128,0},{160,32},{192,64},{224,... | collective-permute-start | bytes 786440 | tf_op jit(solution)/shard_map/ppermute | solution.py:151
  66.6 3.4 %collective-permute-start.7 = (f32[2,64,512]{2,1,0:T(8,128)S(1)}, f32[2,64,512]{2,1,0:T(8,128)S(1)}, u32[]{:S(2)}, u32[]{:S(2)}) collective-permute-start(f32[2,64,512]{2,1,0:T(8,128)S(1)} %slice.37), channel_id=1, source_target_pairs={{0,32},{32,0},{64,96},{96,64},{128,160},{160,128},{192,224},{224,1... | collective-permute-start | bytes 786440 | tf_op jit(solution)/shard_map/ppermute | solution.py:191
  68.5 12.1 %copy-start.6 = (s32[2048]{0:T(1024)S(1)}, s32[2048]{0:T(1024)}, u32[]{:S(2)}) copy-start(s32[2048]{0:T(1024)} %param.9) | copy-start | bytes 24580
  68.5 12.5 %copy-start.7 = (s32[2048]{0:T(1024)S(1)}, s32[2048]{0:T(1024)}, u32[]{:S(2)}) copy-start(s32[2048]{0:T(1024)} %param.8) | copy-start | bytes 24580
  71.5 22.4 %all-to-all-start.1 = ((bf16[32,32,128]{2,1,0:T(8,128)(2,1)}), bf16[32,32,128]{2,1,0:T(8,128)(2,1)S(1)}, u32[]{:S(2)}, u32[]{:S(2)}) async-start(bf16[32,32,128]{2,1,0:T(8,128)(2,1)} %pack.1), calls=%async_computation.1 | async-start | bytes 524288 | tf_op jit(solution)/shard_map/all_to_all | solution.py:356
